TPU v7x, 32 devices: a whole 2x2x4 slice. The times are simulated.
32 devices in a mesh: rep: 2 (over core), shard: 16 (over z, y, x).
Axes of the slice: x: 2, y: 2, z: 4, core: 2. Of those that a mesh axis runs over, the one named last changes fastest.
Arguments:
- streams: bfloat16 [4096, 4, 2048], P(('rep', 'shard')), may hold values from -6 to 6
- cotangent: bfloat16 [4096, 4, 2048], P(('rep', 'shard')), may hold values from -6 to 6
- deal: int32 [4096], P(('rep', 'shard')), may hold values from 0 to 127, as said below
- lengths: int32 [8, 4], replicated, may hold values from 0 to 512, as said below
- mix_attn: float32 [4, 6], replicated, may hold values from -0.9 to 1.9
- mix_mlp: float32 [4, 6], replicated, may hold values from -0.9 to 1.9
- w_qkv: bfloat16 [2048, 6144], P(('rep', 'shard')), may hold values from -0.125 to 0.125
- w_out: bfloat16 [2048, 2048], P(('rep', 'shard')), may hold values from -0.5 to 0.5
- w_gu: bfloat16 [2048, 16384], P(('rep', 'shard')), may hold values from -0.125 to 0.125
- w_down: bfloat16 [2048, 8192], P(('rep', 'shard')), may hold values from -0.0625 to 0.0625
Outputs:
- new_streams: float32 [4096, 4, 2048], P(('rep', 'shard'))
- d_streams: float32 [4096, 4, 2048], P(('rep', 'shard'))
- g_mix_attn: float32 [4, 6], replicated
- g_mix_mlp: float32 [4, 6], replicated
- g_qkv: float32 [2048, 6144], P(('rep', 'shard'))
- g_out: float32 [2048, 2048], P(('rep', 'shard'))
- g_gu: float32 [2048, 16384], P(('rep', 'shard'))
- g_down: float32 [2048, 8192], P(('rep', 'shard'))
Inputs may be any that keep to these rules, and one draw needn't show every extreme that they name: `deal`: within each device's 128 entries every value appears once. `lengths`: each row sums to at most 512; in each group of 4 rows (starting at a multiple of 4) one row is 512 followed by zeros.
All inputs are finite; a program needn't handle non-finite values.
Results may differ from a plain program's by a relative error of at most 0.013.
Values may be sent and summed in bfloat16 or wider, within the bound.
A program may use at most 832 MiB of HBM per device.

v0:
```python
import math

import jax
import jax.numpy as jnp
from jax import lax
from jax.sharding import PartitionSpec as P

HEADS = 16
HEAD_DIM = 128
HEAD_SPLIT = 4


EPSILON = 1e-05
HIGHEST = lax.Precision.HIGHEST
CONTRACT_LAST = (((1,), (1,)), ((), ()))
CONTRACT_FIRST = (((0,), (0,)), ((), ()))


def normalize(inputs):
    centred = inputs - jnp.mean(inputs, -1, keepdims=True)
    inverse = lax.rsqrt(jnp.mean(centred * centred, -1, keepdims=True) + EPSILON)
    return (centred * inverse, inverse)


def normalize_back(grad_out, normed, inverse):
    return inverse * (
        grad_out
        - jnp.mean(grad_out, -1, keepdims=True)
        - normed * jnp.mean(grad_out * normed, -1, keepdims=True)
    )


def read_streams(streams, weights):
    return jnp.sum(streams * weights[None, :, None], axis=1)


def write_streams(streams, mixing, branch, out_weights):
    result = branch[:, None, :] * out_weights[None, :, None]
    for source in range(streams.shape[1]):
        result = result + streams[:, source, None, :] * mixing[source][None, :, None]
    return result


def write_back(grad_out, mixing):
    result = jnp.zeros_like(grad_out)
    for target in range(grad_out.shape[1]):
        result = result + grad_out[:, target, None, :] * mixing[:, target][None, :, None]
    return result


def mixing_grad(streams, grad_out, branch, grad_read):
    first = jnp.einsum("tjd,td->j", streams, grad_read, precision=HIGHEST)
    middle = jnp.einsum("tjd,tid->ji", streams, grad_out, precision=HIGHEST)
    final_cols = jnp.einsum("td,tid->i", branch, grad_out, precision=HIGHEST)
    return jnp.concatenate([first[:, None], middle, final_cols[:, None]], axis=1)


def slot_layout(lengths_row, capacity):
    seq_count = lengths_row.shape[-1]
    seq_ends = jnp.cumsum(lengths_row, axis=-1)
    slot_index = jnp.arange(capacity, dtype=jnp.int32)
    segment = jnp.sum((slot_index[:, None] >= seq_ends[..., None, :]).astype(jnp.int32), axis=-1)
    seq_starts = seq_ends - lengths_row
    chosen = (segment[..., None] == jnp.arange(seq_count, dtype=jnp.int32)).astype(jnp.int32)
    start_of = jnp.sum(chosen * seq_starts[..., None, :], axis=-1)
    is_live = segment < seq_count
    segment = jnp.where(is_live, segment, seq_count + slot_index)
    position = jnp.where(is_live, slot_index - start_of, 0)
    return (segment, position)


def rope_tables(position, head_width):
    half_width = head_width // 2
    frequency = jnp.exp(
        jnp.arange(half_width, dtype=jnp.float32) * (-2.0 * math.log(10000.0) / head_width)
    )
    angles = position.astype(jnp.float32)[..., None] * frequency
    return (jnp.cos(angles), jnp.sin(angles))


def rotate(inputs, cosine, sine_table):
    half_width = inputs.shape[-1] // 2
    first = inputs[..., :half_width]
    second = inputs[..., half_width:]
    return jnp.concatenate(
        [first * cosine - second * sine_table, second * cosine + first * sine_table], axis=-1
    )


def rotate_back(grad_out, cosine, sine_table):
    half_width = grad_out.shape[-1] // 2
    first = grad_out[..., :half_width]
    second = grad_out[..., half_width:]
    return jnp.concatenate(
        [first * cosine + second * sine_table, second * cosine - first * sine_table], axis=-1
    )


def visible(seg_query, pos_query, seg_key, pos_key):
    return (seg_query[:, None] == seg_key[None, :]) & (pos_key[None, :] <= pos_query[:, None])


def pack_owner(sorted_rows, bin_count, split_count, part_count):
    tokens = sorted_rows.shape[0]
    shaped = sorted_rows.reshape(
        bin_count, tokens // bin_count, part_count, split_count, HEADS // split_count, HEAD_DIM
    )
    return shaped.transpose(0, 3, 1, 4, 2, 5).reshape(
        bin_count * split_count, tokens // bin_count, HEADS // split_count, part_count * HEAD_DIM
    )


def unpack_owner(blocks, bin_count, split_count, part_count):
    slot_rows = blocks.shape[1]
    shaped = blocks.reshape(
        bin_count, split_count, slot_rows, HEADS // split_count, part_count, HEAD_DIM
    )
    return shaped.transpose(0, 2, 4, 1, 3, 5).reshape(
        bin_count * slot_rows, part_count * HEADS * HEAD_DIM
    )


def attend_back(packed, log_total, grad_out, cosine, sine_table, segment, position):
    head_width = HEAD_DIM
    score_scale = 1.0 / math.sqrt(head_width)
    capacity = packed.shape[0]
    query_rows = min(512, capacity)
    queries = rotate(packed[..., :head_width].astype(jnp.float32), cosine, sine_table).astype(
        jnp.bfloat16
    )
    key_rows = rotate(
        packed[..., head_width : 2 * head_width].astype(jnp.float32), cosine, sine_table
    ).astype(jnp.bfloat16)
    value_rows = packed[..., 2 * head_width :]

    def back_block(running, offset):
        grad_keys, grad_values = running
        total_part = jnp.transpose(log_total)
        scores = (
            jnp.einsum("qhd,khd->hqk", queries, key_rows, preferred_element_type=jnp.float32)
            * score_scale
        )
        scores = jnp.where(visible(segment, position, segment, position)[None], scores, -1e30)
        probability = jnp.exp(scores - total_part[:, :, None])
        grad_values = grad_values + jnp.einsum(
            "hqk,qhd->khd",
            probability.astype(jnp.bfloat16),
            grad_out,
            preferred_element_type=jnp.float32,
        )
        grad_probs = jnp.einsum(
            "qhd,khd->hqk", grad_out, value_rows, preferred_element_type=jnp.float32
        )
        shared = jnp.sum(grad_probs * probability, -1, keepdims=True)
        grad_scores = (probability * (grad_probs - shared)).astype(jnp.bfloat16)
        grad_query = (
            jnp.einsum("hqk,khd->qhd", grad_scores, key_rows, preferred_element_type=jnp.float32)
            * score_scale
        )
        grad_keys = (
            grad_keys
            + jnp.einsum("hqk,qhd->khd", grad_scores, queries, preferred_element_type=jnp.float32)
            * score_scale
        )
        return ((grad_keys, grad_values), grad_query)

    zero_grads = jnp.zeros(key_rows.shape, jnp.float32)
    offsets = jnp.arange(0, capacity, query_rows, dtype=jnp.int32)
    (grad_keys, grad_values), grad_query = lax.scan(back_block, (zero_grads, zero_grads), offsets)
    grad_query = grad_query.reshape(capacity, key_rows.shape[1], head_width)
    result = jnp.concatenate(
        [
            rotate_back(grad_query, cosine, sine_table),
            rotate_back(grad_keys, cosine, sine_table),
            grad_values,
        ],
        axis=-1,
    )
    return result.astype(jnp.bfloat16)


def shards(streams, cotangent, deal, lengths, mix_attn, mix_mlp, w_qkv, w_out, w_gu, w_down):
    streams_in = streams.astype(jnp.float32)
    stream_count = streams.shape[1]
    rep_size = lax.axis_size("rep")
    shard_size = lax.axis_size("shard")
    bin_count = shard_size // HEAD_SPLIT
    capacity = streams.shape[0] * HEAD_SPLIT
    query_rows = min(512, capacity)
    head_width = HEAD_DIM
    score_scale = 1.0 / math.sqrt(head_width)
    bin_index = lax.axis_index("rep") * bin_count + lax.axis_index("shard") // HEAD_SPLIT
    lengths_row = lax.dynamic_index_in_dim(lengths, bin_index, 0, keepdims=False)
    segment, position = slot_layout(lengths_row, capacity)
    cosine, sine_table = rope_tables(position, head_width)
    cosine = cosine[:, None, :]
    sine_table = sine_table[:, None, :]
    qkv_full, out_full = (
        lax.all_gather(w_qkv, ("rep", "shard"), axis=0, tiled=True),
        lax.all_gather(w_out, ("rep", "shard"), axis=0, tiled=True),
    )
    read_attn = read_streams(streams_in, mix_attn[:, 0])
    normed_attn, inverse_attn = normalize(read_attn)
    low_attn = normed_attn.astype(jnp.bfloat16)
    qkv_rows = jnp.dot(low_attn, qkv_full, preferred_element_type=jnp.float32).astype(jnp.bfloat16)
    sorted_qkv = jnp.zeros_like(qkv_rows).at[deal].set(qkv_rows)
    sending = pack_owner(sorted_qkv, bin_count, HEAD_SPLIT, 3)
    packed = lax.all_to_all(sending, "shard", split_axis=0, concat_axis=1, tiled=True)
    rows_here = packed[0]
    queries = rotate(rows_here[..., :head_width].astype(jnp.float32), cosine, sine_table).astype(
        jnp.bfloat16
    )
    key_rows = rotate(
        rows_here[..., head_width : 2 * head_width].astype(jnp.float32), cosine, sine_table
    ).astype(jnp.bfloat16)
    value_rows = rows_here[..., 2 * head_width :]

    def attend_block(offset):
        scores = (
            jnp.einsum("qhd,khd->hqk", queries, key_rows, preferred_element_type=jnp.float32)
            * score_scale
        )
        scores = jnp.where(visible(segment, position, segment, position)[None], scores, -1e30)
        row_peak = jnp.max(scores, -1, keepdims=True)
        exp_scores = jnp.exp(scores - row_peak)
        row_total = jnp.sum(exp_scores, -1, keepdims=True)
        probability = (exp_scores / row_total).astype(jnp.bfloat16)
        attended = jnp.einsum(
            "hqk,khd->qhd", probability, value_rows, preferred_element_type=jnp.float32
        ).astype(jnp.bfloat16)
        return (attended, jnp.transpose((row_peak + jnp.log(row_total))[..., 0]))

    attended, log_total = lax.map(
        attend_block, jnp.arange(0, capacity, query_rows, dtype=jnp.int32)
    )
    returned = lax.all_to_all(attended, "shard", split_axis=1, concat_axis=0, tiled=True)
    attn_rows = unpack_owner(returned, bin_count, HEAD_SPLIT, 1)[deal]
    branch_attn = jnp.dot(attn_rows, out_full, preferred_element_type=jnp.float32)
    middle_streams = write_streams(
        streams_in, mix_attn[:, 1 : 1 + stream_count], branch_attn, mix_attn[:, stream_count + 1]
    )
    gu_full, down_full = (
        lax.all_gather(w_gu, ("rep", "shard"), axis=0, tiled=True),
        lax.all_gather(w_down, ("rep", "shard"), axis=0, tiled=True),
    )
    read_mlp = read_streams(middle_streams, mix_mlp[:, 0])
    normed_mlp, inverse_mlp = normalize(read_mlp)
    low_mlp = normed_mlp.astype(jnp.bfloat16)
    gate_up = jnp.dot(low_mlp, gu_full, preferred_element_type=jnp.float32)
    hidden_width = down_full.shape[1]
    up_part = gate_up[:, :hidden_width]
    gate_part = gate_up[:, hidden_width:]
    sigmoid = jax.nn.sigmoid(gate_part)
    silu_value = gate_part * sigmoid
    hidden = (silu_value * up_part).astype(jnp.bfloat16)
    branch_mlp = lax.dot_general(
        hidden, down_full, CONTRACT_LAST, preferred_element_type=jnp.float32
    )
    new_streams = write_streams(
        middle_streams, mix_mlp[:, 1 : 1 + stream_count], branch_mlp, mix_mlp[:, stream_count + 1]
    )

    def shard_major(columns):
        token_rows, column_count = columns.shape
        shaped = columns.reshape(
            token_rows, rep_size, shard_size, column_count // (rep_size * shard_size)
        )
        return shaped.transpose(0, 2, 1, 3).reshape(token_rows, column_count)

    grad_new = cotangent.astype(jnp.float32)
    gu_full, down_full = (
        lax.all_gather(w_gu, ("rep", "shard"), axis=0, tiled=True),
        lax.all_gather(w_down, ("rep", "shard"), axis=0, tiled=True),
    )
    grad_branch_mlp = jnp.sum(grad_new * mix_mlp[:, stream_count + 1][None, :, None], axis=1)
    low_grad_mlp = grad_branch_mlp.astype(jnp.bfloat16)
    grad_hidden = jnp.dot(low_grad_mlp, down_full, preferred_element_type=jnp.float32)
    grad_up = grad_hidden * silu_value
    grad_gate = grad_hidden * up_part * sigmoid * (1.0 + gate_part * (1.0 - sigmoid))
    grad_gate_up = jnp.concatenate([grad_up, grad_gate], axis=1).astype(jnp.bfloat16)
    grad_normed_mlp = lax.dot_general(
        grad_gate_up, gu_full, CONTRACT_LAST, preferred_element_type=jnp.float32
    )
    grad_read_mlp = normalize_back(grad_normed_mlp, normed_mlp, inverse_mlp)
    mix_grad_mlp = mixing_grad(middle_streams, grad_new, branch_mlp, grad_read_mlp)
    grad_middle = (
        write_back(grad_new, mix_mlp[:, 1 : 1 + stream_count])
        + grad_read_mlp[:, None, :] * mix_mlp[:, 0][None, :, None]
    )
    first = lax.dot_general(
        shard_major(low_mlp), grad_gate_up, CONTRACT_FIRST, preferred_element_type=jnp.float32
    )
    second = lax.dot_general(
        shard_major(low_grad_mlp), hidden, CONTRACT_FIRST, preferred_element_type=jnp.float32
    )
    mlp_part = lax.psum_scatter(
        jnp.concatenate([first, second], axis=1), "shard", scatter_dimension=0, tiled=True
    )
    qkv_full, out_full = (
        lax.all_gather(w_qkv, ("rep", "shard"), axis=0, tiled=True),
        lax.all_gather(w_out, ("rep", "shard"), axis=0, tiled=True),
    )
    grad_branch_attn = jnp.sum(grad_middle * mix_attn[:, stream_count + 1][None, :, None], axis=1)
    low_grad_attn = grad_branch_attn.astype(jnp.bfloat16)
    grad_attn_rows = lax.dot_general(
        low_grad_attn, out_full, CONTRACT_LAST, preferred_element_type=jnp.float32
    ).astype(jnp.bfloat16)
    sorted_grad = jnp.zeros_like(grad_attn_rows).at[deal].set(grad_attn_rows)
    grad_owner = lax.all_to_all(
        pack_owner(sorted_grad, bin_count, HEAD_SPLIT, 1),
        "shard",
        split_axis=0,
        concat_axis=1,
        tiled=True,
    )
    grad_packed = attend_back(
        packed[0], log_total[0], grad_owner[0], cosine, sine_table, segment, position
    )
    grad_home = lax.all_to_all(grad_packed[None], "shard", split_axis=1, concat_axis=0, tiled=True)
    grad_qkv = unpack_owner(grad_home, bin_count, HEAD_SPLIT, 3)[deal]
    grad_normed_attn = lax.dot_general(
        grad_qkv, qkv_full, CONTRACT_LAST, preferred_element_type=jnp.float32
    )
    grad_read_attn = normalize_back(grad_normed_attn, normed_attn, inverse_attn)
    mix_grad_attn = mixing_grad(streams_in, grad_middle, branch_attn, grad_read_attn)
    d_streams = (
        write_back(grad_middle, mix_attn[:, 1 : 1 + stream_count])
        + grad_read_attn[:, None, :] * mix_attn[:, 0][None, :, None]
    )
    first = lax.dot_general(
        shard_major(low_attn), grad_qkv, CONTRACT_FIRST, preferred_element_type=jnp.float32
    )
    second = lax.dot_general(
        shard_major(attn_rows), low_grad_attn, CONTRACT_FIRST, preferred_element_type=jnp.float32
    )
    attn_part = lax.psum_scatter(
        jnp.concatenate([first, second], axis=1), "shard", scatter_dimension=0, tiled=True
    )
    attn_part, mlp_part = (
        lax.psum_scatter(
            attn_part.astype(jnp.bfloat16), "rep", scatter_dimension=0, tiled=True
        ).astype(jnp.float32),
        lax.psum_scatter(
            mlp_part.astype(jnp.bfloat16), "rep", scatter_dimension=0, tiled=True
        ).astype(jnp.float32),
    )
    g_mix_attn, g_mix_mlp = lax.psum((mix_grad_attn, mix_grad_mlp), ("rep", "shard"))
    qkv_cols = qkv_full.shape[1]
    gu_cols = gu_full.shape[1]
    return (
        new_streams,
        d_streams,
        g_mix_attn,
        g_mix_mlp,
        attn_part[:, :qkv_cols],
        attn_part[:, qkv_cols:],
        mlp_part[:, :gu_cols],
        mlp_part[:, gu_cols:],
    )


def solution(mesh):
    return jax.shard_map(
        shards,
        mesh=mesh,
        in_specs=(
            P(("rep", "shard"), None, None),
            P(("rep", "shard"), None, None),
            P(("rep", "shard")),
            P(),
            P(),
            P(),
            P(("rep", "shard"), None),
            P(("rep", "shard"), None),
            P(("rep", "shard"), None),
            P(("rep", "shard"), None),
        ),
        out_specs=(
            P(("rep", "shard"), None, None),
            P(("rep", "shard"), None, None),
            P(),
            P(),
            P(("rep", "shard"), None),
            P(("rep", "shard"), None),
            P(("rep", "shard"), None),
            P(("rep", "shard"), None),
        ),
        check_vma=False,
    )
```

profile of v0, /device:TPU:0, one launch (start us, length us, event | category | flops | bytes accessed | tf_op | source)
XLA Modules:
  0.0 5368.2 jit_solution(17693259014147405220)
XLA Ops:
  14.5 153.7 %all-gather.5.cloned.1.call-done = bf16[2048,6144]{1,0:T(8,128)(2,1)} async-done(((bf16[64,6144]{1,0:T(8,128)(2,1)}), bf16[2048,6144]{1,0:T(8,128)(2,1)}) %all-gather.5.cloned.1.call-update) | async-done | bytes 25165840 | tf_op jit(solution)/shard_map/all_gather | solution.py:199
  168.3 12.8 convolution_convert_fusion
  211.0 40.4 all-to-all-done
  258.0 19.5 all-to-all-start.1
  312.5 20.1 multiply_reduce_fusion.5
  334.4 298.5 %all-gather.9.cloned.1.call-done = bf16[2048,16384]{1,0:T(8,128)(2,1)} async-done(((bf16[64,16384]{1,0:T(8,128)(2,1)}), bf16[2048,16384]{1,0:T(8,128)(2,1)}) %all-gather.9.cloned.1.call-update) | async-done | bytes 67108880 | tf_op jit(solution)/shard_map/all_gather | solution.py:243
  632.9 27.7 fusion.28
  660.6 168.0 %all-gather.11.cloned.1.call-done = bf16[2048,8192]{1,0:T(8,128)(2,1)} async-done(((bf16[64,8192]{1,0:T(8,128)(2,1)}), bf16[2048,8192]{1,0:T(8,128)(2,1)}) %all-gather.11.cloned.1.call-update) | async-done | bytes 33554448 | tf_op jit(solution)/shard_map/all_gather | solution.py:244
  828.7 19.3 multiply_convert_fusion.2
  847.9 29.9 fusion.56
  882.0 16.9 multiply_reduce_fusion.1
  911.8 15.5 all-to-all-done.2
  970.2 23.3 all-to-all-done.3
  1007.7 20.8 fusion.63
  1028.5 43.4 pad_maximum_fusion.1
  1076.0 24.8 fusion.64
  1100.8 46.9 fusion.3
  1147.7 132.5 %pad_maximum_fusion = f32[2048,24576]{1,0:T(8,128)} fusion(f32[2048,8192]{1,0:T(8,128)} %fusion.64, f32[2048,16384]{1,0:T(8,128)} %fusion.3), kind=kLoop, calls=%fused_computation.4 | loop fusion | flops 50331648 | bytes 402653184 | tf_op jit(solution)/shard_map/concatenate | solution.py:297
  1280.2 1151.1 %reduce-scatter.7.cloned.1.call-done = f32[128,8192]{1,0:T(8,128)} async-done(((f32[2048,8192]{1,0:T(8,128)}), f32[128,8192]{1,0:T(8,128)}) %reduce-scatter.7.cloned.1.call-update) | async-done | bytes 4194320 | tf_op jit(solution)/shard_map/reduce_scatter | solution.py:336
  2435.4 2684.4 %reduce-scatter.13.cloned.1.call-done = f32[128,24576]{1,0:T(8,128)} async-done(((f32[2048,24576]{1,0:T(8,128)}), f32[128,24576]{1,0:T(8,128)}) %reduce-scatter.13.cloned.1.call-update) | async-done | bytes 12582928
  5119.7 8.1 convert_element_type.123
  5139.0 12.1 fusion.59
  5160.3 12.0 convolution_bitcast_fusion
  5172.3 16.2 fusion.62
  5198.5 11.9 fusion.58
  5218.1 9.0 convolution_bitcast_fusion.2
  5227.2 18.6 convolution_bitcast_fusion.3
  5245.9 18.5 convolution_bitcast_fusion.4
  5264.4 9.0 convolution_bitcast_fusion.1
  5273.5 14.6 fusion.55
  5290.9 10.9 convolution_bitcast_fusion.5
  5304.4 39.8 all-reduce.1
  (260 shorter events, 222.7 us)
Async XLA Ops:
  7.2 161.1 %all-gather.5.cloned.1.call-start = ((), (), s32[]{:S(2)}) async-start(), calls=%async_computation.8 | async-start | bytes 25952256 | tf_op jit(solution)/shard_map/all_gather | solution.py:199
  7.9 298.4 %all-gather.7.cloned.1.call-start = ((), (), s32[]{:S(2)}) async-start(), calls=%async_computation.9 | async-start | bytes 8650752 | tf_op jit(solution)/shard_map/all_gather | solution.py:200
  8.7 624.2 %all-gather.9.cloned.1.call-start = ((), (), s32[]{:S(2)}) async-start(), calls=%async_computation.10 | async-start | bytes 69206016 | tf_op jit(solution)/shard_map/all_gather | solution.py:243
  9.4 819.2 %all-gather.11.cloned.1.call-start = ((), (), s32[]{:S(2)}) async-start(), calls=%async_computation.11 | async-start | bytes 34603008 | tf_op jit(solution)/shard_map/all_gather | solution.py:244
  10.9 170.2 %copy-start.50 = (f32[4]{0:T(128)}, f32[4]{0:T(128)S(1)}, u32[]{:S(2)}) copy-start(f32[4]{0:T(128)S(1)} %get-tuple-element.108) | copy-start | bytes 52
  14.2 946.2 %copy-start.4 = (f32[128,2048]{1,0:T(8,128)}, f32[128,2048]{1,0:T(8,128)S(1)}, u32[]{:S(2)}) copy-start(f32[128,2048]{1,0:T(8,128)S(1)} %get-tuple-element.100) | copy-start | bytes 3145732
  14.2 946.5 %copy-start.46 = (f32[128]{0:T(128)}, f32[128]{0:T(128)S(1)}, u32[]{:S(2)}) copy-start(f32[128]{0:T(128)S(1)} %broadcast_multiply_fusion.5) | copy-start | bytes 1540
  14.5 946.3 %copy-start.48 = (f32[128]{0:T(128)}, f32[128]{0:T(128)S(1)}, u32[]{:S(2)}) copy-start(f32[128]{0:T(128)S(1)} %add_rsqrt_fusion.1) | copy-start | bytes 1540
  196.2 55.2 %all-to-all-start = ((bf16[16,32,4,384]{3,1,2,0:T(8,128)(2,1)}), bf16[16,32,4,384]{3,1,2,0:T(8,128)(2,1)S(1)}, u32[]{:S(2)}, u32[]{:S(2)}) async-start(bf16[16,32,4,384]{3,1,2,0:T(8,128)(2,1)} %reshape.409), calls=%async_computation | async-start | bytes 3145728 | tf_op jit(solution)/shard_map/all_to_all | solution.py:208
  202.0 49.8 copy-start.37
  258.0 46.5 all-to-all-start.1
  311.0 21.6 copy-start.17
  334.4 494.2 %copy-start.40 = (bf16[128,2048]{1,0:T(8,128)(2,1)S(1)}, bf16[128,2048]{1,0:T(8,128)(2,1)}, u32[]{:S(2)}) copy-start(bf16[128,2048]{1,0:T(8,128)(2,1)} %multiply_reduce_fusion.2) | copy-start | bytes 1572868
  908.0 19.3 all-to-all-start.2
  955.8 37.7 all-to-all-start.3
  960.2 1471.2 %reduce-scatter.7.cloned.1.call-start = ((), (), s32[]{:S(2)}) async-start(), calls=%async_computation.12 | async-start | bytes 71303168 | tf_op jit(solution)/shard_map/reduce_scatter | solution.py:336
  1007.7 20.8 copy-start.6
  1071.9 4047.8 %reduce-scatter.13.cloned.1.call-start = ((), (), s32[]{:S(2)}) async-start(), calls=%async_computation.15 | async-start | bytes 213909504
  1280.2 4071.7 %reduce-scatter.9.cloned.1.call-start = ((), (), s32[]{:S(2)}) async-start(), calls=%async_computation.13 | async-start | bytes 3145728 | tf_op jit(solution)/shard_map/reduce_scatter | solution.py:340
  2435.2 2920.9 %reduce-scatter.11.cloned.1.call-start = ((), (), s32[]{:S(2)}) async-start(), calls=%async_computation.14 | async-start | bytes 9437184 | tf_op jit(solution)/shard_map/reduce_scatter | solution.py:343
  5172.2 16.3 copy-start.34
  5227.2 18.7 copy-start.11
  5227.2 18.7 copy-start.41
  5245.8 18.6 copy-start.39
  5290.8 53.4 copy-start.30
  5290.8 53.4 copy-start.31
  5290.8 53.4 copy-start.32
  5290.8 53.4 copy-start.51
  5290.8 53.4 copy-start.54
  5290.8 53.4 copy-start.55
  5290.8 53.4 copy-start.56
  5290.9 53.4 copy-start.57
  (39 other events, 209.6 us)
Sparse Core Ops, SparseCore 0:
  10.9 157.3 all-gather.4
  171.2 97.9 all-gather.6
  272.1 360.7 all-gather.8
  635.7 192.9 all-gather.10
  1072.0 1359.2 reduce-scatter.6
  2438.2 2681.5 reduce-scatter.12
  5122.0 8.7 reduce-scatter.8
  5133.2 15.6 reduce-scatter.10
where the time goes:
time: 5380 us; the launch traced here: 5370 us
  waiting for transfers between devices  4540 us (84%)
  matrix products  321 us (6%)
  other arithmetic  256 us (5%)
  local copies, waits for them, and re-layouts  165 us (3%)
    unnamed x9, waiting for transfers between devices  2690 us
    reduce_scatter x1, waiting for transfers between devices, shards(): lax.psum_scatter(jnp.concatenate([first, second], axis=1), 'shard', scatt...  1150 us
    all_gather x1, waiting for transfers between devices, shards(): lax.all_gather(w_gu, ('rep', 'shard'), axis=0, tiled=True)  298 us
    concatenate x2, other arithmetic, shards(): jnp.concatenate([first, second], axis=1)  176 us
    all_gather x1, waiting for transfers between devices, shards(): lax.all_gather(w_down, ('rep', 'shard'), axis=0, tiled=True)  168 us
    all_gather x1, waiting for transfers between devices, shards(): lax.all_gather(w_qkv, ('rep', 'shard'), axis=0, tiled=True)  154 us
  transfers between devices with their start and end apart: 12, of which 8 were waited for; matrix products, arithmetic and copies ran while one was open for 10% of the time, Pallas kernels for 0%

commit v1 on v0

v1 whole, which is shorter than its diff:
```python
import functools
import math

import jax
import jax.numpy as jnp
from jax import lax
from jax.experimental import pallas as pl
from jax.experimental.pallas import tpu as pltpu
from jax.sharding import PartitionSpec as P

HEADS = 16
HEAD_DIM = 128
GROUP = 16
EPSILON = 1e-05
MESH = pl.DeviceIdType.MESH
CONTRACT_LAST = (((1,), (1,)), ((), ()))
CONTRACT_FIRST = (((0,), (0,)), ((), ()))
MIB = 1 << 20
BF = jnp.bfloat16
F32 = jnp.float32


class Here:
    def __init__(self):
        self.rep = lax.axis_index("rep")
        shard = lax.axis_index("shard")
        self.lo = shard % GROUP
        self.base = shard - self.lo
        self.bits = [(self.lo // (1 << i)) % 2 for i in range(4)]

    def flip(self, mask):
        out = self.lo
        for i in range(4):
            if mask & (1 << i):
                out = out + (1 << i) * (1 - 2 * self.bits[i])
        return out

    def dev(self, mask):
        return (self.rep, self.base + self.flip(mask))

    def partner(self):
        return (1 - self.rep, self.base + self.lo)


def barrier(here, masks, partner):
    sem = pltpu.get_barrier_semaphore()
    targets = [here.dev(m) for m in masks]
    if partner:
        targets.append(here.partner())
    for t in targets:
        pl.semaphore_signal(sem, inc=1, device_id=t, device_id_type=MESH)
    pl.semaphore_wait(sem, len(targets))


TREE = (1, 2, 4, 8, 12)
ALL = tuple(range(1, GROUP))


def rcopy(src, dst, send, recv, dev):
    return pltpu.make_async_remote_copy(
        src_ref=src, dst_ref=dst, send_sem=send, recv_sem=recv, device_id=dev, device_id_type=MESH
    )


class Gather:
    sems = (4, 7)

    def __init__(self, here, x, out, send, recv):
        self.here, self.x, self.out, self.send, self.recv = here, x, out, send, recv
        self.half = x.shape[0] // 2
        self.sent = []

    def _go(self, block, part, j, slot, mask):
        ref = self.out.at[block, pl.ds(part * self.half, self.half)]
        c = rcopy(ref, ref, self.send.at[j, slot], self.recv.at[j, slot], self.here.dev(mask))
        c.start()
        self.sent.append(c)

    def _wait(self, j, slot, block, part):
        ref = self.out.at[block, pl.ds(part * self.half, self.half)]
        rcopy(ref, ref, self.send.at[j, slot], self.recv.at[j, slot], self.here.dev(1)).wait_recv()

    def begin(self, own_sem):
        own = pltpu.make_async_copy(self.x, self.out.at[self.here.lo], own_sem)
        own.start()
        for j in (1, 3, 2):
            c = rcopy(self.x, self.out.at[self.here.lo], self.send.at[j, 6], self.recv.at[j, 6], self.here.dev(4 * j))
            c.start()
            self.sent.append(c)
        own.wait()
        self.spread(0)

    def spread(self, j):
        b = self.here.flip(4 * j)
        if j:
            ref = self.out.at[b]
            rcopy(ref, ref, self.send.at[j, 6], self.recv.at[j, 6], self.here.dev(4)).wait_recv()
        self._go(b, 0, j, 0, 1)
        self._go(b, 1, j, 1, 2)
        self._go(b, 0, j, 2, 2)
        self._go(b, 1, j, 3, 1)

    def forward(self, j):
        m = 4 * j
        self._wait(j, 0, self.here.flip(m ^ 1), 0)
        self._go(self.here.flip(m ^ 1), 0, j, 4, 2)
        self._wait(j, 1, self.here.flip(m ^ 2), 1)
        self._go(self.here.flip(m ^ 2), 1, j, 5, 1)

    def settle(self, j):
        m = 4 * j
        self._wait(j, 2, self.here.flip(m ^ 2), 0)
        self._wait(j, 3, self.here.flip(m ^ 1), 1)
        self._wait(j, 4, self.here.flip(m ^ 3), 0)
        self._wait(j, 5, self.here.flip(m ^ 3), 1)

    def end(self):
        for c in self.sent:
            c.wait_send()

    ORDER = (0, 1, 3, 2)


def run_gathers(gathers, own_sems):
    for i, g in enumerate(gathers):
        if i == 0:
            g.begin(own_sems.at[0])
        order = g.ORDER
        g.spread(order[1])
        g.forward(order[0])
        g.spread(order[2])
        g.forward(order[1])
        g.spread(order[3])
        g.forward(order[2])
        if i + 1 < len(gathers):
            gathers[i + 1].begin(own_sems.at[i + 1])
        g.forward(order[3])
    for g in gathers:
        for j in range(4):
            g.settle(j)


def rowwise(n, step, body):
    def at(i, carry):
        body(pl.ds(pl.multiple_of(i * step, step), step))
        return carry

    lax.fori_loop(0, n // step, at, 0)


class Scatter:
    sems = (4, 7)

    @staticmethod
    def scratch(rows, d):
        h = rows // 2
        return [
            pltpu.VMEM((4, 4, h, d), BF),
            pltpu.VMEM((4, 2, h, d), BF),
            pltpu.VMEM((4, 2, h, d), BF),
            pltpu.VMEM((4, rows, d), BF),
            pltpu.VMEM((4, rows, d), BF),
            pltpu.SemaphoreType.DMA(Scatter.sems),
            pltpu.SemaphoreType.DMA(Scatter.sems),
        ]

    def __init__(self, here, part, scratch):
        self.here, self.part = here, part
        self.first, self.second, self.mid, self.zin, self.zout, self.send, self.recv = scratch
        self.rows = part.shape[1]
        self.half = self.rows // 2
        self.sent = []

    def _copy(self, j, slot, src, dst, mask):
        return rcopy(src, dst, self.send.at[j, slot], self.recv.at[j, slot], self.here.dev(mask))

    def _go(self, *a):
        c = self._copy(*a)
        c.start()
        self.sent.append(c)

    def _piece(self, mask, part):
        return self.part.at[self.here.flip(mask), pl.ds(part * self.half, self.half)]

    def start(self, j):
        m = 4 * j
        self._go(j, 1, self._piece(m ^ 3, 0), self.first.at[j, 1], 2)
        self._go(j, 3, self._piece(m ^ 3, 1), self.first.at[j, 3], 1)
        self._go(j, 0, self._piece(m ^ 2, 0), self.first.at[j, 0], 2)
        self._go(j, 2, self._piece(m ^ 1, 1), self.first.at[j, 2], 1)

    def cross(self, j):
        m = 4 * j
        h = self.half
        for slot, mask, part, to in ((1, 1, 0, 1), (3, 2, 1, 2)):
            self._copy(j, slot, self.first.at[j, slot], self.first.at[j, slot], 1).wait_recv()
            own = self._piece(m ^ mask, part)

            def body(r, own=own, slot=slot, part=part):
                self.mid[j, part, r] = (own[r].astype(F32) + self.first[j, slot, r].astype(F32)).astype(BF)

            rowwise(h, 16, body)
            self._go(j, 4 + part, self.mid.at[j, part], self.second.at[j, part], to)

    def finish(self, j, out=None):
        m = 4 * j
        h = self.half
        for part, slot in ((0, 0), (1, 2)):
            self._copy(j, slot, self.first.at[j, slot], self.first.at[j, slot], 1).wait_recv()
            self._copy(j, 4 + part, self.second.at[j, part], self.second.at[j, part], 1).wait_recv()
        if out is not None:
            for k in (1, 2, 3):
                self._copy(k, 6, self.zin.at[k], self.zin.at[k], 4).wait_recv()
        for part, slot in ((0, 0), (1, 2)):
            own = self._piece(m, part)

            def body(r, own=own, part=part, slot=slot):
                total = own[r].astype(F32) + self.first[j, slot, r].astype(F32) + self.second[j, part, r].astype(F32)
                at = pl.ds(part * h + r.start, r.size)
                if out is None:
                    self.zout[j, at] = total.astype(BF)
                else:
                    for k in (1, 2, 3):
                        total = total + self.zin[k, at].astype(F32)
                    out[at] = total.astype(out.dtype)

            rowwise(h, 16, body)
        if out is None:
            self._go(j, 6, self.zout.at[j], self.zin.at[j], m)

    def end(self):
        for c in self.sent:
            c.wait_send()

    ORDER = (2, 3, 1, 0)


def run_scatters(scatters, outs):
    for i, (s, out) in enumerate(zip(scatters, outs)):
        order = s.ORDER
        if i == 0:
            s.start(order[0])
        s.start(order[1])
        s.cross(order[0])
        s.start(order[2])
        s.cross(order[1])
        s.finish(order[0])
        s.start(order[3])
        s.cross(order[2])
        s.finish(order[1])
        if i + 1 < len(scatters):
            scatters[i + 1].start(order[0])
        s.cross(order[3])
        s.finish(order[2])
        s.finish(order[3], out)
    for s in scatters:
        s.end()


def any_spec(n):
    return [pl.BlockSpec(memory_space=pl.ANY)] * n


def vmem_spec(n):
    return [pl.BlockSpec(memory_space=pltpu.VMEM)] * n


def params(cid, mib=60):
    return pltpu.CompilerParams(collective_id=cid, has_side_effects=True, vmem_limit_bytes=mib * MIB)


def exchange_columns(here, src, dst, width, cols, send, recv, own_sem):
    copies = []
    own = []
    for i, c in enumerate(cols):
        for m in range(GROUP):
            peer = here.flip(m)
            at = src.at[:, :, pl.ds(pl.multiple_of(c + peer * width, 128), width)]
            to = dst.at[here.rep, :, here.lo, :, pl.ds(i * width, width)]
            if m == 0:
                cp = pltpu.make_async_copy(at, to, own_sem.at[i])
                cp.start()
                own.append(cp)
            else:
                cp = rcopy(at, to, send.at[i, m], recv.at[i, m], here.dev(m))
                cp.start()
                copies.append(cp)

    def arrive():
        for cp in own:
            cp.wait()
        for i, c in enumerate(cols):
            for m in ALL:
                to = dst.at[here.rep, :, here.flip(m), :, pl.ds(i * width, width)]
                rcopy(to, to, send.at[i, m], recv.at[i, m], here.dev(m)).wait_recv()

    def end():
        for cp in copies:
            cp.wait_send()

    return arrive, end


def front_kernel(
    n1, dy2, wqkv, wout, wgu, wdn,
    n1g, dy2g, qkvs, outs, gus, dns,
    gsend, grecv, own, csend, crecv, cown, psend, precv,
):
    here = Here()
    barrier(here, ALL, True)
    q = exchange_columns(here, wqkv, qkvs, 128, (0, 2048, 4096), csend.at[0], crecv.at[0], cown.at[0])
    half = wgu.shape[2] // 2
    ga = Gather(here, n1, n1g, gsend.at[0], grecv.at[0])
    gb = Gather(here, dy2, dy2g, gsend.at[1], grecv.at[1])
    gc = Gather(here, wout, outs.at[here.rep], gsend.at[2], grecv.at[2])
    ga.begin(own.at[0])
    u = exchange_columns(here, wgu, gus, half // GROUP, (0, half), csend.at[1], crecv.at[1], cown.at[1])
    d = exchange_columns(here, wdn, dns, half // GROUP, (0,), csend.at[2], crecv.at[2], cown.at[2])
    gathers = [ga, gb, gc]
    for i, g in enumerate(gathers):
        order = g.ORDER
        g.spread(order[1])
        g.forward(order[0])
        g.spread(order[2])
        g.forward(order[1])
        g.spread(order[3])
        g.forward(order[2])
        if i + 1 < len(gathers):
            gathers[i + 1].begin(own.at[i + 1])
        g.forward(order[3])
    passes = []
    for i, ((arrive, _), dst) in enumerate(zip((q, u, d), (qkvs, gus, dns))):
        arrive()
        cp = rcopy(dst.at[here.rep], dst.at[here.rep], psend.at[i], precv.at[i], here.partner())
        cp.start()
        passes.append((cp, dst))
    for g in gathers:
        for j in range(4):
            g.settle(j)
    cp = rcopy(outs.at[here.rep], outs.at[here.rep], psend.at[3], precv.at[3], here.partner())
    cp.start()
    passes.append((cp, outs))
    for i, (cp, dst) in enumerate(passes):
        cp.wait_send()
        other = dst.at[1 - here.rep]
        rcopy(other, other, psend.at[i], precv.at[i], here.partner()).wait_recv()
    for g in gathers:
        g.end()
    for _, end in (q, u, d):
        end()


def front(n1, dy2, wqkv, wout, wgu, wdn, cid):
    hi, rows, _ = wqkv.shape
    d = n1.shape[1]
    ff = wdn.shape[2]
    shape = lambda *s: jax.ShapeDtypeStruct(s, BF)
    out_rows = wout.shape[0]
    return pl.pallas_call(
        front_kernel,
        out_shape=(
            shape(GROUP, *n1.shape),
            shape(GROUP, *dy2.shape),
            shape(2, hi, GROUP, rows, 3 * HEAD_DIM),
            shape(2, GROUP, out_rows, wout.shape[1]),
            shape(2, hi, GROUP, rows, 2 * ff // GROUP),
            shape(2, hi, GROUP, rows, ff // GROUP),
        ),
        in_specs=any_spec(6),
        out_specs=any_spec(6),
        scratch_shapes=[
            pltpu.SemaphoreType.DMA((3,) + Gather.sems),
            pltpu.SemaphoreType.DMA((3,) + Gather.sems),
            pltpu.SemaphoreType.DMA((3,)),
            pltpu.SemaphoreType.DMA((3, 3, GROUP)),
            pltpu.SemaphoreType.DMA((3, 3, GROUP)),
            pltpu.SemaphoreType.DMA((3, 3)),
            pltpu.SemaphoreType.DMA((4,)),
            pltpu.SemaphoreType.DMA((4,)),
        ],
        compiler_params=params(cid, 16),
    )(n1, dy2, wqkv, wout, wgu, wdn)


def gather_kernel(x, out, send, recv, own):
    here = Here()
    barrier(here, TREE, False)
    g = Gather(here, x, out, send, recv)
    run_gathers([g], own)
    g.end()


def gather(x, cid):
    return pl.pallas_call(
        gather_kernel,
        out_shape=jax.ShapeDtypeStruct((GROUP,) + x.shape, x.dtype),
        in_specs=any_spec(1),
        out_specs=pl.BlockSpec(memory_space=pl.ANY),
        scratch_shapes=[
            pltpu.SemaphoreType.DMA(Gather.sems),
            pltpu.SemaphoreType.DMA(Gather.sems),
            pltpu.SemaphoreType.DMA((1,)),
        ],
        compiler_params=params(cid, 16),
    )(x)


def swap_kernel(x, out, send, recv, own):
    here = Here()
    barrier(here, ALL, False)
    cps = []
    for m in ALL:
        c = rcopy(x.at[here.flip(m)], out.at[here.lo], send.at[m], recv.at[m], here.dev(m))
        c.start()
        cps.append(c)
    c = pltpu.make_async_copy(x.at[here.lo], out.at[here.lo], own)
    c.start()
    c.wait()
    for m in ALL:
        ref = out.at[here.flip(m)]
        rcopy(ref, ref, send.at[m], recv.at[m], here.dev(m)).wait_recv()
    for c in cps:
        c.wait_send()


def swap(x, cid):
    return pl.pallas_call(
        swap_kernel,
        out_shape=jax.ShapeDtypeStruct(x.shape, x.dtype),
        in_specs=any_spec(1),
        out_specs=pl.BlockSpec(memory_space=pl.ANY),
        scratch_shapes=[
            pltpu.SemaphoreType.DMA((GROUP,)),
            pltpu.SemaphoreType.DMA((GROUP,)),
            pltpu.SemaphoreType.DMA,
        ],
        compiler_params=params(cid, 16),
    )(x)


def pair_add(here, g, inbox, total, send, recv):
    cp = rcopy(g.at[1 - here.rep], inbox, send, recv, here.partner())
    cp.start()
    cp.wait()

    def body(r):
        total[r] = (g[here.rep, r].astype(F32) + inbox[r].astype(F32)).astype(BF)

    rowwise(inbox.shape[0], 16, body)


def send_home(here, total, out, send, recv, own):
    rows = out.shape[1]
    cps = []
    for m in ALL:
        at = total.at[pl.ds(pl.multiple_of(here.flip(m) * rows, rows), rows)]
        c = rcopy(at, out.at[here.lo], send.at[m], recv.at[m], here.dev(m))
        c.start()
        cps.append(c)
    at = total.at[pl.ds(pl.multiple_of(here.lo * rows, rows), rows)]
    c = pltpu.make_async_copy(at, out.at[here.lo], own)
    c.start()
    c.wait()

    def end():
        for m in ALL:
            ref = out.at[here.flip(m)]
            rcopy(ref, ref, send.at[m], recv.at[m], here.dev(m)).wait_recv()
        for c in cps:
            c.wait_send()

    return end


def mlp_home_kernel(g, out, inbox, total, psend, precv, send, recv, own):
    here = Here()
    barrier(here, ALL, True)
    pair_add(here, g, inbox, total, psend, precv)
    send_home(here, total, out, send, recv, own)()


def home_scratch(n, w):
    return [
        pltpu.VMEM((n, w), BF),
        pltpu.VMEM((n, w), BF),
        pltpu.SemaphoreType.DMA,
        pltpu.SemaphoreType.DMA,
        pltpu.SemaphoreType.DMA((GROUP,)),
        pltpu.SemaphoreType.DMA((GROUP,)),
        pltpu.SemaphoreType.DMA,
    ]


def mlp_home(g, cid):
    _, n, w = g.shape
    return pl.pallas_call(
        mlp_home_kernel,
        out_shape=jax.ShapeDtypeStruct((GROUP, n // GROUP, w), BF),
        in_specs=vmem_spec(1),
        out_specs=pl.BlockSpec(memory_space=pl.ANY),
        scratch_shapes=home_scratch(n, w),
        compiler_params=params(cid),
    )(g)


def scatter_kernel(a, b, aout, bout, *scratch):
    here = Here()
    barrier(here, TREE, False)
    n = len(scratch) // 2
    run_scatters([Scatter(here, a, scratch[:n]), Scatter(here, b, scratch[n:])], [aout, bout])


def scatter_two(a, b, cid):
    _, rows, d = a.shape
    return pl.pallas_call(
        scatter_kernel,
        out_shape=(jax.ShapeDtypeStruct((rows, d), F32),) * 2,
        in_specs=vmem_spec(2),
        out_specs=tuple(vmem_spec(2)),
        scratch_shapes=Scatter.scratch(rows, d) * 2,
        compiler_params=params(cid),
    )(a, b)


def back_kernel(dn, gout, gqkv, dn_out, gout_out, gqkv_out, *scratch):
    here = Here()
    barrier(here, ALL, True)
    n = len(Scatter.scratch(16, 128))
    s1, scratch = scratch[:n], scratch[n:]
    s2, scratch = scratch[:n], scratch[n:]
    (obox, osum, osend, orecv), scratch = scratch[:4], scratch[4:]
    pair_add(here, gqkv, *scratch[:4])
    end = send_home(here, scratch[1], gqkv_out, *scratch[4:])
    pair_add(here, gout, obox, osum, osend, orecv)
    sums = osum.reshape(GROUP, gout.shape[1] // GROUP, gout.shape[2])
    run_scatters([Scatter(here, dn, s1), Scatter(here, sums, s2)], [dn_out, gout_out])
    end()


def back(dn, gout, gqkv, cid):
    _, rows, d = dn.shape
    n, w = gqkv.shape[1:]
    on, od = gout.shape[1:]
    return pl.pallas_call(
        back_kernel,
        out_shape=(
            jax.ShapeDtypeStruct((rows, d), F32),
            jax.ShapeDtypeStruct((on // GROUP, od), F32),
            jax.ShapeDtypeStruct((GROUP, n // GROUP, w), BF),
        ),
        in_specs=vmem_spec(3),
        out_specs=(*vmem_spec(2), *any_spec(1)),
        scratch_shapes=[
            *Scatter.scratch(rows, d),
            *Scatter.scratch(on // GROUP, od),
            pltpu.VMEM((on, od), BF),
            pltpu.VMEM((on, od), BF),
            pltpu.SemaphoreType.DMA,
            pltpu.SemaphoreType.DMA,
            *home_scratch(n, w),
        ],
        compiler_params=params(cid),
    )(dn, gout, gqkv)


def normalize(inputs):
    centred = inputs - jnp.mean(inputs, -1, keepdims=True)
    inverse = lax.rsqrt(jnp.mean(centred * centred, -1, keepdims=True) + EPSILON)
    return (centred * inverse, inverse)


def normalize_back(grad_out, normed, inverse):
    return inverse * (
        grad_out
        - jnp.mean(grad_out, -1, keepdims=True)
        - normed * jnp.mean(grad_out * normed, -1, keepdims=True)
    )


def write_streams(streams, mixing, branch, out_weights):
    result = branch[:, None, :] * out_weights[None, :, None]
    for source in range(streams.shape[1]):
        result = result + streams[:, source, None, :] * mixing[source][None, :, None]
    return result


def write_back(grad_out, mixing):
    result = jnp.zeros_like(grad_out)
    for target in range(grad_out.shape[1]):
        result = result + grad_out[:, target, None, :] * mixing[:, target][None, :, None]
    return result


def mixing_grad(streams, grad_out, branch, grad_read):
    highest = lax.Precision.HIGHEST
    first = jnp.einsum("tjd,td->j", streams, grad_read, precision=highest)
    middle = jnp.einsum("tjd,tid->ji", streams, grad_out, precision=highest)
    final_cols = jnp.einsum("td,tid->i", branch, grad_out, precision=highest)
    return jnp.concatenate([first[:, None], middle, final_cols[:, None]], axis=1)


def slot_layout(lengths_row, capacity):
    seq_count = lengths_row.shape[-1]
    seq_ends = jnp.cumsum(lengths_row, axis=-1)
    slot_index = jnp.arange(capacity, dtype=jnp.int32)
    segment = jnp.sum((slot_index[:, None] >= seq_ends[..., None, :]).astype(jnp.int32), axis=-1)
    seq_starts = seq_ends - lengths_row
    chosen = (segment[..., None] == jnp.arange(seq_count, dtype=jnp.int32)).astype(jnp.int32)
    start_of = jnp.sum(chosen * seq_starts[..., None, :], axis=-1)
    is_live = segment < seq_count
    segment = jnp.where(is_live, segment, seq_count + slot_index)
    position = jnp.where(is_live, slot_index - start_of, 0)
    return (segment, position)


def rope_tables(position, head_width):
    half_width = head_width // 2
    frequency = jnp.exp(
        jnp.arange(half_width, dtype=jnp.float32) * (-2.0 * math.log(10000.0) / head_width)
    )
    angles = position.astype(jnp.float32)[..., None] * frequency
    return (jnp.cos(angles), jnp.sin(angles))


def rotate(inputs, cosine, sine_table):
    half_width = inputs.shape[-1] // 2
    first = inputs[..., :half_width]
    second = inputs[..., half_width:]
    return jnp.concatenate(
        [first * cosine - second * sine_table, second * cosine + first * sine_table], axis=-1
    )


def dot(a, b):
    return jnp.dot(a, b, preferred_element_type=F32)


def dot_t(a, b):
    return lax.dot_general(a, b, CONTRACT_LAST, preferred_element_type=F32)


def t_dot(a, b):
    return lax.dot_general(a, b, CONTRACT_FIRST, preferred_element_type=F32)


def shards(streams, cotangent, deal, lengths, mix_attn, mix_mlp, w_qkv, w_out, w_gu, w_down):
    tokens, stream_count, width = streams.shape
    shard_size = lax.axis_size("shard")
    hi = shard_size // GROUP
    hi_groups = [[h * GROUP + l for h in range(hi)] for l in range(GROUP)]
    shard = lax.axis_index("shard")
    my_hi = shard // GROUP
    bin_count = shard_size // 4
    my_bins = bin_count // hi
    per_bin = tokens // bin_count
    capacity = per_bin * shard_size
    ff = w_down.shape[1]

    def swap_hi(rows):
        if hi == 1:
            return rows
        return lax.all_to_all(rows, "shard", 0, 0, axis_index_groups=hi_groups, tiled=True)

    def to_bins(rows):
        return swap_hi(rows).reshape(hi, my_bins, per_bin, -1).swapaxes(0, 1).reshape(tokens, -1)

    def from_bins(rows):
        return swap_hi(rows.reshape(my_bins, hi, per_bin, -1).swapaxes(0, 1).reshape(tokens, -1))

    def gather_hi(rows):
        if hi == 1:
            return rows[None]
        return lax.all_gather(rows, "shard", axis_index_groups=hi_groups)

    def sum_hi(rows):
        if hi == 1:
            return rows[0]
        return lax.psum_scatter(rows, "shard", axis_index_groups=hi_groups)

    sorter = (jnp.arange(tokens, dtype=jnp.int32)[:, None] == deal[None, :]).astype(BF)

    streams_in = streams.astype(F32)
    grad_new = cotangent.astype(F32)
    read_attn = jnp.sum(streams_in * mix_attn[:, 0][None, :, None], axis=1)
    normed_attn, inverse_attn = normalize(read_attn)
    low_attn = to_bins(dot(sorter, normed_attn.astype(BF)).astype(BF))
    low_grad_mlp = jnp.sum(grad_new * mix_mlp[:, stream_count + 1][None, :, None], axis=1).astype(BF)

    n1g, dy2g, qkvs, outs, gus, dns = front(
        low_attn, low_grad_mlp, gather_hi(w_qkv), gather_hi(w_out).reshape(-1, width), gather_hi(w_gu), gather_hi(w_down), 1
    )
    rows = w_qkv.shape[0]
    n1g = n1g.reshape(GROUP * tokens, width)
    dy2g = dy2g.reshape(GROUP * tokens, width)
    qkvs = qkvs.reshape(width, 3 * HEAD_DIM)
    outs = outs.reshape(2, GROUP, hi, rows, width).swapaxes(1, 2).reshape(width, width)
    gus = gus.reshape(width, 2 * ff // GROUP)
    dns = dns.reshape(width, ff // GROUP)

    bins = lax.axis_index("rep") * bin_count + my_hi * my_bins
    lengths_here = lax.dynamic_slice_in_dim(lengths, bins, my_bins, 0)
    segment, position = slot_layout(lengths_here, capacity)

    def local_order(x):
        return x.reshape(my_bins, hi, GROUP, per_bin).swapaxes(1, 2).reshape(my_bins, capacity)

    segment, position = local_order(segment), local_order(position)
    cosine, sine = rope_tables(position, HEAD_DIM)
    slots = GROUP * tokens // my_bins // GROUP

    def by_bin(x):
        return x.reshape(GROUP, my_bins, slots, -1).swapaxes(0, 1).reshape(my_bins, capacity, -1)

    def by_token(x):
        return x.reshape(my_bins, GROUP, slots, -1).swapaxes(0, 1).reshape(GROUP, tokens, -1)

    scale = 1.0 / math.sqrt(HEAD_DIM)
    qkv = by_bin(dot(n1g, qkvs).astype(BF))
    queries = rotate(qkv[..., :HEAD_DIM].astype(F32), cosine, sine).astype(BF)
    keys = rotate(qkv[..., HEAD_DIM : 2 * HEAD_DIM].astype(F32), cosine, sine).astype(BF)
    values = qkv[..., 2 * HEAD_DIM :]
    seen = (segment[:, :, None] == segment[:, None, :]) & (position[:, None, :] <= position[:, :, None])
    scores = jnp.einsum("bqd,bkd->bqk", queries, keys, preferred_element_type=F32) * scale
    scores = jnp.where(seen, scores, -1e30)
    peak = jnp.max(scores, -1, keepdims=True)
    weights = jnp.exp(scores - peak)
    probability = weights / jnp.sum(weights, -1, keepdims=True)
    low_probability = probability.astype(BF)
    attended = jnp.einsum("bqk,bkd->bqd", low_probability, values, preferred_element_type=F32).astype(BF)
    home = swap(by_token(attended), 2)
    attn_sorted = from_bins(home.swapaxes(0, 1).reshape(tokens, width))
    attn_rows = t_dot(sorter, attn_sorted).astype(BF)

    branch_attn = dot(attn_rows, outs)
    middle_streams = write_streams(
        streams_in, mix_attn[:, 1 : 1 + stream_count], branch_attn, mix_attn[:, stream_count + 1]
    )
    read_mlp = jnp.sum(middle_streams * mix_mlp[:, 0][None, :, None], axis=1)
    normed_mlp, inverse_mlp = normalize(read_mlp)
    n2g = gather(normed_mlp.astype(BF), 3).reshape(GROUP * tokens, width)
    gate_up = dot(n2g, gus)
    up_part = gate_up[:, : ff // GROUP]
    gate_part = gate_up[:, ff // GROUP :]
    sigmoid = jax.nn.sigmoid(gate_part)
    silu_value = gate_part * sigmoid
    hidden = (silu_value * up_part).astype(BF)
    y2_part = dot_t(hidden, dns).astype(BF).reshape(GROUP, tokens, width)
    grad_hidden = dot(dy2g, dns)
    grad_up = grad_hidden * silu_value
    grad_gate = grad_hidden * up_part * sigmoid * (1.0 + gate_part * (1.0 - sigmoid))
    grad_gate_up = jnp.concatenate([grad_up, grad_gate], axis=1).astype(BF)
    dn2_part = dot_t(grad_gate_up, gus).astype(BF).reshape(GROUP, tokens, width)
    branch_mlp, grad_normed_mlp = scatter_two(y2_part, dn2_part, 4)
    grad_read_mlp = normalize_back(grad_normed_mlp, normed_mlp, inverse_mlp)
    new_streams = write_streams(
        middle_streams, mix_mlp[:, 1 : 1 + stream_count], branch_mlp, mix_mlp[:, stream_count + 1]
    )
    mix_grad_mlp = mixing_grad(middle_streams, grad_new, branch_mlp, grad_read_mlp)
    grad_middle = (
        write_back(grad_new, mix_mlp[:, 1 : 1 + stream_count])
        + grad_read_mlp[:, None, :] * mix_mlp[:, 0][None, :, None]
    )
    g_mlp = jnp.concatenate([t_dot(n2g, grad_gate_up), t_dot(dy2g, hidden)], axis=1).astype(BF)

    def row_order(x):
        return x.reshape(2, hi, GROUP, rows, -1).swapaxes(1, 2).reshape(2, GROUP * hi * rows, -1)

    def own_rows(x):
        x = x.astype(F32).reshape(GROUP, hi, rows, -1).transpose(1, 2, 0, 3)
        return sum_hi(x.reshape(hi, rows, -1)).reshape(rows, GROUP, -1)

    g_mlp = own_rows(mlp_home(row_order(g_mlp), 5))
    low_grad_attn = jnp.sum(grad_middle * mix_attn[:, stream_count + 1][None, :, None], axis=1).astype(BF)
    grad_attn = dot_t(low_grad_attn, outs).astype(BF)
    grad_sorted = to_bins(dot(sorter, grad_attn).astype(BF))
    d_out = by_bin(swap(grad_sorted.reshape(tokens, GROUP, HEAD_DIM).swapaxes(0, 1), 6))
    grad_values = jnp.einsum("bqk,bqd->bkd", low_probability, d_out, preferred_element_type=F32)
    grad_probs = jnp.einsum("bqd,bkd->bqk", d_out, values, preferred_element_type=F32)
    shared = jnp.sum(grad_probs * probability, -1, keepdims=True)
    grad_scores = (probability * (grad_probs - shared)).astype(BF)
    grad_query = jnp.einsum("bqk,bkd->bqd", grad_scores, keys, preferred_element_type=F32) * scale
    grad_keys = jnp.einsum("bqk,bqd->bkd", grad_scores, queries, preferred_element_type=F32) * scale
    grad_qkv = by_token(
        jnp.concatenate(
            [rotate(grad_query, cosine, -sine), rotate(grad_keys, cosine, -sine), grad_values], axis=-1
        ).astype(BF)
    ).reshape(GROUP * tokens, 3 * HEAD_DIM)
    dn1_part = dot_t(grad_qkv, qkvs).astype(BF).reshape(GROUP, tokens, width)
    g_qkv = row_order(t_dot(n1g, grad_qkv).astype(BF))
    g_out = row_order(t_dot(attn_rows, low_grad_attn).astype(BF))
    dn1, g_out, g_qkv = back(dn1_part, g_out, g_qkv, 7)
    g_out = sum_hi(g_out.reshape(hi, rows, width))
    g_qkv = own_rows(g_qkv)
    dn1 = lax.dot_general(
        sorter.astype(F32), from_bins(dn1), CONTRACT_FIRST, precision=lax.Precision.HIGHEST, preferred_element_type=F32
    )
    grad_read_attn = normalize_back(dn1, normed_attn, inverse_attn)
    mix_grad_attn = mixing_grad(streams_in, grad_middle, branch_attn, grad_read_attn)
    d_streams = (
        write_back(grad_middle, mix_attn[:, 1 : 1 + stream_count])
        + grad_read_attn[:, None, :] * mix_attn[:, 0][None, :, None]
    )
    g_mix_attn, g_mix_mlp = lax.psum((mix_grad_attn, mix_grad_mlp), ("rep", "shard"))
    block = ff // GROUP
    return (
        new_streams,
        d_streams,
        g_mix_attn,
        g_mix_mlp,
        g_qkv.reshape(rows, GROUP, 3, HEAD_DIM).swapaxes(1, 2).reshape(rows, -1),
        g_out,
        jnp.concatenate([g_mlp[:, :, :block].reshape(rows, ff), g_mlp[:, :, block : 2 * block].reshape(rows, ff)], axis=1),
        g_mlp[:, :, 2 * block :].reshape(rows, ff),
    )


def solution(mesh):
    both = ("rep", "shard")
    return jax.shard_map(
        shards,
        mesh=mesh,
        in_specs=(
            P(both, None, None),
            P(both, None, None),
            P(both),
            P(),
            P(),
            P(),
            P(both, None),
            P(both, None),
            P(both, None),
            P(both, None),
        ),
        out_specs=(
            P(both, None, None),
            P(both, None, None),
            P(),
            P(),
            P(both, None),
            P(both, None),
            P(both, None),
            P(both, None),
        ),
        check_vma=False,
    )
```

time: 5380 us -> 1210 us (0.22)
  waiting for transfers between devices: 4540 us -> 0 us
  Pallas kernels: 0 us -> 738 us
  other arithmetic: 256 us -> 79.8 us
  matrix products: 321 us -> 220 us
    unnamed x9 -> x0, waiting for transfers between devices: 2690 us -> none
    reduce_scatter x3 -> x0, waiting for transfers between devices: 1150 us -> none  [the longest x1 1150 us: shards(): lax.psum_scatter(jnp.concatenate([first, second], axis=1), 'shard', scatt...]
    pallas_call x0 -> x7, Pallas kernels: none -> 738 us  [the longest x1 251 us: front(): pl.pallas_call(front_kernel, out_shape=(shape(GROUP, *n1.shape), shape(GR...]
    all_gather x4 -> x0, waiting for transfers between devices: 620 us -> none  [the longest x1 298 us: shards(): lax.all_gather(w_gu, ('rep', 'shard'), axis=0, tiled=True)]
    concatenate x3 -> x2, other arithmetic: 178 us -> 5.66 us  [the longest x1 3.22 us: shards(): jnp.concatenate([t_dot(n2g, grad_gate_up), t_dot(dy2g, hidden)], axis=1)]
    dot_general x24 -> x26, matrix products: 321 us -> 215 us  [the longest x6 52.3 us: dot(): return jnp.dot(a, b, preferred_element_type=F32)]
    all_to_all x4 -> x0, waiting for transfers between devices: 79.1 us -> none  [the longest x1 40.4 us: shards(): lax.all_to_all(sending, 'shard', split_axis=0, concat_axis=1, tiled=True)]
  transfers between devices with their start and end apart: 12 -> 0, of which waited for: 8 -> 0; matrix products, arithmetic and copies ran while one was open for 10% -> 0% of each run, Pallas kernels for 0% -> 0%
where the time goes in v1:
time: 1210 us; the launch traced here: 1200 us
  Pallas kernels  738 us (61%)
  matrix products  220 us (18%)
  local copies, waits for them, and re-layouts  122 us (10%)
  other arithmetic  79.8 us (7%)
  blocking collectives  38.4 us (3%)
    pallas_call x1, Pallas kernels, front(): pl.pallas_call(front_kernel, out_shape=(shape(GROUP, *n1.shape), shape(GR...  251 us
    pallas_call x1, Pallas kernels, scatter_two(): pl.pallas_call(scatter_kernel, out_shape=(jax.ShapeDtypeStruct((rows, d),...  169 us
    pallas_call x1, Pallas kernels, back(): pl.pallas_call(back_kernel, out_shape=(jax.ShapeDtypeStruct((rows, d), F3...  139 us
    pallas_call x1, Pallas kernels, gather(): pl.pallas_call(gather_kernel, out_shape=jax.ShapeDtypeStruct((GROUP,) + x...  76.2 us
    pallas_call x1, Pallas kernels, mlp_home(): pl.pallas_call(mlp_home_kernel, out_shape=jax.ShapeDtypeStruct((GROUP, n...  69.8 us
    dot_general x6, matrix products, dot(): return jnp.dot(a, b, preferred_element_type=F32)  52.3 us
    psum x1, blocking collectives, shards(): lax.psum((mix_grad_attn, mix_grad_mlp), ('rep', 'shard'))  38.4 us
    dot_general x5, matrix products, t_dot(): return lax.dot_general(a, b, CONTRACT_FIRST, preferred_element_type=F32)  37.7 us

profile of v1, /device:TPU:0, one launch (start us, length us, event | category | flops | bytes accessed | tf_op | source)
XLA Modules:
  0.0 1201.1 jit_solution(14287236722296545225)
XLA Ops:
  10.2 250.5 %shard_map.161 = (bf16[16,128,2048]{2,1,0:T(8,128)(2,1)}, bf16[16,128,2048]{2,1,0:T(8,128)(2,1)S(1)}, bf16[2,1,16,64,384]{4,3,2,1,0:T(8,128)(2,1)S(1)}, bf16[2,1...) custom-call(bf16[128,2048]{1,0:T(8,128)(2,1)S(1)} %convolution_conve, ...), custom_call_target="tpu_custom_call" | custom-call | tf_op jit(solution)/shard_map/pallas_call | solution.py:359
  260.8 13.7 %convolution_convert_fusion.5 = bf16[2048,384]{1,0:T(8,128)(2,1)S(1)} fusion(bf16[2048,2048]{1,0:T(8,128)(2,1)} %bitcast.3, bf16[2048,384]{1,0:T(8,128)(2,1)S(1)} %bitcast.210), kind=kOutput, calls=%fused_computation.31 | convolution fusion | flops 3222011904 | bytes 11534336 | tf_op jit(solution)/shard_map/dot_general | solution.py:635
  274.9 5.7 fusion.45
  291.9 20.2 %shard_map.162 = bf16[16,128,128]{2,1,0:T(8,128)(2,1)S(1)} custom-call(bf16[16,128,128]{2,1,0:T(8,128)(2,1)S(1)} %bitcast.200), custom_call_target="tpu_custom_call" | custom-call | tf_op jit(solution)/shard_map/pallas_call | solution.py:427
  313.5 5.7 fusion.86
  337.0 20.1 %multiply_reduce_fusion.5 = (f32[128]{0:T(128)S(1)}, f32[128,2048]{0,1:T(8,128)}, f32[128,4,2048]{0,1,2:T(4,128)}) fusion(f32[4]{0:T(128)S(1)} %copy-done.49, f32[4]{0:T(128)S(1)} %get-tuple-element.131, f32[128,2048]{0,1:T(8,128)} %copy.242, f32[4]{0:T(128)S(1)} %get-tuple-element.132, f32[128,2048]{0,1:T(8,128)} %copy.241, f32[4]{0:T(128)S(1)} %get-tuple-element.133, ...), kind=kLoop, calls=%fused_computation.28 | loop fusion | flops 12320640 | bytes 10486368 | tf_op jit(solution)/shard_map/reduce_sum | solution.py:567
  362.5 76.2 %shard_map.163 = bf16[16,128,2048]{2,1,0:T(8,128)(2,1)S(1)} custom-call(bf16[128,2048]{1,0:T(8,128)(2,1)S(1)} %fusion.57.x), custom_call_target="tpu_custom_call" | custom-call | tf_op jit(solution)/shard_map/pallas_call | solution.py:394
  438.8 15.8 %fusion.87 = f32[2048,1024]{0,1:T(8,128)} fusion(bf16[2048,2048]{1,0:T(8,128)(2,1)S(1)} %bitcast.193, bf16[2048,1024]{1,0:T(8,128)(2,1)} %bitcast.206), kind=kOutput, calls=%fused_computation.191 | convolution fusion | flops 8589934592 | bytes 20971520 | tf_op jit(solution)/shard_map/dot_general | solution.py:635
  454.6 10.4 multiply_convert_fusion.2
  464.9 12.3 %copy.279 = bf16[2048,2048]{1,0:T(8,128)(2,1)} copy(bf16[2048,2048]{0,1:T(8,128)(2,1)} %bitcast.194) | data formatting | bytes 16777216 | tf_op jit(solution)/shard_map/dot_general | solution.py:643
  477.2 13.9 %fusion.4 = bf16[2,1024,1024]{2,1,0:T(8,128)(2,1)} fusion(bf16[2,1024,2048]{2,1,0:T(8,128)(2,1)} %bitcast.219, bf16[2048,512]{0,1:T(8,128)(2,1)} %get-tuple-element.90, bf16[2048,512]{0,1:T(8,128)(2,1)} %get-tuple-element.89), kind=kOutput, calls=%fused_computation.32 | convolution fusion | flops 8600420352 | bytes 16777216 | tf_op jit(solution)/shard_map/dot_general | solution.py:643
  491.1 12.7 %copy.281 = bf16[2048,2048]{1,0:T(8,128)(2,1)} copy(bf16[2048,2048]{0,1:T(8,128)(2,1)} %bitcast.195) | data formatting | bytes 16777216 | tf_op jit(solution)/shard_map/dot_general | solution.py:643
  503.8 8.7 fusion.16
  515.8 69.8 %shard_map.167 = bf16[16,64,1536]{2,1,0:T(8,128)(2,1)} custom-call(bf16[2,1024,1536]{2,1,0:T(8,128)(2,1)} %pad_maximum_fusion.g), custom_call_target="tpu_custom_call" | custom-call | tf_op jit(solution)/shard_map/pallas_call | solution.py:496
  595.7 11.4 convolution_convert_fusion.1
  607.1 7.0 convolution_convert_fusion.2
  614.2 169.1 %shard_map.164 = (f32[128,2048]{1,0:T(8,128)}, f32[128,2048]{1,0:T(8,128)}) custom-call(bf16[16,128,2048]{2,1,0:T(8,128)(2,1)} %bitcast.218, bf16[16,128,2048]{2,1,0:T(8,128)(2,1)} %bitcast.216), custom_call_target="tpu_custom_call" | custom-call | tf_op jit(solution)/shard_map/pallas_call | solution.py:515
  788.4 20.9 %convolution_bitcast_fusion.3 = f32[4,1]{1,0:T(4,128)S(1)} fusion(f32[128,4,2048]{0,1,2:T(4,128)} %get-tuple-element.86, f32[128,2048,1]{0,2,1:T(1,128)} %copy.297), kind=kOutput, calls=%fused_computation.81 | convolution fusion | flops 12582912 | bytes 5242896 | tf_op jit(solution)/shard_map/tjd,td->j/dot_general | solution.py:596
  809.3 9.0 convolution_bitcast_fusion.2
  822.2 11.8 convolution_bitcast_fusion
  846.3 16.0 %multiply_reduce_fusion.1 = (bf16[128,2048]{0,1:T(8,128)(2,1)S(1)}, f32[128,4,2048]{0,1,2:T(4,128)}) fusion(f32[4]{0:T(128)S(1)} %get-tuple-element.72, f32[4]{0:T(128)S(1)} %copy-done.49, f32[128,2048]{0,1:T(8,128)S(1)} %copy-done.24, f32[4]{0:T(128)S(1)} %copy-done.59, f32[128,2048]{0,1:T(8,128)} %copy.251, f32[4]{0:T(128)S(1)} %copy-done.58, ...), kind=kLoop, calls=%fused_computation.14 | loop fusion | flops 11272192 | bytes 9961568 | tf_op jit(solution)/shard_map/reduce_sum | solution.py:773
  863.1 20.0 %convolution_bitcast_fusion.4 = f32[4,1]{1,0:T(4,128)S(1)} fusion(f32[128,2048,1]{0,2,1:T(1,128)S(1)} %copy.296, f32[128,4,2048]{0,1,2:T(4,128)} %get-tuple-element.85), kind=kOutput, calls=%fused_computation.82 | convolution fusion | flops 12582912 | bytes 5242896 | tf_op jit(solution)/shard_map/td,tid->i/dot_general | solution.py:598
  883.1 6.5 convolution_convert_fusion.8
  890.2 13.4 %shard_map.165 = bf16[16,128,128]{2,1,0:T(8,128)(2,1)S(1)} custom-call(bf16[16,128,128]{2,1,0:T(8,128)(2,1)S(1)} %bitcast.202), custom_call_target="tpu_custom_call" | custom-call | tf_op jit(solution)/shard_map/pallas_call | solution.py:427
  915.0 5.8 fusion.43
  924.2 9.2 convolution_convert_fusion.4
  939.0 6.8 convolution_convert_fusion
  945.8 138.9 %shard_map.166 = (f32[128,2048]{1,0:T(8,128)}, f32[64,2048]{1,0:T(8,128)}, bf16[16,64,384]{2,1,0:T(8,128)(2,1)}) custom-call(bf16[16,128,2048]{2,1,0:T(8,128)(2,1)} %bitcast.217, bf16[2,1024,2048]{2,1,0:T(8,128)(2,1)} %bitcast.212, bf16[2,1024,384]{2,1,0:T(8,128)(2,1)} %bitcast.243), custom_call_target="tpu_custom_call" | custom-call | tf_op jit(solution)/shard_map/pallas_call | solution.py:544
  1088.5 9.0 convolution_bitcast_fusion.5
  1101.0 11.9 convolution_bitcast_fusion.1
  1113.0 38.4 %all-reduce = (f32[4,6]{1,0:T(4,128)}, f32[4,6]{1,0:T(4,128)}) all-reduce(f32[4,6]{1,0:T(4,128)S(1)} %pad_maximum_fusion.7, f32[4,6]{1,0:T(4,128)S(1)} %pad_maximum_fusion.8), channel_id=1, replica_groups=mesh['rep'=2,'shard'=16] {'rep','shard'}, use_global_device_ids=true, to_apply=%region_18.19 | all-reduce | flops 48 | bytes 384 | tf_op jit(solution)/shard_map/psum | solution.py:803
  1151.4 11.8 fusion.83
  (239 shorter events, 146.1 us)
Async XLA Ops:
  0.6 8.3 copy-start.14
  2.8 272.1 %copy-start.37 = (f32[4,512]{1,0:T(4,128)}, f32[4,512]{1,0:T(4,128)S(1)}, u32[]{:S(2)}) copy-start(f32[4,512]{1,0:T(4,128)S(1)} %get-tuple-element.87) | copy-start | bytes 24580
  2.8 282.9 %copy-start.45 = (s32[4,512]{1,0:T(4,128)}, s32[4,512]{1,0:T(4,128)S(1)}, u32[]{:S(2)}) copy-start(s32[4,512]{1,0:T(4,128)S(1)} %get-tuple-element.88) | copy-start | bytes 24580
  2.8 282.9 %copy-start.47 = (s32[4,512]{1,0:T(4,128)}, s32[4,512]{1,0:T(4,128)S(1)}, u32[]{:S(2)}) copy-start(s32[4,512]{1,0:T(4,128)S(1)} %get-tuple-element.125) | copy-start | bytes 24580
  8.2 252.5 %copy-start.43 = (f32[128]{0:T(128)}, f32[128]{0:T(128)S(1)}, u32[]{:S(2)}) copy-start(f32[128]{0:T(128)S(1)} %broadcast_multiply_fusion.5) | copy-start | bytes 1540
  8.5 252.2 %copy-start.50 = (f32[128]{0:T(128)}, f32[128]{0:T(128)S(1)}, u32[]{:S(2)}) copy-start(f32[128]{0:T(128)S(1)} %add_rsqrt_fusion.1) | copy-start | bytes 1540
  260.8 13.7 %copy-start = (bf16[2,16,64,2048]{3,2,1,0:T(8,128)(2,1)}, bf16[2,16,64,2048]{3,2,1,0:T(8,128)(2,1)S(1)}, u32[]{:S(2)}) copy-start(bf16[2,16,64,2048]{3,2,1,0:T(8,128)(2,1)S(1)} %get-tuple-element.21) | copy-start | bytes 25165828
  260.8 13.7 %copy-start.2 = (bf16[16,128,2048]{2,1,0:T(8,128)(2,1)}, bf16[16,128,2048]{2,1,0:T(8,128)(2,1)S(1)}, u32[]{:S(2)}) copy-start(bf16[16,128,2048]{2,1,0:T(8,128)(2,1)S(1)} %get-tuple-element.24) | copy-start | bytes 25165828
  260.8 13.7 %copy-start.7 = (bf16[2,1,16,64,1024]{4,3,2,1,0:T(8,128)(2,1)}, bf16[2,1,16,64,1024]{4,3,2,1,0:T(8,128)(2,1)S(1)}, u32[]{:S(2)}) copy-start(bf16[2,1,16,64,1024]{4,3,2,1,0:T(8,128)(2,1)S(1)} %get-tuple-element.22) | copy-start | bytes 12582916
  260.8 13.7 %copy-start.9 = (bf16[2,1,16,64,384]{4,3,2,1,0:T(8,128)(2,1)}, bf16[2,1,16,64,384]{4,3,2,1,0:T(8,128)(2,1)S(1)}, u32[]{:S(2)}) copy-start(bf16[2,1,16,64,384]{4,3,2,1,0:T(8,128)(2,1)S(1)} %get-tuple-element.20) | copy-start | bytes 4718596
  326.7 10.2 copy-start.35
  326.7 10.3 copy-start.49
  362.5 92.0 %slice-start = ((s8[8388608]{0:T(1024)(128)(4,1)}), s8[4194304]{0:T(1024)(128)(4,1)S(1)}, s32[]{:S(2)}) async-start(s8[8388608]{0:T(1024)(128)(4,1)} %bitcast.196), calls=%async_computation | async-start | bytes 8388608
  438.8 15.8 %copy-start.1 = (bf16[16,128,2048]{2,1,0:T(8,128)(2,1)}, bf16[16,128,2048]{2,1,0:T(8,128)(2,1)S(1)}, u32[]{:S(2)}) copy-start(bf16[16,128,2048]{2,1,0:T(8,128)(2,1)S(1)} %shard_map.163) | copy-start | bytes 25165828
  438.8 15.8 %slice-start.1 = ((s8[8388608]{0:T(1024)(128)(4,1)}), s8[4194304]{0:T(1024)(128)(4,1)S(1)}, s32[]{:S(2)}) async-start(s8[8388608]{0:T(1024)(128)(4,1)} %bitcast.196), calls=%async_computation.1 | async-start | bytes 8388608
  503.8 8.7 copy-start.23
  595.7 11.4 copy-start.66
  614.2 169.1 %copy-start.13 = (f32[128,2048]{1,0:T(8,128)S(1)}, f32[128,2048]{1,0:T(8,128)}, u32[]{:S(2)}) copy-start(f32[128,2048]{1,0:T(8,128)} %copy.243) | copy-start | bytes 3145732
  788.4 20.9 %copy-start.15 = (bf16[128,4,2048]{2,1,0:T(4,128)(2,1)S(1)}, bf16[128,4,2048]{2,1,0:T(4,128)(2,1)}, u32[]{:S(2)}) copy-start(bf16[128,4,2048]{2,1,0:T(4,128)(2,1)} %param.11) | copy-start | bytes 6291460
  788.4 20.9 %copy-start.32 = (f32[128,2048]{1,0:T(8,128)S(1)}, f32[128,2048]{1,0:T(8,128)}, u32[]{:S(2)}) copy-start(f32[128,2048]{1,0:T(8,128)} %get-tuple-element.25) | copy-start | bytes 3145732
  846.3 16.1 %copy-start.18 = (f32[128,2048]{1,0:T(8,128)S(1)}, f32[128,2048]{1,0:T(8,128)}, u32[]{:S(2)}) copy-start(f32[128,2048]{1,0:T(8,128)} %fusion.86) | copy-start | bytes 3145732
  863.0 20.1 %copy-start.40 = (s32[128]{0:T(128)S(1)}, s32[128]{0:T(128)}, u32[]{:S(2)}) copy-start(s32[128]{0:T(128)} %param.12) | copy-start | bytes 1540
  889.6 14.1 %copy-start.27 = (bf16[4,512,64]{2,1,0:T(8,128)(2,1)S(1)}, bf16[4,512,64]{2,1,0:T(8,128)(2,1)}, u32[]{:S(2)}) copy-start(bf16[4,512,64]{2,1,0:T(8,128)(2,1)} %copy-done.26) | copy-start | bytes 786436
  889.6 14.1 %copy-start.29 = (bf16[4,512,64]{2,1,0:T(8,128)(2,1)S(1)}, bf16[4,512,64]{2,1,0:T(8,128)(2,1)}, u32[]{:S(2)}) copy-start(bf16[4,512,64]{2,1,0:T(8,128)(2,1)} %copy-done.28) | copy-start | bytes 786436
  889.6 14.1 %copy-start.30 = (bf16[4,512,64]{2,1,0:T(8,128)(2,1)S(1)}, bf16[4,512,64]{2,1,0:T(8,128)(2,1)}, u32[]{:S(2)}) copy-start(bf16[4,512,64]{2,1,0:T(8,128)(2,1)} %get-tuple-element.123) | copy-start | bytes 786436
  889.6 14.1 %copy-start.42 = (f32[4,512]{1,0:T(4,128)S(1)}, f32[4,512]{1,0:T(4,128)}, u32[]{:S(2)}) copy-start(f32[4,512]{1,0:T(4,128)} %copy-done.41) | copy-start | bytes 24580
  889.6 14.1 %copy-start.46 = (s32[4,512]{1,0:T(4,128)S(1)}, s32[4,512]{1,0:T(4,128)}, u32[]{:S(2)}) copy-start(s32[4,512]{1,0:T(4,128)} %copy-done.45) | copy-start | bytes 24580
  889.6 14.1 %copy-start.48 = (s32[4,512]{1,0:T(4,128)S(1)}, s32[4,512]{1,0:T(4,128)}, u32[]{:S(2)}) copy-start(s32[4,512]{1,0:T(4,128)} %copy-done.47) | copy-start | bytes 24580
  924.2 9.2 copy-start.20
  945.8 138.9 %copy-start.12 = (f32[128,2048]{1,0:T(8,128)S(1)}, f32[128,2048]{1,0:T(8,128)}, u32[]{:S(2)}) copy-start(f32[128,2048]{1,0:T(8,128)} %copy-done.11) | copy-start | bytes 3145732
  945.8 138.9 %copy-start.44 = (f32[128]{0:T(128)S(1)}, f32[128]{0:T(128)}, u32[]{:S(2)}) copy-start(f32[128]{0:T(128)} %copy-done.43) | copy-start | bytes 1540
  945.8 138.9 %copy-start.51 = (f32[128]{0:T(128)S(1)}, f32[128]{0:T(128)}, u32[]{:S(2)}) copy-start(f32[128]{0:T(128)} %copy-done.50) | copy-start | bytes 1540
  (39 other events, 183.8 us)

commit v2 on v1

--- a/solution.py
+++ b/solution.py
@@ -121,25 +121,6 @@
     ORDER = (0, 1, 3, 2)
 
 
-def run_gathers(gathers, own_sems):
-    for i, g in enumerate(gathers):
-        if i == 0:
-            g.begin(own_sems.at[0])
-        order = g.ORDER
-        g.spread(order[1])
-        g.forward(order[0])
-        g.spread(order[2])
-        g.forward(order[1])
-        g.spread(order[3])
-        g.forward(order[2])
-        if i + 1 < len(gathers):
-            gathers[i + 1].begin(own_sems.at[i + 1])
-        g.forward(order[3])
-    for g in gathers:
-        for j in range(4):
-            g.settle(j)
-
-
 def rowwise(n, step, body):
     def at(i, carry):
         body(pl.ds(pl.multiple_of(i * step, step), step))
@@ -157,16 +138,14 @@
         return [
             pltpu.VMEM((4, 4, h, d), BF),
             pltpu.VMEM((4, 2, h, d), BF),
-            pltpu.VMEM((4, 2, h, d), BF),
-            pltpu.VMEM((4, rows, d), BF),
-            pltpu.VMEM((4, rows, d), BF),
+            pltpu.VMEM((3, rows, d), BF),
             pltpu.SemaphoreType.DMA(Scatter.sems),
             pltpu.SemaphoreType.DMA(Scatter.sems),
         ]
 
     def __init__(self, here, part, scratch):
         self.here, self.part = here, part
-        self.first, self.second, self.mid, self.zin, self.zout, self.send, self.recv = scratch
+        self.first, self.second, self.zin, self.send, self.recv = scratch
         self.rows = part.shape[1]
         self.half = self.rows // 2
         self.sent = []
@@ -196,11 +175,11 @@
             self._copy(j, slot, self.first.at[j, slot], self.first.at[j, slot], 1).wait_recv()
             own = self._piece(m ^ mask, part)
 
-            def body(r, own=own, slot=slot, part=part):
-                self.mid[j, part, r] = (own[r].astype(F32) + self.first[j, slot, r].astype(F32)).astype(BF)
+            def body(r, own=own, slot=slot):
+                own[r] = (own[r].astype(F32) + self.first[j, slot, r].astype(F32)).astype(BF)
 
             rowwise(h, 16, body)
-            self._go(j, 4 + part, self.mid.at[j, part], self.second.at[j, part], to)
+            self._go(j, 4 + part, own, self.second.at[j, part], to)
 
     def finish(self, j, out=None):
         m = 4 * j
@@ -210,7 +189,7 @@
             self._copy(j, 4 + part, self.second.at[j, part], self.second.at[j, part], 1).wait_recv()
         if out is not None:
             for k in (1, 2, 3):
-                self._copy(k, 6, self.zin.at[k], self.zin.at[k], 4).wait_recv()
+                self._copy(k, 6, self.zin.at[k - 1], self.zin.at[k - 1], 4).wait_recv()
         for part, slot in ((0, 0), (1, 2)):
             own = self._piece(m, part)
 
@@ -218,15 +197,15 @@
                 total = own[r].astype(F32) + self.first[j, slot, r].astype(F32) + self.second[j, part, r].astype(F32)
                 at = pl.ds(part * h + r.start, r.size)
                 if out is None:
-                    self.zout[j, at] = total.astype(BF)
+                    own[r] = total.astype(BF)
                 else:
                     for k in (1, 2, 3):
-                        total = total + self.zin[k, at].astype(F32)
+                        total = total + self.zin[k - 1, at].astype(F32)
                     out[at] = total.astype(out.dtype)
 
             rowwise(h, 16, body)
         if out is None:
-            self._go(j, 6, self.zout.at[j], self.zin.at[j], m)
+            self._go(j, 6, self.part.at[self.here.flip(m)], self.zin.at[j - 1], m)
 
     def end(self):
         for c in self.sent:
@@ -382,51 +361,38 @@
     )(n1, dy2, wqkv, wout, wgu, wdn)
 
 
-def gather_kernel(x, out, send, recv, own):
-    here = Here()
-    barrier(here, TREE, False)
-    g = Gather(here, x, out, send, recv)
-    run_gathers([g], own)
-    g.end()
-
-
-def gather(x, cid):
-    return pl.pallas_call(
-        gather_kernel,
-        out_shape=jax.ShapeDtypeStruct((GROUP,) + x.shape, x.dtype),
-        in_specs=any_spec(1),
-        out_specs=pl.BlockSpec(memory_space=pl.ANY),
-        scratch_shapes=[
-            pltpu.SemaphoreType.DMA(Gather.sems),
-            pltpu.SemaphoreType.DMA(Gather.sems),
-            pltpu.SemaphoreType.DMA((1,)),
-        ],
-        compiler_params=params(cid, 16),
-    )(x)
-
-
 def swap_kernel(x, out, send, recv, own):
     here = Here()
     barrier(here, ALL, False)
+
+    def block(ref, l):
+        if len(ref.shape) == 3:
+            return ref.at[l]
+        return ref.at[:, pl.ds(pl.multiple_of(l * HEAD_DIM, HEAD_DIM), HEAD_DIM)]
+
     cps = []
     for m in ALL:
-        c = rcopy(x.at[here.flip(m)], out.at[here.lo], send.at[m], recv.at[m], here.dev(m))
+        c = rcopy(block(x, here.flip(m)), block(out, here.lo), send.at[m], recv.at[m], here.dev(m))
         c.start()
         cps.append(c)
-    c = pltpu.make_async_copy(x.at[here.lo], out.at[here.lo], own)
+    c = pltpu.make_async_copy(block(x, here.lo), block(out, here.lo), own)
     c.start()
     c.wait()
     for m in ALL:
-        ref = out.at[here.flip(m)]
+        ref = block(out, here.flip(m))
         rcopy(ref, ref, send.at[m], recv.at[m], here.dev(m)).wait_recv()
     for c in cps:
         c.wait_send()
 
 
 def swap(x, cid):
+    if x.ndim == 3:
+        shape = (x.shape[1], GROUP * HEAD_DIM)
+    else:
+        shape = (GROUP, x.shape[0], HEAD_DIM)
     return pl.pallas_call(
         swap_kernel,
-        out_shape=jax.ShapeDtypeStruct(x.shape, x.dtype),
+        out_shape=jax.ShapeDtypeStruct(shape, x.dtype),
         in_specs=any_spec(1),
         out_specs=pl.BlockSpec(memory_space=pl.ANY),
         scratch_shapes=[
@@ -438,106 +404,260 @@
     )(x)
 
 
-def pair_add(here, g, inbox, total, send, recv):
+def pair_add(here, g, inbox, send, recv):
     cp = rcopy(g.at[1 - here.rep], inbox, send, recv, here.partner())
     cp.start()
     cp.wait()
 
     def body(r):
-        total[r] = (g[here.rep, r].astype(F32) + inbox[r].astype(F32)).astype(BF)
+        g[here.rep, r] = (g[here.rep, r].astype(F32) + inbox[r].astype(F32)).astype(BF)
 
     rowwise(inbox.shape[0], 16, body)
 
 
 def send_home(here, total, out, send, recv, own):
-    rows = out.shape[1]
+    _, hi, rows, _ = out.shape
+
+    def block(h, m):
+        at = (h * GROUP + here.flip(m)) * rows
+        return total.at[pl.ds(pl.multiple_of(at, rows), rows)]
+
     cps = []
-    for m in ALL:
-        at = total.at[pl.ds(pl.multiple_of(here.flip(m) * rows, rows), rows)]
-        c = rcopy(at, out.at[here.lo], send.at[m], recv.at[m], here.dev(m))
+    owns = []
+    for h in range(hi):
+        for m in ALL:
+            c = rcopy(block(h, m), out.at[here.lo, h], send.at[h, m], recv.at[h, m], here.dev(m))
+            c.start()
+            cps.append(c)
+        c = pltpu.make_async_copy(block(h, 0), out.at[here.lo, h], own.at[h])
         c.start()
-        cps.append(c)
-    at = total.at[pl.ds(pl.multiple_of(here.lo * rows, rows), rows)]
-    c = pltpu.make_async_copy(at, out.at[here.lo], own)
-    c.start()
-    c.wait()
+        owns.append(c)
 
     def end():
-        for m in ALL:
-            ref = out.at[here.flip(m)]
-            rcopy(ref, ref, send.at[m], recv.at[m], here.dev(m)).wait_recv()
+        for c in owns:
+            c.wait()
+        for h in range(hi):
+            for m in ALL:
+                ref = out.at[here.flip(m), h]
+                rcopy(ref, ref, send.at[h, m], recv.at[h, m], here.dev(m)).wait_recv()
         for c in cps:
             c.wait_send()
 
     return end
 
 
-def mlp_home_kernel(g, out, inbox, total, psend, precv, send, recv, own):
+def home_sems(hi):
+    return [
+        pltpu.SemaphoreType.DMA((hi, GROUP)),
+        pltpu.SemaphoreType.DMA((hi, GROUP)),
+        pltpu.SemaphoreType.DMA((hi,)),
+    ]
+
+
+def mlp_kernel(
+    n2, dy2g_in, wgu_in, wdn_in, dn2, y2p, home,
+    n2g, dy2g, wgu, wdn, part, hidden, dgu, y2s, grads, inbox,
+    gsend, grecv, own, load, y2sem, psend, precv, hsend, hrecv, hown, *scratch,
+):
     here = Here()
     barrier(here, ALL, True)
-    pair_add(here, g, inbox, total, psend, precv)
-    send_home(here, total, out, send, recv, own)()
-
-
-def home_scratch(n, w):
-    return [
-        pltpu.VMEM((n, w), BF),
-        pltpu.VMEM((n, w), BF),
-        pltpu.SemaphoreType.DMA,
-        pltpu.SemaphoreType.DMA,
-        pltpu.SemaphoreType.DMA((GROUP,)),
-        pltpu.SemaphoreType.DMA((GROUP,)),
-        pltpu.SemaphoreType.DMA,
-    ]
-
-
-def mlp_home(g, cid):
-    _, n, w = g.shape
+    g = Gather(here, n2, n2g, gsend, grecv)
+    rs = Scatter(here, part, scratch)
+    g.begin(own)
+    loads = []
+    for i, (src, dst) in enumerate(((wgu_in, wgu), (wdn_in, wdn), (dy2g_in, dy2g))):
+        c = pltpu.make_async_copy(src, dst, load.at[i])
+        c.start()
+        loads.append(c)
+    width, ff = wdn.shape
+    tokens = n2.shape[0]
+    group_rows = 4 * tokens
+    step = 256
+    y2copies = []
+
+    def compute(j):
+        first = here.flip(4 * j) - here.lo % 4
+        blocks = pl.ds(first, 4)
+        if not y2copies:
+            for c in loads:
+                c.wait()
+
+        def gates(k, carry):
+            up_at = pl.ds(pl.multiple_of(k * step, step), step)
+            gate_at = pl.ds(pl.multiple_of(ff + k * step, step), step)
+            x = n2g[blocks].reshape(group_rows, width)
+            up = dot(x, wgu[:, up_at])
+            gate = dot(x, wgu[:, gate_at])
+            dh = dot(dy2g[blocks].reshape(group_rows, width), wdn[:, up_at])
+            sigmoid = 1.0 / (1.0 + jnp.exp(-gate))
+            silu = gate * sigmoid
+            hidden[blocks, :, up_at] = (silu * up).astype(BF).reshape(4, tokens, step)
+            dgu[blocks, :, up_at] = (dh * silu).astype(BF).reshape(4, tokens, step)
+            dgu[blocks, :, gate_at] = (
+                (dh * up * sigmoid * (1.0 + gate * (1.0 - sigmoid))).astype(BF).reshape(4, tokens, step)
+            )
+            return carry
+
+        lax.fori_loop(0, ff // step, gates, 0)
+        if y2copies:
+            y2copies[-1].wait()
+
+        def outputs(k, carry):
+            at = pl.ds(pl.multiple_of(k * step, step), step)
+            h = hidden[blocks].reshape(group_rows, ff)
+            y2s[:, :, at] = dot_t(h, wdn[at, :]).astype(BF).reshape(4, tokens, step)
+            d = dgu[blocks].reshape(group_rows, 2 * ff)
+            part[blocks, :, at] = dot_t(d, wgu[at, :]).astype(BF).reshape(4, tokens, step)
+            return carry
+
+        lax.fori_loop(0, width // step, outputs, 0)
+        c = pltpu.make_async_copy(y2s, y2p.at[blocks], y2sem.at[len(y2copies)])
+        c.start()
+        y2copies.append(c)
+
+    half = width // 2
+    chunks = half // step
+
+    def weight_grads(which, k):
+        cols = pl.ds(pl.multiple_of(which * half + k * step, step), step)
+        rows = pl.ds(pl.multiple_of(k * step, step), step)
+        x = n2g[:, :, cols].reshape(GROUP * tokens, step)
+        grads[which, rows, : 2 * ff] = t_dot(x, dgu[...].reshape(GROUP * tokens, 2 * ff)).astype(BF)
+        x = dy2g[:, :, cols].reshape(GROUP * tokens, step)
+        grads[which, rows, 2 * ff :] = t_dot(x, hidden[...].reshape(GROUP * tokens, ff)).astype(BF)
+
+    def pass_chunk(k):
+        rows = pl.ds(pl.multiple_of(k * step, step), step)
+        return rcopy(grads.at[1 - here.rep, rows], inbox.at[rows], psend.at[k], precv.at[k], here.partner())
+
+    o = g.ORDER
+    g.spread(o[1])
+    g.forward(o[0])
+    g.settle(o[0])
+    compute(o[0])
+    rs.start(o[0])
+    g.spread(o[2])
+    g.forward(o[1])
+    g.settle(o[1])
+    compute(o[1])
+    rs.start(o[1])
+    g.spread(o[3])
+    g.forward(o[2])
+    rs.cross(o[0])
+    g.settle(o[2])
+    compute(o[2])
+    rs.start(o[2])
+    g.forward(o[3])
+    rs.cross(o[1])
+    g.settle(o[3])
+    rs.finish(o[1])
+    compute(o[3])
+    rs.start(o[3])
+    rs.cross(o[2])
+    rs.finish(o[2])
+
+    def other_half(k, carry):
+        weight_grads(1 - here.rep, k)
+        pass_chunk(k).start()
+        return carry
+
+    lax.fori_loop(0, chunks, other_half, 0)
+    rs.cross(o[3])
+    rs.finish(o[3])
+
+    def own_half(k, carry):
+        weight_grads(here.rep, k)
+        return carry
+
+    lax.fori_loop(0, chunks, own_half, 0)
+
+    def add(k, carry):
+        pass_chunk(k).wait()
+
+        def rows_add(i, carry):
+            r = pl.ds(pl.multiple_of(k * step + i * 16, 16), 16)
+            grads[here.rep, r] = (grads[here.rep, r].astype(F32) + inbox[r].astype(F32)).astype(BF)
+            return carry
+
+        return lax.fori_loop(0, step // 16, rows_add, carry)
+
+    lax.fori_loop(0, chunks, add, 0)
+    finish = send_home(here, grads.at[here.rep], home, hsend, hrecv, hown)
+    rs.finish(0, dn2)
+    y2copies[-1].wait()
+    finish()
+    g.end()
+    rs.end()
+
+
+def mlp(n2, dy2g, wgu, wdn, hi, cid):
+    tokens, width = n2.shape
+    ff = wdn.shape[1]
+    half = width // 2
+    blocks = (GROUP, tokens)
     return pl.pallas_call(
-        mlp_home_kernel,
-        out_shape=jax.ShapeDtypeStruct((GROUP, n // GROUP, w), BF),
-        in_specs=vmem_spec(1),
-        out_specs=pl.BlockSpec(memory_space=pl.ANY),
-        scratch_shapes=home_scratch(n, w),
-        compiler_params=params(cid),
-    )(g)
-
-
-def scatter_kernel(a, b, aout, bout, *scratch):
-    here = Here()
-    barrier(here, TREE, False)
-    n = len(scratch) // 2
-    run_scatters([Scatter(here, a, scratch[:n]), Scatter(here, b, scratch[n:])], [aout, bout])
-
-
-def scatter_two(a, b, cid):
-    _, rows, d = a.shape
-    return pl.pallas_call(
-        scatter_kernel,
-        out_shape=(jax.ShapeDtypeStruct((rows, d), F32),) * 2,
-        in_specs=vmem_spec(2),
-        out_specs=tuple(vmem_spec(2)),
-        scratch_shapes=Scatter.scratch(rows, d) * 2,
-        compiler_params=params(cid),
-    )(a, b)
-
-
-def back_kernel(dn, gout, gqkv, dn_out, gout_out, gqkv_out, *scratch):
+        mlp_kernel,
+        out_shape=(
+            jax.ShapeDtypeStruct((tokens, width), F32),
+            jax.ShapeDtypeStruct((*blocks, width), BF),
+            jax.ShapeDtypeStruct((GROUP, hi, half // (hi * GROUP), 3 * ff), BF),
+        ),
+        in_specs=[*vmem_spec(1), *any_spec(3)],
+        out_specs=(*vmem_spec(1), *any_spec(2)),
+        scratch_shapes=[
+            pltpu.VMEM((*blocks, width), BF),
+            pltpu.VMEM((*blocks, width), BF),
+            pltpu.VMEM(wgu.shape, BF),
+            pltpu.VMEM(wdn.shape, BF),
+            pltpu.VMEM((*blocks, width), BF),
+            pltpu.VMEM((*blocks, ff), BF),
+            pltpu.VMEM((*blocks, 2 * ff), BF),
+            pltpu.VMEM((4, tokens, width), BF),
+            pltpu.VMEM((2, half, 3 * ff), BF),
+            pltpu.VMEM((half, 3 * ff), BF),
+            pltpu.SemaphoreType.DMA(Gather.sems),
+            pltpu.SemaphoreType.DMA(Gather.sems),
+            pltpu.SemaphoreType.DMA,
+            pltpu.SemaphoreType.DMA((3,)),
+            pltpu.SemaphoreType.DMA((4,)),
+            pltpu.SemaphoreType.DMA((half // 256,)),
+            pltpu.SemaphoreType.DMA((half // 256,)),
+            *home_sems(hi),
+            *Scatter.scratch(tokens, width),
+        ],
+        compiler_params=params(cid, 63),
+        cost_estimate=pl.CostEstimate(
+            flops=2 * GROUP * tokens * width * ff * 9, bytes_accessed=60 * MIB, transcendentals=0
+        ),
+    )(n2, dy2g, wgu, wdn)
+
+
+def back_kernel(dn_in, y2_in, gout_in, gqkv, dn_out, y2_out, gout_out, gqkv_out, dn, y2, gout, load, *scratch):
     here = Here()
     barrier(here, ALL, True)
+    loads = []
+    for i, (src, dst) in enumerate(((gout_in, gout), (dn_in, dn), (y2_in, y2))):
+        c = pltpu.make_async_copy(src, dst, load.at[i])
+        c.start()
+        loads.append(c)
     n = len(Scatter.scratch(16, 128))
     s1, scratch = scratch[:n], scratch[n:]
     s2, scratch = scratch[:n], scratch[n:]
-    (obox, osum, osend, orecv), scratch = scratch[:4], scratch[4:]
-    pair_add(here, gqkv, *scratch[:4])
-    end = send_home(here, scratch[1], gqkv_out, *scratch[4:])
-    pair_add(here, gout, obox, osum, osend, orecv)
-    sums = osum.reshape(GROUP, gout.shape[1] // GROUP, gout.shape[2])
-    run_scatters([Scatter(here, dn, s1), Scatter(here, sums, s2)], [dn_out, gout_out])
+    s3, scratch = scratch[:n], scratch[n:]
+    (obox, osend, orecv), scratch = scratch[:3], scratch[3:]
+    pair_add(here, gqkv, *scratch[:3])
+    end = send_home(here, gqkv.at[here.rep], gqkv_out, *scratch[3:])
+    for c in loads:
+        c.wait()
+    pair_add(here, gout, obox, osend, orecv)
+    sums = gout.reshape(2, GROUP, gout.shape[1] // GROUP, gout.shape[2]).at[here.rep]
+    run_scatters(
+        [Scatter(here, dn, s1), Scatter(here, y2, s2), Scatter(here, sums, s3)], [dn_out, y2_out, gout_out]
+    )
     end()
 
 
-def back(dn, gout, gqkv, cid):
+def back(dn, y2, gout, gqkv, hi, cid):
     _, rows, d = dn.shape
     n, w = gqkv.shape[1:]
     on, od = gout.shape[1:]
@@ -545,28 +665,47 @@
         back_kernel,
         out_shape=(
             jax.ShapeDtypeStruct((rows, d), F32),
+            jax.ShapeDtypeStruct((rows, d), F32),
             jax.ShapeDtypeStruct((on // GROUP, od), F32),
-            jax.ShapeDtypeStruct((GROUP, n // GROUP, w), BF),
+            jax.ShapeDtypeStruct((GROUP, hi, n // (hi * GROUP), w), BF),
         ),
-        in_specs=vmem_spec(3),
-        out_specs=(*vmem_spec(2), *any_spec(1)),
+        in_specs=[*any_spec(3), *vmem_spec(1)],
+        out_specs=(*vmem_spec(3), *any_spec(1)),
         scratch_shapes=[
+            pltpu.VMEM(dn.shape, BF),
+            pltpu.VMEM(y2.shape, BF),
+            pltpu.VMEM(gout.shape, BF),
+            pltpu.SemaphoreType.DMA((3,)),
+            *Scatter.scratch(rows, d),
             *Scatter.scratch(rows, d),
             *Scatter.scratch(on // GROUP, od),
             pltpu.VMEM((on, od), BF),
-            pltpu.VMEM((on, od), BF),
             pltpu.SemaphoreType.DMA,
             pltpu.SemaphoreType.DMA,
-            *home_scratch(n, w),
+            pltpu.VMEM((n, w), BF),
+            pltpu.SemaphoreType.DMA,
+            pltpu.SemaphoreType.DMA,
+            *home_sems(hi),
         ],
-        compiler_params=params(cid),
-    )(dn, gout, gqkv)
-
-
-def normalize(inputs):
-    centred = inputs - jnp.mean(inputs, -1, keepdims=True)
+        compiler_params=params(cid, 63),
+    )(dn, y2, gout, gqkv)
+
+
+def read_mix(ref):
+    return [[ref[i, k] for k in range(6)] for i in range(4)]
+
+
+def mixed(weights, planes):
+    total = weights[0] * planes[0]
+    for w, p in zip(weights[1:], planes[1:]):
+        total = total + w * p
+    return total
+
+
+def moments(x):
+    centred = x - jnp.mean(x, -1, keepdims=True)
     inverse = lax.rsqrt(jnp.mean(centred * centred, -1, keepdims=True) + EPSILON)
-    return (centred * inverse, inverse)
+    return centred * inverse, inverse
 
 
 def normalize_back(grad_out, normed, inverse):
@@ -577,26 +716,244 @@
     )
 
 
-def write_streams(streams, mixing, branch, out_weights):
-    result = branch[:, None, :] * out_weights[None, :, None]
-    for source in range(streams.shape[1]):
-        result = result + streams[:, source, None, :] * mixing[source][None, :, None]
-    return result
-
-
-def write_back(grad_out, mixing):
-    result = jnp.zeros_like(grad_out)
-    for target in range(grad_out.shape[1]):
-        result = result + grad_out[:, target, None, :] * mixing[:, target][None, :, None]
-    return result
-
-
-def mixing_grad(streams, grad_out, branch, grad_read):
-    highest = lax.Precision.HIGHEST
-    first = jnp.einsum("tjd,td->j", streams, grad_read, precision=highest)
-    middle = jnp.einsum("tjd,tid->ji", streams, grad_out, precision=highest)
-    final_cols = jnp.einsum("td,tid->i", branch, grad_out, precision=highest)
-    return jnp.concatenate([first[:, None], middle, final_cols[:, None]], axis=1)
+def lane_sums(x):
+    total = x[:, :128]
+    for c in range(128, x.shape[1], 128):
+        total = total + x[:, c : c + 128]
+    return total
+
+
+def read_x2(m, p, h, y1):
+    fold = [sum(p[s][0] * m[j][1 + s] for s in range(4)) for j in range(4)]
+    return mixed(fold + [sum(p[s][0] * m[s][5] for s in range(4))], [*h, y1])
+
+
+TILE = 512
+
+
+def open_kernel(mixa, mixm, sorter, x, g, hs, gs, n1, dy2, plane):
+    m, p = read_mix(mixa), read_mix(mixm)
+    tokens, streams, width = x.shape
+    for src, dst in ((x, hs), (g, gs)):
+
+        def split(r, src=src):
+            v = src[r].astype(F32)
+            for i in range(streams):
+                plane[i, r] = v[:, i, :].astype(BF)
+
+        rowwise(tokens, 16, split)
+        for i in range(streams):
+            for c in range(0, width, TILE):
+                at = slice(c, c + TILE)
+                dst[i, :, at] = dot(sorter[...], plane[i, :, at]).astype(BF)
+
+    def norm(r):
+        x1 = mixed([m[j][0] for j in range(4)], [hs[j, r].astype(F32) for j in range(4)])
+        n1[r] = moments(x1)[0].astype(BF)
+        dy2[r] = mixed([p[j][5] for j in range(4)], [gs[j, r].astype(F32) for j in range(4)]).astype(BF)
+
+    rowwise(tokens, 16, norm)
+
+
+def smem_spec(n):
+    return [pl.BlockSpec(memory_space=pltpu.SMEM)] * n
+
+
+def local_params(mib=60):
+    return pltpu.CompilerParams(vmem_limit_bytes=mib * MIB)
+
+
+def open_streams(mixa, mixm, sorter, x, g):
+    tokens, streams, width = x.shape
+    return pl.pallas_call(
+        open_kernel,
+        out_shape=(
+            jax.ShapeDtypeStruct((streams, tokens, width), BF),
+            jax.ShapeDtypeStruct((streams, tokens, width), BF),
+            jax.ShapeDtypeStruct((tokens, width), BF),
+            jax.ShapeDtypeStruct((tokens, width), BF),
+        ),
+        in_specs=[*smem_spec(2), *vmem_spec(3)],
+        out_specs=tuple(vmem_spec(4)),
+        scratch_shapes=[pltpu.VMEM((streams, tokens, width), BF)],
+        compiler_params=local_params(),
+    )(mixa, mixm, sorter, x, g)
+
+
+def middle_kernel(mixa, mixm, hs, attn, wout, y1, n2):
+    m, p = read_mix(mixa), read_mix(mixm)
+    tokens, width = attn.shape
+
+    def tile(i, carry):
+        at = pl.ds(pl.multiple_of(i * TILE, TILE), TILE)
+        y1[:, at] = dot(attn[...], wout[:, at])
+        return carry
+
+    lax.fori_loop(0, width // TILE, tile, 0)
+
+    def norm(r):
+        x2 = read_x2(m, p, [hs[j, r].astype(F32) for j in range(4)], y1[r])
+        n2[r] = moments(x2)[0].astype(BF)
+
+    rowwise(tokens, 16, norm)
+
+
+def middle(mixa, mixm, hs, attn, wout):
+    tokens, width = attn.shape
+    return pl.pallas_call(
+        middle_kernel,
+        out_shape=(
+            jax.ShapeDtypeStruct((tokens, width), F32),
+            jax.ShapeDtypeStruct((tokens, width), BF),
+        ),
+        in_specs=[*smem_spec(2), *vmem_spec(3)],
+        out_specs=tuple(vmem_spec(2)),
+        compiler_params=local_params(),
+    )(mixa, mixm, hs, attn, wout)
+
+
+def unsort(sorter, planes, out):
+    streams, tokens, width = planes.shape
+    for i in range(streams):
+
+        def tile(k, carry, i=i):
+            at = pl.ds(pl.multiple_of(k * TILE, TILE), TILE)
+            v = planes[i, :, at]
+            high = v.astype(BF)
+            low = (v - high.astype(F32)).astype(BF)
+            out[:, i, at] = t_dot(sorter[...], high) + t_dot(sorter[...], low)
+            return carry
+
+        lax.fori_loop(0, width // TILE, tile, 0)
+
+
+def turn_kernel(mixa, mixm, hs, gs, y1, dn2, wout, dx2, dy1, d_out, sums):
+    m, p = read_mix(mixa), read_mix(mixm)
+    tokens, width = y1.shape
+    sums[...] = jnp.zeros_like(sums)
+
+    def body(r):
+        x2 = read_x2(m, p, [hs[j, r].astype(F32) for j in range(4)], y1[r])
+        normed, inverse = moments(x2)
+        dx2[r] = normalize_back(dn2[r], normed, inverse)
+        for c in range(0, width, TILE):
+            at = slice(c, c + TILE)
+            h = [hs[j, r, at].astype(F32) for j in range(4)]
+            y = y1[r, at]
+            h1 = [mixed([*(m[j][1 + i] for j in range(4)), m[i][5]], [*h, y]) for i in range(4)]
+            g = [gs[j, r, at].astype(F32) for j in range(4)]
+            dx = dx2[r, at]
+            g1 = [mixed([*(p[j][1 + i] for i in range(4)), p[j][0]], [*g, dx]) for j in range(4)]
+            dy1[r, at] = mixed([m[j][5] for j in range(4)], g1).astype(BF)
+            for j in range(4):
+                sums[j * 6] += lane_sums(h1[j] * dx)
+                for i in range(4):
+                    sums[j * 6 + 1 + i] += lane_sums(h1[j] * g[i])
+
+    rowwise(tokens, 16, body)
+
+    def tile(i, carry):
+        at = pl.ds(pl.multiple_of(i * TILE, TILE), TILE)
+        d_out[:, at] = dot_t(dy1[...], wout[at, :]).astype(BF)
+        return carry
+
+    lax.fori_loop(0, width // TILE, tile, 0)
+
+
+def turn(mixa, mixm, hs, gs, y1, dn2, wout):
+    streams, tokens, width = hs.shape
+    return pl.pallas_call(
+        turn_kernel,
+        out_shape=(
+            jax.ShapeDtypeStruct((tokens, width), F32),
+            jax.ShapeDtypeStruct((tokens, width), BF),
+            jax.ShapeDtypeStruct((tokens, width), BF),
+            jax.ShapeDtypeStruct((24, 16, 128), F32),
+        ),
+        in_specs=[*smem_spec(2), *vmem_spec(5)],
+        out_specs=tuple(vmem_spec(4)),
+        compiler_params=local_params(),
+    )(mixa, mixm, hs, gs, y1, dn2, wout)
+
+
+def close_kernel(
+    mixa, mixm, sorter, hs, gs, dx2, y1, y2, dn1, other, new, d_streams, total,
+    sums, planes, fresh, mine, inbox, send, recv,
+):
+    here = Here()
+    barrier(here, ALL, True)
+    m, p = read_mix(mixa), read_mix(mixm)
+    tokens, width = y1.shape
+    sums[:24] = jnp.zeros((24, *sums.shape[1:]), F32)
+    sums[24:] = other[...]
+
+    def body(r):
+        x1 = mixed([m[j][0] for j in range(4)], [hs[j, r].astype(F32) for j in range(4)])
+        normed, inverse = moments(x1)
+        planes[0, r] = normalize_back(dn1[r], normed, inverse)
+        for c in range(0, width, TILE):
+            at = slice(c, c + TILE)
+            h = [hs[j, r, at].astype(F32) for j in range(4)]
+            g = [gs[j, r, at].astype(F32) for j in range(4)]
+            y = y1[r, at]
+            dx = planes[0, r, at]
+            dm = dx2[r, at]
+            g1 = [mixed([*(p[j][1 + i] for i in range(4)), p[j][0]], [*g, dm]) for j in range(4)]
+            for j in range(4):
+                planes[j, r, at] = mixed([*(m[j][1 + i] for i in range(4)), m[j][0]], [*g1, dx])
+                sums[j * 6] += lane_sums(h[j] * dx)
+                for i in range(4):
+                    sums[j * 6 + 1 + i] += lane_sums(h[j] * g1[i])
+                sums[j * 6 + 5] += lane_sums(y * g1[j])
+            h1 = [mixed([*(m[j][1 + i] for j in range(4)), m[i][5]], [*h, y]) for i in range(4)]
+            y = y2[r, at]
+            for i in range(4):
+                fresh[i, r, at] = mixed([*(p[j][1 + i] for j in range(4)), p[i][5]], [*h1, y])
+                sums[24 + i * 6 + 5] += lane_sums(y * g[i])
+
+    rowwise(tokens, 16, body)
+    mine[0] = jnp.sum(sums[...], axis=1)
+    pair = rcopy(mine.at[0], inbox.at[0], send.at[0], recv.at[0], here.partner())
+    pair.start()
+    pair.wait()
+    mine[1] = mine[0] + inbox[0]
+    cps = []
+    for k in ALL:
+        c = rcopy(mine.at[1], inbox.at[k], send.at[k], recv.at[k], here.dev(k))
+        c.start()
+        cps.append(c)
+    unsort(sorter, fresh, new)
+    unsort(sorter, planes, d_streams)
+    everyone = mine[1]
+    for c in cps:
+        c.wait()
+    for k in ALL:
+        everyone = everyone + inbox[k]
+    total[...] = everyone
+
+
+def close(mixa, mixm, sorter, hs, gs, dx2, y1, y2, dn1, other, cid):
+    streams, tokens, width = hs.shape
+    return pl.pallas_call(
+        close_kernel,
+        out_shape=(
+            jax.ShapeDtypeStruct((tokens, streams, width), F32),
+            jax.ShapeDtypeStruct((tokens, streams, width), F32),
+            jax.ShapeDtypeStruct((48, 128), F32),
+        ),
+        in_specs=[*smem_spec(2), *vmem_spec(8)],
+        out_specs=tuple(vmem_spec(3)),
+        scratch_shapes=[
+            pltpu.VMEM((48, 16, 128), F32),
+            pltpu.VMEM((streams, tokens, width), F32),
+            pltpu.VMEM((streams, tokens, width), F32),
+            pltpu.VMEM((2, 48, 128), F32),
+            pltpu.VMEM((GROUP, 48, 128), F32),
+            pltpu.SemaphoreType.DMA((GROUP,)),
+            pltpu.SemaphoreType.DMA((GROUP,)),
+        ],
+        compiler_params=params(cid),
+    )(mixa, mixm, sorter, hs, gs, dx2, y1, y2, dn1, other)
 
 
 def slot_layout(lengths_row, capacity):
@@ -679,19 +1036,14 @@
 
     sorter = (jnp.arange(tokens, dtype=jnp.int32)[:, None] == deal[None, :]).astype(BF)
 
-    streams_in = streams.astype(F32)
-    grad_new = cotangent.astype(F32)
-    read_attn = jnp.sum(streams_in * mix_attn[:, 0][None, :, None], axis=1)
-    normed_attn, inverse_attn = normalize(read_attn)
-    low_attn = to_bins(dot(sorter, normed_attn.astype(BF)).astype(BF))
-    low_grad_mlp = jnp.sum(grad_new * mix_mlp[:, stream_count + 1][None, :, None], axis=1).astype(BF)
+    hs, gs, n1, low_grad_mlp = open_streams(mix_attn, mix_mlp, sorter, streams, cotangent)
+    low_attn = to_bins(n1)
 
     n1g, dy2g, qkvs, outs, gus, dns = front(
         low_attn, low_grad_mlp, gather_hi(w_qkv), gather_hi(w_out).reshape(-1, width), gather_hi(w_gu), gather_hi(w_down), 1
     )
     rows = w_qkv.shape[0]
     n1g = n1g.reshape(GROUP * tokens, width)
-    dy2g = dy2g.reshape(GROUP * tokens, width)
     qkvs = qkvs.reshape(width, 3 * HEAD_DIM)
     outs = outs.reshape(2, GROUP, hi, rows, width).swapaxes(1, 2).reshape(width, width)
     gus = gus.reshape(width, 2 * ff // GROUP)
@@ -727,53 +1079,17 @@
     probability = weights / jnp.sum(weights, -1, keepdims=True)
     low_probability = probability.astype(BF)
     attended = jnp.einsum("bqk,bkd->bqd", low_probability, values, preferred_element_type=F32).astype(BF)
-    home = swap(by_token(attended), 2)
-    attn_sorted = from_bins(home.swapaxes(0, 1).reshape(tokens, width))
-    attn_rows = t_dot(sorter, attn_sorted).astype(BF)
-
-    branch_attn = dot(attn_rows, outs)
-    middle_streams = write_streams(
-        streams_in, mix_attn[:, 1 : 1 + stream_count], branch_attn, mix_attn[:, stream_count + 1]
-    )
-    read_mlp = jnp.sum(middle_streams * mix_mlp[:, 0][None, :, None], axis=1)
-    normed_mlp, inverse_mlp = normalize(read_mlp)
-    n2g = gather(normed_mlp.astype(BF), 3).reshape(GROUP * tokens, width)
-    gate_up = dot(n2g, gus)
-    up_part = gate_up[:, : ff // GROUP]
-    gate_part = gate_up[:, ff // GROUP :]
-    sigmoid = jax.nn.sigmoid(gate_part)
-    silu_value = gate_part * sigmoid
-    hidden = (silu_value * up_part).astype(BF)
-    y2_part = dot_t(hidden, dns).astype(BF).reshape(GROUP, tokens, width)
-    grad_hidden = dot(dy2g, dns)
-    grad_up = grad_hidden * silu_value
-    grad_gate = grad_hidden * up_part * sigmoid * (1.0 + gate_part * (1.0 - sigmoid))
-    grad_gate_up = jnp.concatenate([grad_up, grad_gate], axis=1).astype(BF)
-    dn2_part = dot_t(grad_gate_up, gus).astype(BF).reshape(GROUP, tokens, width)
-    branch_mlp, grad_normed_mlp = scatter_two(y2_part, dn2_part, 4)
-    grad_read_mlp = normalize_back(grad_normed_mlp, normed_mlp, inverse_mlp)
-    new_streams = write_streams(
-        middle_streams, mix_mlp[:, 1 : 1 + stream_count], branch_mlp, mix_mlp[:, stream_count + 1]
-    )
-    mix_grad_mlp = mixing_grad(middle_streams, grad_new, branch_mlp, grad_read_mlp)
-    grad_middle = (
-        write_back(grad_new, mix_mlp[:, 1 : 1 + stream_count])
-        + grad_read_mlp[:, None, :] * mix_mlp[:, 0][None, :, None]
-    )
-    g_mlp = jnp.concatenate([t_dot(n2g, grad_gate_up), t_dot(dy2g, hidden)], axis=1).astype(BF)
-
-    def row_order(x):
-        return x.reshape(2, hi, GROUP, rows, -1).swapaxes(1, 2).reshape(2, GROUP * hi * rows, -1)
+    attn_rows = from_bins(swap(by_token(attended), 2))
+    y1, n2 = middle(mix_attn, mix_mlp, hs, attn_rows, outs)
+    dn2, y2_part, g_mlp = mlp(n2, dy2g, gus, dns, hi, 4)
+    dx2, low_grad_attn, grad_attn, mlp_sums = turn(mix_attn, mix_mlp, hs, gs, y1, dn2, outs)
 
     def own_rows(x):
-        x = x.astype(F32).reshape(GROUP, hi, rows, -1).transpose(1, 2, 0, 3)
+        x = x.astype(F32).transpose(1, 2, 0, 3)
         return sum_hi(x.reshape(hi, rows, -1)).reshape(rows, GROUP, -1)
 
-    g_mlp = own_rows(mlp_home(row_order(g_mlp), 5))
-    low_grad_attn = jnp.sum(grad_middle * mix_attn[:, stream_count + 1][None, :, None], axis=1).astype(BF)
-    grad_attn = dot_t(low_grad_attn, outs).astype(BF)
-    grad_sorted = to_bins(dot(sorter, grad_attn).astype(BF))
-    d_out = by_bin(swap(grad_sorted.reshape(tokens, GROUP, HEAD_DIM).swapaxes(0, 1), 6))
+    g_mlp = own_rows(g_mlp)
+    d_out = by_bin(swap(to_bins(grad_attn), 6))
     grad_values = jnp.einsum("bqk,bqd->bkd", low_probability, d_out, preferred_element_type=F32)
     grad_probs = jnp.einsum("bqd,bkd->bqk", d_out, values, preferred_element_type=F32)
     shared = jnp.sum(grad_probs * probability, -1, keepdims=True)
@@ -786,21 +1102,19 @@
         ).astype(BF)
     ).reshape(GROUP * tokens, 3 * HEAD_DIM)
     dn1_part = dot_t(grad_qkv, qkvs).astype(BF).reshape(GROUP, tokens, width)
-    g_qkv = row_order(t_dot(n1g, grad_qkv).astype(BF))
-    g_out = row_order(t_dot(attn_rows, low_grad_attn).astype(BF))
-    dn1, g_out, g_qkv = back(dn1_part, g_out, g_qkv, 7)
+    g_qkv = t_dot(n1g, grad_qkv).astype(BF).reshape(2, width // 2, -1)
+    g_out = t_dot(attn_rows, low_grad_attn).astype(BF)
+    g_out = g_out.reshape(2, hi, GROUP, rows, width).swapaxes(1, 2).reshape(2, width // 2, width)
+    dn1, y2, g_out, g_qkv = back(dn1_part, y2_part, g_out, g_qkv, hi, 7)
     g_out = sum_hi(g_out.reshape(hi, rows, width))
     g_qkv = own_rows(g_qkv)
-    dn1 = lax.dot_general(
-        sorter.astype(F32), from_bins(dn1), CONTRACT_FIRST, precision=lax.Precision.HIGHEST, preferred_element_type=F32
+    new_streams, d_streams, sums = close(
+        mix_attn, mix_mlp, sorter, hs, gs, dx2, y1, y2, from_bins(dn1), mlp_sums, 8
     )
-    grad_read_attn = normalize_back(dn1, normed_attn, inverse_attn)
-    mix_grad_attn = mixing_grad(streams_in, grad_middle, branch_attn, grad_read_attn)
-    d_streams = (
-        write_back(grad_middle, mix_attn[:, 1 : 1 + stream_count])
-        + grad_read_attn[:, None, :] * mix_attn[:, 0][None, :, None]
-    )
-    g_mix_attn, g_mix_mlp = lax.psum((mix_grad_attn, mix_grad_mlp), ("rep", "shard"))
+    if hi > 1:
+        sums = lax.psum(sums, "shard", axis_index_groups=hi_groups)
+    sums = jnp.sum(sums, axis=-1).reshape(2, 4, 6)
+    g_mix_attn, g_mix_mlp = sums[0], sums[1]
     block = ff // GROUP
     return (
         new_streams,

time: 1210 us -> 935 us (0.77)
  matrix products: 220 us -> 46 us
  local copies, waits for them, and re-layouts: 122 us -> 35.7 us
  Pallas kernels: 738 us -> 824 us
  other arithmetic: 79.8 us -> 19.2 us
  blocking collectives: 38.4 us -> 0 us
    dot_general x7 -> x0, matrix products: 85 us -> none  [the longest x2 29.9 us: mixing_grad(): first = jnp.einsum('tjd,td->j', streams, grad_read, precision=highest)]
    pallas_call x1, Pallas kernels: 139 us -> 206 us  [back(): pl.pallas_call(back_kernel, out_shape=(jax.ShapeDtypeStruct((rows, d), F3...]
    dot_general x6 -> x1, matrix products: 52.3 us -> 4.52 us  [dot(): return jnp.dot(a, b, preferred_element_type=F32)]
    reduce_sum x7 -> x1, other arithmetic: 44 us -> 0.85 us  [shards(): sums = jnp.sum(sums, axis=-1).reshape(2, 4, 6)]
    psum x1 -> x0, blocking collectives: 38.4 us -> none  [shards(): lax.psum((mix_grad_attn, mix_grad_mlp), ('rep', 'shard'))]
    mul x22 -> x0, local copies, waits for them, and re-layouts: 34.8 us -> none  [the longest x11 17.2 us: write_streams(): streams[:, source, None, :] * mixing[source][None, :, None]]
    dot_general x4 -> x0, local copies, waits for them, and re-layouts: 28.2 us -> none  [the longest x2 25 us: t_dot(): return lax.dot_general(a, b, CONTRACT_FIRST, preferred_element_type=F32)]
    dot_general x5 -> x2, matrix products: 37.7 us -> 14.8 us  [t_dot(): return lax.dot_general(a, b, CONTRACT_FIRST, preferred_element_type=F32)]
where the time goes in v2:
time: 935 us; the launch traced here: 926 us
  Pallas kernels  824 us (88%)
  matrix products  46 us (5%)
  local copies, waits for them, and re-layouts  35.7 us (4%)
  other arithmetic  19.2 us (2%)
    pallas_call x1, Pallas kernels, front(): pl.pallas_call(front_kernel, out_shape=(shape(GROUP, *n1.shape), shape(GR...  250 us
    pallas_call x1, Pallas kernels, mlp(): pl.pallas_call(mlp_kernel, out_shape=(jax.ShapeDtypeStruct((tokens, width...  248 us
    pallas_call x1, Pallas kernels, back(): pl.pallas_call(back_kernel, out_shape=(jax.ShapeDtypeStruct((rows, d), F3...  206 us
    pallas_call x2, Pallas kernels, swap(): pl.pallas_call(swap_kernel, out_shape=jax.ShapeDtypeStruct(shape, x.dtype...  43.6 us
    pallas_call x1, Pallas kernels, close(): pl.pallas_call(close_kernel, out_shape=(jax.ShapeDtypeStruct((tokens, str...  31.4 us
    unnamed x61, local copies, waits for them, and re-layouts  22.4 us

profile of v2, /device:TPU:0, one launch (start us, length us, event | category | flops | bytes accessed | tf_op | source)
XLA Modules:
  0.0 926.1 jit_solution(4649417010120604034)
XLA Ops:
  2.8 1.3 fusion.48.sorter
  4.1 18.5 %shard_map.161 = (bf16[4,128,2048]{2,1,0:T(8,128)(2,1)}, bf16[4,128,2048]{2,1,0:T(8,128)(2,1)}, bf16[128,2048]{1,0:T(8,128)(2,1)}, bf16[128,2048]{1,0:T(8,128)(2,1)}) custom-call(f32[4,6]{1,0:T(4,128)} %mixa.7, f32[4,6]{1,0:T(4,128)} %mixm.7, bf16[128,128]{1,0:T(8,128)(2,1)} %fusion.48.sorter, bf16[128,4,2048]{2,1,0:T(4,128)(2,1)} %x.1, bf16[128,4,2048]{2,1,0:T(4,128)(2,1)} %g.1), custom_call_target="tpu_custom_call" | custom-call | tf_op jit(solution)/shard_map/pallas_call | solution.py:768
  25.8 250.4 %shard_map.162 = (bf16[16,128,2048]{2,1,0:T(8,128)(2,1)S(1)}, bf16[16,128,2048]{2,1,0:T(8,128)(2,1)S(1)}, bf16[2,1,16,64,384]{4,3,2,1,0:T(8,128)(2,1)S(1)}, bf16...) custom-call(bf16[128,2048]{1,0:T(8,128)(2,1)S(1)} %copy-done.6, ...), custom_call_target="tpu_custom_call" | custom-call | tf_op jit(solution)/shard_map/pallas_call | solution.py:338
  276.3 3.2 copy-done.11
  279.5 4.5 convolution_convert_fusion.3
  284.0 1.2 copy-done.10
  285.2 1.6 copy-done.12
  288.2 5.7 fusion.34
  293.9 5.2 fusion.53
  299.1 4.9 convolution_convert_fusion.5
  305.1 20.2 %shard_map.163.attn = bf16[128,2048]{1,0:T(8,128)(2,1)S(1)} custom-call(bf16[16,128,128]{2,1,0:T(8,128)(2,1)S(1)} %bitcast.69), custom_call_target="tpu_custom_call" | custom-call | tf_op jit(solution)/shard_map/pallas_call | solution.py:393
  326.1 9.1 shard_map.164
  335.3 248.3 %shard_map.165 = (f32[128,2048]{1,0:T(8,128)}, bf16[16,128,2048]{2,1,0:T(8,128)(2,1)}, bf16[16,1,64,1536]{3,2,1,0:T(8,128)(2,1)}) custom-call(bf16[128,2048]{1,0:T(8,128)(2,1)} %get-tuple-element.42.n2, bf16[16,128,2048]{2,1,0:T(8,128)(2,1)} %copy-done.11, bf16[2048,1024]{1,0:T(8,128)(2,1)} %bitcast.75, bf16[2048,512]{1,0:T(8,128)(2,1)} %bitcast.76), custom_call_target="tpu_custom_call" | custom-call | flops 38654705664 | bytes 62914560 | tf_op jit(solution)/shard_map/pallas_call | solution.py:598
  583.6 16.6 %shard_map.166 = (f32[128,2048]{1,0:T(8,128)}, bf16[128,2048]{1,0:T(8,128)(2,1)}, bf16[128,2048]{1,0:T(8,128)(2,1)}, f32[24,16,128]{2,1,0:T(8,128)}) custom-call(f32[4,6]{1,0:T(4,128)} %mixa.7, f32[4,6]{1,0:T(4,128)} %mixm.7, bf16[4,128,2048]{2,1,0:T(8,128)(2,1)} %get-tuple-element.34.hs, bf16[4,128,2048]{2,1,0:T(8,128)(2,1)} %get-tuple-element.35.gs, ...), custom_call_target="tpu_custom_call" | custom-call | tf_op jit(solution)/shard_map/pallas_call | solution.py:865
  601.2 23.3 %shard_map.167 = bf16[16,128,128]{2,1,0:T(8,128)(2,1)S(1)} custom-call(bf16[128,2048]{1,0:T(8,128)(2,1)S(1)} %copy-done.8), custom_call_target="tpu_custom_call" | custom-call | tf_op jit(solution)/shard_map/pallas_call | solution.py:393
  624.6 4.5 convolution_convert_fusion.4
  629.1 3.2 multiply_reduce_fusion
  635.7 5.7 fusion.32
  641.5 2.7 concatenate.35
  644.4 9.2 convolution_convert_fusion.2
  653.7 7.0 convolution_convert_fusion
  662.3 1.5 copy.106
  664.3 2.3 pad_maximum_fusion
  666.6 5.6 convolution_convert_fusion.1
  672.2 205.9 %shard_map.168 = (f32[128,2048]{1,0:T(8,128)}, f32[128,2048]{1,0:T(8,128)}, f32[64,2048]{1,0:T(8,128)}, bf16[16,1,64,384]{3,2,1,0:T(8,128)(2,1)}) custom-call(bf16[16,128,2048]{2,1,0:T(8,128)(2,1)} %bitcast.80, bf16[16,128,2048]{2,1,0:T(8,128)(2,1)} %get-tuple-element.49.y2_in, bf16[2,1024,2048]{2,1,0:T(8,128)(2,1)} %bitcast.79, bf16[2,1024,384]{2,1,0:T(8,128)(2,1)} %bitcast.93), custom_call_target="tpu_custom_call" | custom-call | tf_op jit(solution)/shard_map/pallas_call | solution.py:664
  878.1 31.4 %shard_map.169 = (f32[128,4,2048]{2,1,0:T(4,128)}, f32[128,4,2048]{2,1,0:T(4,128)}, f32[48,128]{1,0:T(8,128)}) custom-call(f32[4,6]{1,0:T(4,128)} %mixa.7, f32[4,6]{1,0:T(4,128)} %mixm.7, bf16[128,128]{1,0:T(8,128)(2,1)} %fusion.48.sorter, bf16[4,128,2048]{2,1,0:T(8,128)(2,1)} %get-tuple-element.34.hs, bf16[4,128,2048]{2,1,0:T(8,128)(2,1)} %get-tuple-element.35.gs, ...), custom_call_target="tpu_custom_call" | custom-call | tf_op jit(solution)/shard_map/pallas_call | solution.py:937
  911.9 2.1 copy.91
  914.0 2.5 reshape.190
  916.6 1.6 copy.109
  919.2 2.1 copy.113
  921.3 1.6 copy-done.18
  922.9 2.0 copy.114
  (81 shorter events, 19.7 us)
Async XLA Ops:
  0.6 22.0 %copy-start.4 = (bf16[64,8192]{1,0:T(8,128)(2,1)S(1)}, bf16[64,8192]{1,0:T(8,128)(2,1)}, u32[]{:S(2)}) copy-start(bf16[64,8192]{1,0:T(8,128)(2,1)} %param.19) | copy-start | bytes 3145732
  0.6 22.0 %copy-start.3 = (bf16[64,16384]{1,0:T(8,128)(2,1)S(1)}, bf16[64,16384]{1,0:T(8,128)(2,1)}, u32[]{:S(2)}) copy-start(bf16[64,16384]{1,0:T(8,128)(2,1)} %param.18) | copy-start | bytes 6291460
  0.7 22.0 %copy-start.9 = (bf16[64,2048]{1,0:T(8,128)(2,1)S(1)}, bf16[64,2048]{1,0:T(8,128)(2,1)}, u32[]{:S(2)}) copy-start(bf16[64,2048]{1,0:T(8,128)(2,1)} %wout.1) | copy-start | bytes 786436
  22.6 1.1 copy-start.5
  23.8 1.0 copy-start.6
  24.8 1.0 copy-start.7
  276.3 3.2 copy-start.11
  279.5 4.5 copy-start
  279.5 5.7 copy-start.10
  279.5 7.3 copy-start.12
  279.5 7.9 copy-start.13
  279.5 8.3 copy-start.14
  288.0 11.0 %copy-start.16 = (bf16[4,16,32,384]{3,2,1,0:T(8,128)(2,1)}, bf16[4,16,32,384]{3,2,1,0:T(8,128)(2,1)S(1)}, u32[]{:S(2)}) copy-start(bf16[4,16,32,384]{3,2,1,0:T(8,128)(2,1)S(1)} %copy.76) | copy-start | bytes 4718596
  293.9 5.2 copy-start.21
  325.4 0.8 copy-start.1
  583.6 41.0 %copy-start.22 = (bf16[4,512,64]{2,1,0:T(8,128)(2,1)S(1)}, bf16[4,512,64]{2,1,0:T(8,128)(2,1)}, u32[]{:S(2)}) copy-start(bf16[4,512,64]{2,1,0:T(8,128)(2,1)} %copy-done.21) | copy-start | bytes 786436
  583.6 41.0 %copy-start.23 = (bf16[4,512,64]{2,1,0:T(8,128)(2,1)S(1)}, bf16[4,512,64]{2,1,0:T(8,128)(2,1)}, u32[]{:S(2)}) copy-start(bf16[4,512,64]{2,1,0:T(8,128)(2,1)} %get-tuple-element.71) | copy-start | bytes 786436
  600.2 1.0 copy-start.8
  629.1 3.6 copy-start.17
  632.7 1.2 copy-start.24
  644.4 9.2 copy-start.15
  653.7 7.0 copy-start.20
  664.2 2.3 copy-start.2
  664.3 2.3 copy-start.26
  878.1 33.6 %copy-start.25 = (bf16[16,1,64,384]{3,2,1,0:T(8,128)(2,1)S(1)}, bf16[16,1,64,384]{3,2,1,0:T(8,128)(2,1)}, u32[]{:S(2)}) copy-start(bf16[16,1,64,384]{3,2,1,0:T(8,128)(2,1)} %get-tuple-element.57) | copy-start | bytes 2359300
  916.5 2.8 copy-start.19
  919.2 3.7 copy-start.18
  922.9 2.0 copy-start.27

commit v3 on v2

--- a/solution.py
+++ b/solution.py
@@ -455,12 +455,12 @@
 
 
 def mlp_kernel(
-    n2, dy2g_in, wgu_in, wdn_in, dn2, y2p, home,
-    n2g, dy2g, wgu, wdn, part, hidden, dgu, y2s, grads, inbox,
-    gsend, grecv, own, load, y2sem, psend, precv, hsend, hrecv, hown, *scratch,
+    mixa, mixm, n2, dy2g_in, wgu_in, wdn_in, hs, gs, wout, y1, y2p, grads_out, dx2, dy1, d_out, sums,
+    n2g, dy2g, wgu, wdn, part, hidden, dgu, y2s, grads, inbox, dn2,
+    gsend, grecv, own, load, y2sem, psend, precv, late, *scratch,
 ):
     here = Here()
-    barrier(here, ALL, True)
+    barrier(here, TREE, True)
     g = Gather(here, n2, n2g, gsend, grecv)
     rs = Scatter(here, part, scratch)
     g.begin(own)
@@ -570,6 +570,13 @@
         return carry
 
     lax.fori_loop(0, chunks, own_half, 0)
+    g.end()
+    streams = hs.shape[0]
+    loads = []
+    for i, (src, dst) in enumerate(((hs, n2g.at[:streams]), (gs, n2g.at[streams : 2 * streams]), (wout, dy2g))):
+        c = pltpu.make_async_copy(src, dst, late.at[i])
+        c.start()
+        loads.append(c)
 
     def add(k, carry):
         pass_chunk(k).wait()
@@ -582,15 +589,18 @@
         return lax.fori_loop(0, step // 16, rows_add, carry)
 
     lax.fori_loop(0, chunks, add, 0)
-    finish = send_home(here, grads.at[here.rep], home, hsend, hrecv, hown)
+    out = pltpu.make_async_copy(grads.at[here.rep], grads_out, late.at[3])
+    out.start()
     rs.finish(0, dn2)
+    for c in loads:
+        c.wait()
+    turn(read_mix(mixa), read_mix(mixm), n2g, y1, dn2, dy2g, dx2, dy1, d_out, sums)
+    out.wait()
     y2copies[-1].wait()
-    finish()
-    g.end()
     rs.end()
 
 
-def mlp(n2, dy2g, wgu, wdn, hi, cid):
+def mlp(mixa, mixm, n2, dy2g, wgu, wdn, hs, gs, wout, y1, cid):
     tokens, width = n2.shape
     ff = wdn.shape[1]
     half = width // 2
@@ -598,12 +608,15 @@
     return pl.pallas_call(
         mlp_kernel,
         out_shape=(
+            jax.ShapeDtypeStruct((*blocks, width), BF),
+            jax.ShapeDtypeStruct((half, 3 * ff), BF),
             jax.ShapeDtypeStruct((tokens, width), F32),
-            jax.ShapeDtypeStruct((*blocks, width), BF),
-            jax.ShapeDtypeStruct((GROUP, hi, half // (hi * GROUP), 3 * ff), BF),
+            jax.ShapeDtypeStruct((tokens, width), BF),
+            jax.ShapeDtypeStruct((tokens, width), BF),
+            jax.ShapeDtypeStruct((24, 16, 128), F32),
         ),
-        in_specs=[*vmem_spec(1), *any_spec(3)],
-        out_specs=(*vmem_spec(1), *any_spec(2)),
+        in_specs=[*smem_spec(2), *vmem_spec(1), *any_spec(6), *vmem_spec(1)],
+        out_specs=(*any_spec(2), *vmem_spec(4)),
         scratch_shapes=[
             pltpu.VMEM((*blocks, width), BF),
             pltpu.VMEM((*blocks, width), BF),
@@ -615,6 +628,7 @@
             pltpu.VMEM((4, tokens, width), BF),
             pltpu.VMEM((2, half, 3 * ff), BF),
             pltpu.VMEM((half, 3 * ff), BF),
+            pltpu.VMEM((tokens, width), F32),
             pltpu.SemaphoreType.DMA(Gather.sems),
             pltpu.SemaphoreType.DMA(Gather.sems),
             pltpu.SemaphoreType.DMA,
@@ -622,73 +636,246 @@
             pltpu.SemaphoreType.DMA((4,)),
             pltpu.SemaphoreType.DMA((half // 256,)),
             pltpu.SemaphoreType.DMA((half // 256,)),
-            *home_sems(hi),
+            pltpu.SemaphoreType.DMA((4,)),
             *Scatter.scratch(tokens, width),
         ],
         compiler_params=params(cid, 63),
         cost_estimate=pl.CostEstimate(
             flops=2 * GROUP * tokens * width * ff * 9, bytes_accessed=60 * MIB, transcendentals=0
         ),
-    )(n2, dy2g, wgu, wdn)
-
-
-def back_kernel(dn_in, y2_in, gout_in, gqkv, dn_out, y2_out, gout_out, gqkv_out, dn, y2, gout, load, *scratch):
+    )(mixa, mixm, n2, dy2g, wgu, wdn, hs, gs, wout.reshape(GROUP, tokens, width), y1)
+
+
+def rope_parts(rope):
+    other = pltpu.roll(rope, HEAD_DIM // 2, 1)
+    first = lax.broadcasted_iota(jnp.int32, rope.shape, 1) < HEAD_DIM // 2
+    return jnp.where(first, rope, other), jnp.where(first, -other, rope)
+
+
+def turned(x, cosine, sine):
+    return x * cosine + pltpu.roll(x, HEAD_DIM // 2, 1) * sine
+
+
+CODE = 4096
+
+
+def head_of_bin(qkv, tables, b):
+    rope, code_row, code_col = tables
+    slots = qkv.shape[1] // rope.shape[0]
+    rows = pl.ds(b * slots, slots)
+    n = GROUP * slots
+
+    def piece(i):
+        return qkv[:, rows, i * HEAD_DIM : (i + 1) * HEAD_DIM].reshape(n, HEAD_DIM)
+
+    cos, sin = rope_parts(rope[b])
+    queries = turned(piece(0).astype(F32), cos, sin).astype(BF)
+    keys = turned(piece(1).astype(F32), cos, sin).astype(BF)
+    query_code, key_code = code_row[b], code_col[b]
+    segment_code = query_code - jnp.bitwise_and(query_code, CODE - 1)
+    seen = (key_code <= query_code) & (key_code >= segment_code)
+    scores = jnp.where(seen, dot_t(queries, keys) * (1.0 / math.sqrt(HEAD_DIM)), -1e30)
+    weights = jnp.exp(scores - jnp.max(scores, -1, keepdims=True))
+    probability = weights / jnp.sum(weights, -1, keepdims=True)
+    return queries, keys, piece(2), probability, rows, cos, sin
+
+
+def attend_back(qkv, d_out, dqkv, tables, b):
+    queries, keys, values, probability, rows, cos, sin = head_of_bin(qkv, tables, b)
+    n, slots = queries.shape[0], rows.size
+    scale = 1.0 / math.sqrt(HEAD_DIM)
+    grad = d_out[:, rows].reshape(n, HEAD_DIM)
+    grad_values = t_dot(probability.astype(BF), grad)
+    grad_probs = dot_t(grad, values)
+    shared = jnp.sum(grad_probs * probability, -1, keepdims=True)
+    grad_scores = (probability * (grad_probs - shared)).astype(BF)
+    grad_query = dot(grad_scores, keys) * scale
+    grad_keys = t_dot(grad_scores, queries) * scale
+    for i, v in enumerate((turned(grad_query, cos, -sin), turned(grad_keys, cos, -sin), grad_values)):
+        dqkv[:, rows, i * HEAD_DIM : (i + 1) * HEAD_DIM] = v.astype(BF).reshape(GROUP, slots, HEAD_DIM)
+
+
+def back_kernel(
+    d_rows, qkv, qkvs, dy1, attn, rope, code_row, code_col, n1g, y2_in, gmlp,
+    dn_out, y2_out, gout_out, gqkv_out, gmlp_out,
+    d_out, dqkv, dn, y2, gout, stage, gqkv, tiles, obox, qbox,
+    dsend, drecv, down, load, tile_sem, osend, orecv, qsend, qrecv, *scratch,
+):
     here = Here()
     barrier(here, ALL, True)
-    loads = []
-    for i, (src, dst) in enumerate(((gout_in, gout), (dn_in, dn), (y2_in, y2))):
-        c = pltpu.make_async_copy(src, dst, load.at[i])
+    tables = (rope, code_row, code_col)
+    bins = rope.shape[0]
+    swaps = []
+    for m in ALL:
+        at = pl.ds(pl.multiple_of(here.flip(m) * HEAD_DIM, HEAD_DIM), HEAD_DIM)
+        c = rcopy(d_rows.at[:, at], d_out.at[here.lo], dsend.at[m], drecv.at[m], here.dev(m))
         c.start()
-        loads.append(c)
-    n = len(Scatter.scratch(16, 128))
-    s1, scratch = scratch[:n], scratch[n:]
-    s2, scratch = scratch[:n], scratch[n:]
-    s3, scratch = scratch[:n], scratch[n:]
-    (obox, osend, orecv), scratch = scratch[:3], scratch[3:]
-    pair_add(here, gqkv, *scratch[:3])
-    end = send_home(here, gqkv.at[here.rep], gqkv_out, *scratch[3:])
-    for c in loads:
-        c.wait()
-    pair_add(here, gout, obox, osend, orecv)
-    sums = gout.reshape(2, GROUP, gout.shape[1] // GROUP, gout.shape[2]).at[here.rep]
-    run_scatters(
-        [Scatter(here, dn, s1), Scatter(here, y2, s2), Scatter(here, sums, s3)], [dn_out, y2_out, gout_out]
-    )
-    end()
-
-
-def back(dn, y2, gout, gqkv, hi, cid):
-    _, rows, d = dn.shape
-    n, w = gqkv.shape[1:]
-    on, od = gout.shape[1:]
+        swaps.append(c)
+    at = pl.ds(pl.multiple_of(here.lo * HEAD_DIM, HEAD_DIM), HEAD_DIM)
+    mine = pltpu.make_async_copy(d_rows.at[:, at], d_out.at[here.lo], down)
+    mine.start()
+    y2_load = pltpu.make_async_copy(y2_in, y2, load)
+    y2_load.start()
+    _, tokens, width = dn.shape
+    k = len(Scatter.scratch(16, 128))
+    rs_dn = Scatter(here, dn, scratch[:k])
+    rs_y2 = Scatter(here, y2, scratch[k : 2 * k])
+    rs_go = Scatter(here, gout.reshape(GROUP, gout.shape[0] // GROUP, width), scratch[2 * k : 3 * k])
+    qhome, mhome = scratch[3 * k : 3 * k + 3], scratch[3 * k + 3 :]
+    order = rs_y2.ORDER
+    y2_load.wait()
+    for j in order:
+        rs_y2.start(j)
+    end_mlp = send_home(here, gmlp, gmlp_out, *mhome)
+    mine.wait()
+    for m in ALL:
+        ref = d_out.at[here.flip(m)]
+        rcopy(ref, ref, dsend.at[m], drecv.at[m], here.dev(m)).wait_recv()
+
+    half = width // 2
+    step = 256
+    chunks = half // step
+
+    def out_grads(which, k):
+        cols = pl.ds(pl.multiple_of(which * half + k * step, step), step)
+        return t_dot(attn[:, cols], dy1[...]).astype(BF)
+
+    def gout_pass(k):
+        at = pl.ds(k * step, step)
+        return rcopy(stage.at[k % 2], obox.at[at], osend.at[k], orecv.at[k], here.partner())
+
+    gqkv_pair = rcopy(gqkv.at[1 - here.rep], qbox, qsend, qrecv, here.partner())
+
+    for b in range(bins):
+        attend_back(qkv, d_out, dqkv, tables, b)
+        if b == 0:
+            rs_y2.cross(order[0])
+        elif b < 3:
+            rs_y2.cross(order[b])
+            rs_y2.finish(order[b - 1])
+    rs_y2.cross(order[3])
+    rs_y2.finish(order[2])
+
+    narrow = tiles.shape[3]
+
+    def qkv_tile(k):
+        cols = pl.ds(k * narrow, narrow)
+        return pltpu.make_async_copy(n1g.at[:, :, cols], tiles.at[k % 2], tile_sem.at[k % 2])
+
+    qkv_tile(0).start()
+    for j in order:
+        blocks = pl.ds(here.flip(4 * j) - here.lo % 4, 4)
+
+        def part(k, carry, blocks=blocks):
+            at = pl.ds(pl.multiple_of(k * TILE, TILE), TILE)
+            d = dqkv[blocks].reshape(4 * tokens, 3 * HEAD_DIM)
+            dn[blocks, :, at] = dot_t(d, qkvs[at, :]).astype(BF).reshape(4, tokens, TILE)
+            return carry
+
+        lax.fori_loop(0, width // TILE, part, 0)
+        rs_dn.start(j)
+    count = width // narrow
+    for k in range(count):
+        if k + 1 < count:
+            qkv_tile(k + 1).start()
+        qkv_tile(k).wait()
+        x = tiles[k % 2].reshape(GROUP * tokens, narrow)
+        rows = pl.ds((k % (count // 2)) * narrow, narrow)
+        gqkv[k // (count // 2), rows, :] = t_dot(x, dqkv[...].reshape(GROUP * tokens, 3 * HEAD_DIM)).astype(BF)
+    gqkv_pair.start()
+    rs_y2.finish(0, y2_out)
+    rs_dn.cross(order[0])
+    for k in range(chunks):
+        if k >= 2:
+            gout_pass(k - 2).wait_send()
+        stage[k % 2] = out_grads(1 - here.rep, k)
+        gout_pass(k).start()
+    rs_dn.cross(order[1])
+    rs_dn.finish(order[0])
+    for k in range(chunks):
+        gout[k * step : (k + 1) * step, :] = out_grads(here.rep, k)
+
+    def add(ref, box):
+        def body(r):
+            ref[r] = (ref[r].astype(F32) + box[r].astype(F32)).astype(BF)
+
+        rowwise(box.shape[0], 16, body)
+
+    gqkv_pair.wait()
+    add(gqkv.at[here.rep], qbox)
+    end_qkv = send_home(here, gqkv.at[here.rep], gqkv_out, *qhome)
+    rs_dn.cross(order[2])
+    rs_dn.finish(order[1])
+    for k in range(chunks):
+        gout_pass(k).wait_recv()
+        if k >= chunks - 2:
+            gout_pass(k).wait_send()
+    add(gout, obox)
+    for j in order:
+        rs_go.start(j)
+    rs_dn.cross(order[3])
+    rs_dn.finish(order[2])
+    rs_go.cross(order[0])
+    rs_go.cross(order[1])
+    rs_go.finish(order[0])
+    rs_go.cross(order[2])
+    rs_go.finish(order[1])
+    rs_go.cross(order[3])
+    rs_go.finish(order[2])
+    rs_dn.finish(0, dn_out)
+    rs_go.finish(0, gout_out)
+    end_mlp()
+    end_qkv()
+    for c in swaps:
+        c.wait_send()
+    for rs in (rs_dn, rs_y2, rs_go):
+        rs.end()
+
+
+def back(d_rows, qkv, qkvs, dy1, attn, tables, n1g, y2, gmlp, hi, cid):
+    tokens, width = d_rows.shape
+    half = width // 2
+    w = qkv.shape[2]
+    blocks = (GROUP, tokens, width)
     return pl.pallas_call(
         back_kernel,
         out_shape=(
-            jax.ShapeDtypeStruct((rows, d), F32),
-            jax.ShapeDtypeStruct((rows, d), F32),
-            jax.ShapeDtypeStruct((on // GROUP, od), F32),
-            jax.ShapeDtypeStruct((GROUP, hi, n // (hi * GROUP), w), BF),
+            jax.ShapeDtypeStruct((tokens, width), F32),
+            jax.ShapeDtypeStruct((tokens, width), F32),
+            jax.ShapeDtypeStruct((half // GROUP, width), F32),
+            jax.ShapeDtypeStruct((GROUP, hi, half // (hi * GROUP), w), BF),
+            jax.ShapeDtypeStruct((GROUP, hi, half // (hi * GROUP), gmlp.shape[1]), BF),
         ),
-        in_specs=[*any_spec(3), *vmem_spec(1)],
-        out_specs=(*vmem_spec(3), *any_spec(1)),
+        in_specs=[*vmem_spec(8), *any_spec(3)],
+        out_specs=(*vmem_spec(3), *any_spec(2)),
         scratch_shapes=[
-            pltpu.VMEM(dn.shape, BF),
-            pltpu.VMEM(y2.shape, BF),
-            pltpu.VMEM(gout.shape, BF),
-            pltpu.SemaphoreType.DMA((3,)),
-            *Scatter.scratch(rows, d),
-            *Scatter.scratch(rows, d),
-            *Scatter.scratch(on // GROUP, od),
-            pltpu.VMEM((on, od), BF),
+            pltpu.VMEM((GROUP, tokens, HEAD_DIM), BF),
+            pltpu.VMEM((GROUP, tokens, w), BF),
+            pltpu.VMEM(blocks, BF),
+            pltpu.VMEM(blocks, BF),
+            pltpu.VMEM((half, width), BF),
+            pltpu.VMEM((2, 256, width), BF),
+            pltpu.VMEM((2, half, w), BF),
+            pltpu.VMEM((2, GROUP, tokens, TILE // 4), BF),
+            pltpu.VMEM((half, width), BF),
+            pltpu.VMEM((half, w), BF),
+            pltpu.SemaphoreType.DMA((GROUP,)),
+            pltpu.SemaphoreType.DMA((GROUP,)),
             pltpu.SemaphoreType.DMA,
             pltpu.SemaphoreType.DMA,
-            pltpu.VMEM((n, w), BF),
+            pltpu.SemaphoreType.DMA((2,)),
+            pltpu.SemaphoreType.DMA((half // 256,)),
+            pltpu.SemaphoreType.DMA((half // 256,)),
             pltpu.SemaphoreType.DMA,
             pltpu.SemaphoreType.DMA,
+            *Scatter.scratch(tokens, width),
+            *Scatter.scratch(tokens, width),
+            *Scatter.scratch(half // GROUP, width),
+            *home_sems(hi),
             *home_sems(hi),
         ],
         compiler_params=params(cid, 63),
-    )(dn, y2, gout, gqkv)
+    )(d_rows, qkv, qkvs, dy1, attn, *tables, n1g, y2, gmlp)
 
 
 def read_mix(ref):
@@ -827,21 +1014,20 @@
         lax.fori_loop(0, width // TILE, tile, 0)
 
 
-def turn_kernel(mixa, mixm, hs, gs, y1, dn2, wout, dx2, dy1, d_out, sums):
-    m, p = read_mix(mixa), read_mix(mixm)
+def turn(m, p, planes, y1, dn2, wout, dx2, dy1, d_out, sums):
     tokens, width = y1.shape
     sums[...] = jnp.zeros_like(sums)
 
     def body(r):
-        x2 = read_x2(m, p, [hs[j, r].astype(F32) for j in range(4)], y1[r])
+        x2 = read_x2(m, p, [planes[j, r].astype(F32) for j in range(4)], y1[r])
         normed, inverse = moments(x2)
         dx2[r] = normalize_back(dn2[r], normed, inverse)
         for c in range(0, width, TILE):
             at = slice(c, c + TILE)
-            h = [hs[j, r, at].astype(F32) for j in range(4)]
+            h = [planes[j, r, at].astype(F32) for j in range(4)]
             y = y1[r, at]
             h1 = [mixed([*(m[j][1 + i] for j in range(4)), m[i][5]], [*h, y]) for i in range(4)]
-            g = [gs[j, r, at].astype(F32) for j in range(4)]
+            g = [planes[4 + j, r, at].astype(F32) for j in range(4)]
             dx = dx2[r, at]
             g1 = [mixed([*(p[j][1 + i] for i in range(4)), p[j][0]], [*g, dx]) for j in range(4)]
             dy1[r, at] = mixed([m[j][5] for j in range(4)], g1).astype(BF)
@@ -851,29 +1037,15 @@
                     sums[j * 6 + 1 + i] += lane_sums(h1[j] * g[i])
 
     rowwise(tokens, 16, body)
+    blocks = TILE // wout.shape[1]
 
     def tile(i, carry):
         at = pl.ds(pl.multiple_of(i * TILE, TILE), TILE)
-        d_out[:, at] = dot_t(dy1[...], wout[at, :]).astype(BF)
+        rows = wout[pl.ds(i * blocks, blocks)].reshape(TILE, width)
+        d_out[:, at] = dot_t(dy1[...], rows).astype(BF)
         return carry
 
     lax.fori_loop(0, width // TILE, tile, 0)
-
-
-def turn(mixa, mixm, hs, gs, y1, dn2, wout):
-    streams, tokens, width = hs.shape
-    return pl.pallas_call(
-        turn_kernel,
-        out_shape=(
-            jax.ShapeDtypeStruct((tokens, width), F32),
-            jax.ShapeDtypeStruct((tokens, width), BF),
-            jax.ShapeDtypeStruct((tokens, width), BF),
-            jax.ShapeDtypeStruct((24, 16, 128), F32),
-        ),
-        in_specs=[*smem_spec(2), *vmem_spec(5)],
-        out_specs=tuple(vmem_spec(4)),
-        compiler_params=local_params(),
-    )(mixa, mixm, hs, gs, y1, dn2, wout)
 
 
 def close_kernel(
@@ -1043,7 +1215,6 @@
         low_attn, low_grad_mlp, gather_hi(w_qkv), gather_hi(w_out).reshape(-1, width), gather_hi(w_gu), gather_hi(w_down), 1
     )
     rows = w_qkv.shape[0]
-    n1g = n1g.reshape(GROUP * tokens, width)
     qkvs = qkvs.reshape(width, 3 * HEAD_DIM)
     outs = outs.reshape(2, GROUP, hi, rows, width).swapaxes(1, 2).reshape(width, width)
     gus = gus.reshape(width, 2 * ff // GROUP)
@@ -1067,7 +1238,8 @@
         return x.reshape(my_bins, GROUP, slots, -1).swapaxes(0, 1).reshape(GROUP, tokens, -1)
 
     scale = 1.0 / math.sqrt(HEAD_DIM)
-    qkv = by_bin(dot(n1g, qkvs).astype(BF))
+    raw_qkv = dot(n1g.reshape(GROUP * tokens, width), qkvs).astype(BF)
+    qkv = by_bin(raw_qkv)
     queries = rotate(qkv[..., :HEAD_DIM].astype(F32), cosine, sine).astype(BF)
     keys = rotate(qkv[..., HEAD_DIM : 2 * HEAD_DIM].astype(F32), cosine, sine).astype(BF)
     values = qkv[..., 2 * HEAD_DIM :]
@@ -1081,31 +1253,22 @@
     attended = jnp.einsum("bqk,bkd->bqd", low_probability, values, preferred_element_type=F32).astype(BF)
     attn_rows = from_bins(swap(by_token(attended), 2))
     y1, n2 = middle(mix_attn, mix_mlp, hs, attn_rows, outs)
-    dn2, y2_part, g_mlp = mlp(n2, dy2g, gus, dns, hi, 4)
-    dx2, low_grad_attn, grad_attn, mlp_sums = turn(mix_attn, mix_mlp, hs, gs, y1, dn2, outs)
+    y2_part, g_mlp, dx2, low_grad_attn, grad_attn, mlp_sums = mlp(
+        mix_attn, mix_mlp, n2, dy2g, gus, dns, hs, gs, outs, y1, 4
+    )
 
     def own_rows(x):
         x = x.astype(F32).transpose(1, 2, 0, 3)
         return sum_hi(x.reshape(hi, rows, -1)).reshape(rows, GROUP, -1)
 
+    code = segment * CODE + position
+    tables = (jnp.concatenate([cosine, sine], -1), code[:, :, None], code[:, None, :])
+    attn_cols = attn_rows.reshape(tokens, 2, hi, GROUP, rows).swapaxes(2, 3).reshape(tokens, width)
+    dn1, y2, g_out, g_qkv, g_mlp = back(
+        to_bins(grad_attn), raw_qkv.reshape(GROUP, tokens, -1), qkvs, low_grad_attn, attn_cols, tables,
+        n1g, y2_part, g_mlp, hi, 7,
+    )
     g_mlp = own_rows(g_mlp)
-    d_out = by_bin(swap(to_bins(grad_attn), 6))
-    grad_values = jnp.einsum("bqk,bqd->bkd", low_probability, d_out, preferred_element_type=F32)
-    grad_probs = jnp.einsum("bqd,bkd->bqk", d_out, values, preferred_element_type=F32)
-    shared = jnp.sum(grad_probs * probability, -1, keepdims=True)
-    grad_scores = (probability * (grad_probs - shared)).astype(BF)
-    grad_query = jnp.einsum("bqk,bkd->bqd", grad_scores, keys, preferred_element_type=F32) * scale
-    grad_keys = jnp.einsum("bqk,bqd->bkd", grad_scores, queries, preferred_element_type=F32) * scale
-    grad_qkv = by_token(
-        jnp.concatenate(
-            [rotate(grad_query, cosine, -sine), rotate(grad_keys, cosine, -sine), grad_values], axis=-1
-        ).astype(BF)
-    ).reshape(GROUP * tokens, 3 * HEAD_DIM)
-    dn1_part = dot_t(grad_qkv, qkvs).astype(BF).reshape(GROUP, tokens, width)
-    g_qkv = t_dot(n1g, grad_qkv).astype(BF).reshape(2, width // 2, -1)
-    g_out = t_dot(attn_rows, low_grad_attn).astype(BF)
-    g_out = g_out.reshape(2, hi, GROUP, rows, width).swapaxes(1, 2).reshape(2, width // 2, width)
-    dn1, y2, g_out, g_qkv = back(dn1_part, y2_part, g_out, g_qkv, hi, 7)
     g_out = sum_hi(g_out.reshape(hi, rows, width))
     g_qkv = own_rows(g_qkv)
     new_streams, d_streams, sums = close(

time: 935 us -> 858 us (0.918)
  Pallas kernels: 824 us -> 785 us
  matrix products: 46 us -> 13 us
    dot_general x7 -> x0, matrix products: 31.4 us -> none  [the longest x2 14.8 us: t_dot(): return lax.dot_general(a, b, CONTRACT_FIRST, preferred_element_type=F32)]
    pallas_call x2 -> x1, Pallas kernels: 43.6 us -> 20.2 us  [swap(): pl.pallas_call(swap_kernel, out_shape=jax.ShapeDtypeStruct(shape, x.dtype...]
    pallas_call x3 -> x2, Pallas kernels: 471 us -> 454 us  [the longest x1 253 us: back(): pl.pallas_call(back_kernel, out_shape=(jax.ShapeDtypeStruct((tokens, widt...]
    another operation x2 -> x0, other arithmetic: 11.4 us -> none
    unnamed x61 -> x41, local copies, waits for them, and re-layouts: 22.4 us -> 21.2 us
where the time goes in v3:
time: 858 us; the launch traced here: 849 us
  Pallas kernels  785 us (91%)
  local copies, waits for them, and re-layouts  32.4 us (4%)
  other arithmetic  17.3 us (2%)
  matrix products  13 us (2%)
    pallas_call x1, Pallas kernels, back(): pl.pallas_call(back_kernel, out_shape=(jax.ShapeDtypeStruct((tokens, widt...  253 us
    pallas_call x1, Pallas kernels, front(): pl.pallas_call(front_kernel, out_shape=(shape(GROUP, *n1.shape), shape(GR...  250 us
    pallas_call x1, Pallas kernels, mlp(): pl.pallas_call(mlp_kernel, out_shape=(jax.ShapeDtypeStruct((*blocks, widt...  201 us
    pallas_call x1, Pallas kernels, close(): pl.pallas_call(close_kernel, out_shape=(jax.ShapeDtypeStruct((tokens, str...  32.8 us
    unnamed x41, local copies, waits for them, and re-layouts  21.2 us
    pallas_call x1, Pallas kernels, swap(): pl.pallas_call(swap_kernel, out_shape=jax.ShapeDtypeStruct(shape, x.dtype...  20.2 us
    pallas_call x1, Pallas kernels, open_streams(): pl.pallas_call(open_kernel, out_shape=(jax.ShapeDtypeStruct((streams, tok...  18.5 us

profile of v3, /device:TPU:0, one launch (start us, length us, event | category | flops | bytes accessed | tf_op | source)
XLA Modules:
  0.0 848.9 jit_solution(8031322203972137074)
XLA Ops:
  2.8 1.3 fusion.32.sorter
  4.1 18.5 %shard_map.161 = (bf16[4,128,2048]{2,1,0:T(8,128)(2,1)}, bf16[4,128,2048]{2,1,0:T(8,128)(2,1)}, bf16[128,2048]{1,0:T(8,128)(2,1)}, bf16[128,2048]{1,0:T(8,128)(2,1)}) custom-call(f32[4,6]{1,0:T(4,128)} %mixa.7, f32[4,6]{1,0:T(4,128)} %mixm.7, bf16[128,128]{1,0:T(8,128)(2,1)} %fusion.32.sorter, bf16[128,4,2048]{2,1,0:T(4,128)(2,1)} %x.1, bf16[128,4,2048]{2,1,0:T(4,128)(2,1)} %g.1), custom_call_target="tpu_custom_call" | custom-call | tf_op jit(solution)/shard_map/pallas_call | solution.py:955
  22.6 1.1 copy-done.6
  23.8 1.0 copy-done.7
  24.8 1.0 copy-done.8
  25.9 250.4 %shard_map.162 = (bf16[16,128,2048]{2,1,0:T(8,128)(2,1)S(1)}, bf16[16,128,2048]{2,1,0:T(8,128)(2,1)S(1)}, bf16[2,1,16,64,384]{4,3,2,1,0:T(8,128)(2,1)S(1)}, bf16...) custom-call(bf16[128,2048]{1,0:T(8,128)(2,1)S(1)} %copy-done.7, ...), custom_call_target="tpu_custom_call" | custom-call | tf_op jit(solution)/shard_map/pallas_call | solution.py:338
  276.3 3.2 copy-done.10
  279.5 4.5 convolution_convert_fusion
  284.0 1.2 copy-done.1
  285.8 1.5 copy-done.11
  288.2 5.6 multiply_cosine_fusion
  293.8 1.3 pad_maximum_fusion.1.rope
  295.1 3.7 fusion.50
  298.7 4.8 fusion.17
  303.5 1.1 copy.66
  304.6 20.2 %shard_map.163.attn = bf16[128,2048]{1,0:T(8,128)(2,1)S(1)} custom-call(bf16[16,128,128]{2,1,0:T(8,128)(2,1)S(1)} %bitcast.49), custom_call_target="tpu_custom_call" | custom-call | tf_op jit(solution)/shard_map/pallas_call | solution.py:393
  325.7 9.1 %shard_map.164 = (f32[128,2048]{1,0:T(8,128)}, bf16[128,2048]{1,0:T(8,128)(2,1)}) custom-call(f32[4,6]{1,0:T(4,128)} %mixa.7, f32[4,6]{1,0:T(4,128)} %mixm.7, bf16[4,128,2048]{2,1,0:T(8,128)(2,1)} %get-tuple-element.34.hs, bf16[128,2048]{1,0:T(8,128)(2,1)} %copy-done.2, bf16[2048,2048]{1,0:T(8,128)(2,1)} %bitcast.45), custom_call_target="tpu_custom_call" | custom-call | tf_op jit(solution)/shard_map/pallas_call | solution.py:990
  334.8 201.0 %shard_map.165 = (bf16[16,128,2048]{2,1,0:T(8,128)(2,1)}, bf16[1024,1536]{1,0:T(8,128)(2,1)}, f32[128,2048]{1,0:T(8,128)}, bf16[128,2048]{1,0:T(8,128)(2,1)}, bf...) custom-call(f32[4,6]{1,0:T(4,128)} %mixa.7, f32[4,6]{1,0:T(4,128)} %mixm.7, bf16[128,2048]{1,0:T(8,128)(2,1)} %get-tuple-element.41.n2, ...), custom_call_target="tpu_custom_call" | custom-call | flops 38654705664 | bytes 62914560 | tf_op jit(solution)/shard_map/pallas_call | solution.py:608
  536.5 1.2 fusion.19.code_row
  538.4 252.9 %shard_map.166 = (f32[128,2048]{1,0:T(8,128)}, f32[128,2048]{1,0:T(8,128)}, f32[64,2048]{1,0:T(8,128)}, bf16[16,1,64,384]{3,2,1,0:T(8,128)(2,1)}, bf16[16,1,64,1536]{3,2,1,0:T(8,128)(2,1)}) custom-call(bf16[128,2048]{1,0:T(8,128)(2,1)} %get-tuple-element.47.d_rows, bf16[16,128,384]{2,1,0:T(8,128)(2,1)} %bitcast.60, bf16[2048,384]{1,0:T(8,128)(2,1)} %bitcast.51, ...), custom_call_target="tpu_custom_call" | custom-call | tf_op jit(solution)/shard_map/pallas_call | solution.py:840
  791.3 2.7 convert_bitcast_fusion
  794.0 1.1 slice_bitcast_fusion
  795.6 2.3 pad_maximum_fusion
  797.9 1.5 copy.78
  799.4 32.8 %shard_map.167 = (f32[128,4,2048]{2,1,0:T(4,128)}, f32[128,4,2048]{2,1,0:T(4,128)}, f32[48,128]{1,0:T(8,128)}) custom-call(f32[4,6]{1,0:T(4,128)} %mixa.7, f32[4,6]{1,0:T(4,128)} %mixm.7, bf16[128,128]{1,0:T(8,128)(2,1)} %fusion.32.sorter, bf16[4,128,2048]{2,1,0:T(8,128)(2,1)} %get-tuple-element.34.hs, bf16[4,128,2048]{2,1,0:T(8,128)(2,1)} %get-tuple-element.35.gs, ...), custom_call_target="tpu_custom_call" | custom-call | tf_op jit(solution)/shard_map/pallas_call | solution.py:1109
  834.6 2.1 copy.70
  836.7 2.5 reshape.252
  839.3 1.6 copy.81
  840.9 1.0 copy-done.15
  841.9 2.1 copy.85
  844.1 1.6 copy-done.14
  845.6 2.0 copy.86
  (52 shorter events, 9.6 us)
Async XLA Ops:
  0.6 22.0 %copy-start.3 = (bf16[64,16384]{1,0:T(8,128)(2,1)S(1)}, bf16[64,16384]{1,0:T(8,128)(2,1)}, u32[]{:S(2)}) copy-start(bf16[64,16384]{1,0:T(8,128)(2,1)} %param.18) | copy-start | bytes 6291460
  0.6 22.0 %copy-start.5 = (bf16[64,8192]{1,0:T(8,128)(2,1)S(1)}, bf16[64,8192]{1,0:T(8,128)(2,1)}, u32[]{:S(2)}) copy-start(bf16[64,8192]{1,0:T(8,128)(2,1)} %param.19) | copy-start | bytes 3145732
  0.7 22.0 %copy-start.9 = (bf16[64,2048]{1,0:T(8,128)(2,1)S(1)}, bf16[64,2048]{1,0:T(8,128)(2,1)}, u32[]{:S(2)}) copy-start(bf16[64,2048]{1,0:T(8,128)(2,1)} %wout.1) | copy-start | bytes 786436
  22.6 1.1 copy-start.6
  23.8 1.0 copy-start.7
  24.8 1.0 copy-start.8
  276.3 3.2 copy-start.10
  279.5 4.6 copy-start
  279.5 5.7 copy-start.1
  279.5 6.3 copy-start.4
  279.5 7.8 copy-start.11
  279.5 8.3 copy-start.12
  287.8 5.9 copy-start.13
  324.9 0.8 copy-start.2
  799.4 35.0 %copy-start.16 = (bf16[16,1,64,384]{3,2,1,0:T(8,128)(2,1)S(1)}, bf16[16,1,64,384]{3,2,1,0:T(8,128)(2,1)}, u32[]{:S(2)}) copy-start(bf16[16,1,64,384]{3,2,1,0:T(8,128)(2,1)} %get-tuple-element.57) | copy-start | bytes 2359300
  839.2 2.8 copy-start.15
  841.9 3.7 copy-start.14
  845.6 2.0 copy-start.17

commit v4 on v3

--- a/solution.py
+++ b/solution.py
@@ -11,6 +11,7 @@
 HEADS = 16
 HEAD_DIM = 128
 GROUP = 16
+CUBE = 8
 EPSILON = 1e-05
 MESH = pl.DeviceIdType.MESH
 CONTRACT_LAST = (((1,), (1,)), ((), ()))
@@ -68,7 +69,12 @@
     def __init__(self, here, x, out, send, recv):
         self.here, self.x, self.out, self.send, self.recv = here, x, out, send, recv
         self.half = x.shape[0] // 2
+        self.off = here.lo - here.lo % out.shape[0]
+        self.far = (1, 3, 2) if out.shape[0] == GROUP else (1,)
         self.sent = []
+
+    def block(self, mask):
+        return self.here.flip(mask) - self.off
 
     def _go(self, block, part, j, slot, mask):
         ref = self.out.at[block, pl.ds(part * self.half, self.half)]
@@ -81,17 +87,17 @@
         rcopy(ref, ref, self.send.at[j, slot], self.recv.at[j, slot], self.here.dev(1)).wait_recv()
 
     def begin(self, own_sem):
-        own = pltpu.make_async_copy(self.x, self.out.at[self.here.lo], own_sem)
+        own = pltpu.make_async_copy(self.x, self.out.at[self.block(0)], own_sem)
         own.start()
-        for j in (1, 3, 2):
-            c = rcopy(self.x, self.out.at[self.here.lo], self.send.at[j, 6], self.recv.at[j, 6], self.here.dev(4 * j))
+        for j in self.far:
+            c = rcopy(self.x, self.out.at[self.block(0)], self.send.at[j, 6], self.recv.at[j, 6], self.here.dev(4 * j))
             c.start()
             self.sent.append(c)
         own.wait()
         self.spread(0)
 
     def spread(self, j):
-        b = self.here.flip(4 * j)
+        b = self.block(4 * j)
         if j:
             ref = self.out.at[b]
             rcopy(ref, ref, self.send.at[j, 6], self.recv.at[j, 6], self.here.dev(4)).wait_recv()
@@ -102,23 +108,21 @@
 
     def forward(self, j):
         m = 4 * j
-        self._wait(j, 0, self.here.flip(m ^ 1), 0)
-        self._go(self.here.flip(m ^ 1), 0, j, 4, 2)
-        self._wait(j, 1, self.here.flip(m ^ 2), 1)
-        self._go(self.here.flip(m ^ 2), 1, j, 5, 1)
+        self._wait(j, 0, self.block(m ^ 1), 0)
+        self._go(self.block(m ^ 1), 0, j, 4, 2)
+        self._wait(j, 1, self.block(m ^ 2), 1)
+        self._go(self.block(m ^ 2), 1, j, 5, 1)
 
     def settle(self, j):
         m = 4 * j
-        self._wait(j, 2, self.here.flip(m ^ 2), 0)
-        self._wait(j, 3, self.here.flip(m ^ 1), 1)
-        self._wait(j, 4, self.here.flip(m ^ 3), 0)
-        self._wait(j, 5, self.here.flip(m ^ 3), 1)
+        self._wait(j, 2, self.block(m ^ 2), 0)
+        self._wait(j, 3, self.block(m ^ 1), 1)
+        self._wait(j, 4, self.block(m ^ 3), 0)
+        self._wait(j, 5, self.block(m ^ 3), 1)
 
     def end(self):
         for c in self.sent:
             c.wait_send()
-
-    ORDER = (0, 1, 3, 2)
 
 
 def rowwise(n, step, body):
@@ -133,12 +137,13 @@
     sems = (4, 7)
 
     @staticmethod
-    def scratch(rows, d):
+    def scratch(rows, d, span=GROUP):
         h = rows // 2
+        zs = span // 4
         return [
-            pltpu.VMEM((4, 4, h, d), BF),
-            pltpu.VMEM((4, 2, h, d), BF),
-            pltpu.VMEM((3, rows, d), BF),
+            pltpu.VMEM((zs, 4, h, d), BF),
+            pltpu.VMEM((zs, 2, h, d), BF),
+            pltpu.VMEM((zs - 1, rows, d), BF),
             pltpu.SemaphoreType.DMA(Scatter.sems),
             pltpu.SemaphoreType.DMA(Scatter.sems),
         ]
@@ -147,6 +152,8 @@
         self.here, self.part = here, part
         self.first, self.second, self.zin, self.send, self.recv = scratch
         self.rows = part.shape[1]
+        self.off = here.lo - here.lo % part.shape[0]
+        self.far = tuple(range(1, part.shape[0] // 4))
         self.half = self.rows // 2
         self.sent = []
 
@@ -159,7 +166,7 @@
         self.sent.append(c)
 
     def _piece(self, mask, part):
-        return self.part.at[self.here.flip(mask), pl.ds(part * self.half, self.half)]
+        return self.part.at[self.here.flip(mask) - self.off, pl.ds(part * self.half, self.half)]
 
     def start(self, j):
         m = 4 * j
@@ -188,7 +195,7 @@
             self._copy(j, slot, self.first.at[j, slot], self.first.at[j, slot], 1).wait_recv()
             self._copy(j, 4 + part, self.second.at[j, part], self.second.at[j, part], 1).wait_recv()
         if out is not None:
-            for k in (1, 2, 3):
+            for k in self.far:
                 self._copy(k, 6, self.zin.at[k - 1], self.zin.at[k - 1], 4).wait_recv()
         for part, slot in ((0, 0), (1, 2)):
             own = self._piece(m, part)
@@ -199,42 +206,18 @@
                 if out is None:
                     own[r] = total.astype(BF)
                 else:
-                    for k in (1, 2, 3):
+                    for k in self.far:
                         total = total + self.zin[k - 1, at].astype(F32)
                     out[at] = total.astype(out.dtype)
 
             rowwise(h, 16, body)
         if out is None:
-            self._go(j, 6, self.part.at[self.here.flip(m)], self.zin.at[j - 1], m)
+            self._go(j, 6, self.part.at[self.here.flip(m) - self.off], self.zin.at[j - 1], m)
 
     def end(self):
         for c in self.sent:
             c.wait_send()
 
-    ORDER = (2, 3, 1, 0)
-
-
-def run_scatters(scatters, outs):
-    for i, (s, out) in enumerate(zip(scatters, outs)):
-        order = s.ORDER
-        if i == 0:
-            s.start(order[0])
-        s.start(order[1])
-        s.cross(order[0])
-        s.start(order[2])
-        s.cross(order[1])
-        s.finish(order[0])
-        s.start(order[3])
-        s.cross(order[2])
-        s.finish(order[1])
-        if i + 1 < len(scatters):
-            scatters[i + 1].start(order[0])
-        s.cross(order[3])
-        s.finish(order[2])
-        s.finish(order[3], out)
-    for s in scatters:
-        s.end()
-
 
 def any_spec(n):
     return [pl.BlockSpec(memory_space=pl.ANY)] * n
@@ -248,13 +231,13 @@
     return pltpu.CompilerParams(collective_id=cid, has_side_effects=True, vmem_limit_bytes=mib * MIB)
 
 
-def exchange_columns(here, src, dst, width, cols, send, recv, own_sem):
+def exchange_columns(here, src, dst, width, cols, span, send, recv, own_sem):
     copies = []
     own = []
     for i, c in enumerate(cols):
         for m in range(GROUP):
             peer = here.flip(m)
-            at = src.at[:, :, pl.ds(pl.multiple_of(c + peer * width, 128), width)]
+            at = src.at[:, :, pl.ds(pl.multiple_of(c + (peer % span) * width, 128), width)]
             to = dst.at[here.rep, :, here.lo, :, pl.ds(i * width, width)]
             if m == 0:
                 cp = pltpu.make_async_copy(at, to, own_sem.at[i])
@@ -280,74 +263,167 @@
     return arrive, end
 
 
+def rope_parts(rope):
+    other = pltpu.roll(rope, HEAD_DIM // 2, 1)
+    first = lax.broadcasted_iota(jnp.int32, rope.shape, 1) < HEAD_DIM // 2
+    return jnp.where(first, rope, other), jnp.where(first, -other, rope)
+
+
+def turned(x, cosine, sine):
+    return x * cosine + pltpu.roll(x, HEAD_DIM // 2, 1) * sine
+
+
+CODE = 4096
+
+
+def head_of_bin(qkv, tables, b):
+    rope, code_row, code_col = tables
+    slots = qkv.shape[1] // rope.shape[0]
+    rows = pl.ds(b * slots, slots)
+    n = GROUP * slots
+
+    def piece(i):
+        return qkv[:, rows, i * HEAD_DIM : (i + 1) * HEAD_DIM].reshape(n, HEAD_DIM)
+
+    cos, sin = rope_parts(rope[b])
+    queries = turned(piece(0).astype(F32), cos, sin).astype(BF)
+    keys = turned(piece(1).astype(F32), cos, sin).astype(BF)
+    query_code, key_code = code_row[b], code_col[b]
+    segment_code = query_code - jnp.bitwise_and(query_code, CODE - 1)
+    seen = (key_code <= query_code) & (key_code >= segment_code)
+    scores = jnp.where(seen, dot_t(queries, keys) * (1.0 / math.sqrt(HEAD_DIM)), -1e30)
+    weights = jnp.exp(scores - jnp.max(scores, -1, keepdims=True))
+    probability = weights / jnp.sum(weights, -1, keepdims=True)
+    return queries, keys, piece(2), probability, rows, cos, sin
+
+
+def attend(qkv, out, tables, b):
+    _, _, values, probability, rows, _, _ = head_of_bin(qkv, tables, b)
+    attended = dot(probability.astype(BF), values).astype(BF)
+    out[:, rows] = attended.reshape(GROUP, rows.size, HEAD_DIM)
+
+
 def front_kernel(
-    n1, dy2, wqkv, wout, wgu, wdn,
-    n1g, dy2g, qkvs, outs, gus, dns,
-    gsend, grecv, own, csend, crecv, cown, psend, precv,
+    n1, rope, code_row, code_col, dy2, wqkv, wout, wgu, wdn,
+    raw, n1g_out, dy2g, qkvs, outs, gus, dns, attn,
+    n1g, wq, attended,
+    gsend, grecv, own, csend, crecv, cown, psend, precv, late, group_out, ssend, srecv, sown,
 ):
     here = Here()
     barrier(here, ALL, True)
-    q = exchange_columns(here, wqkv, qkvs, 128, (0, 2048, 4096), csend.at[0], crecv.at[0], cown.at[0])
+    tables = (rope, code_row, code_col)
+    tokens, width = n1.shape
+    q = exchange_columns(here, wqkv, qkvs, 128, (0, 2048, 4096), GROUP, csend.at[0], crecv.at[0], cown.at[0])
     half = wgu.shape[2] // 2
     ga = Gather(here, n1, n1g, gsend.at[0], grecv.at[0])
     gb = Gather(here, dy2, dy2g, gsend.at[1], grecv.at[1])
     gc = Gather(here, wout, outs.at[here.rep], gsend.at[2], grecv.at[2])
-    ga.begin(own.at[0])
-    u = exchange_columns(here, wgu, gus, half // GROUP, (0, half), csend.at[1], crecv.at[1], cown.at[1])
-    d = exchange_columns(here, wdn, dns, half // GROUP, (0,), csend.at[2], crecv.at[2], cown.at[2])
-    gathers = [ga, gb, gc]
-    for i, g in enumerate(gathers):
-        order = g.ORDER
-        g.spread(order[1])
-        g.forward(order[0])
-        g.spread(order[2])
-        g.forward(order[1])
-        g.spread(order[3])
-        g.forward(order[2])
-        if i + 1 < len(gathers):
-            gathers[i + 1].begin(own.at[i + 1])
-        g.forward(order[3])
-    passes = []
-    for i, ((arrive, _), dst) in enumerate(zip((q, u, d), (qkvs, gus, dns))):
-        arrive()
+    o = (0, 1, 3, 2)
+
+    def hand_over(i, dst):
         cp = rcopy(dst.at[here.rep], dst.at[here.rep], psend.at[i], precv.at[i], here.partner())
         cp.start()
-        passes.append((cp, dst))
-    for g in gathers:
-        for j in range(4):
-            g.settle(j)
-    cp = rcopy(outs.at[here.rep], outs.at[here.rep], psend.at[3], precv.at[3], here.partner())
-    cp.start()
-    passes.append((cp, outs))
-    for i, (cp, dst) in enumerate(passes):
-        cp.wait_send()
+        return cp
+
+    def other_core(i, dst):
         other = dst.at[1 - here.rep]
         rcopy(other, other, psend.at[i], precv.at[i], here.partner()).wait_recv()
-    for g in gathers:
+
+    ga.begin(own.at[0])
+    ga.spread(o[1])
+    ga.forward(o[0])
+    q[0]()
+    q_pass = hand_over(0, qkvs)
+    ga.spread(o[2])
+    ga.forward(o[1])
+    ga.spread(o[3])
+    ga.forward(o[2])
+    gc.begin(own.at[2])
+    u = exchange_columns(here, wgu, gus, half // CUBE, (0, half), CUBE, csend.at[1], crecv.at[1], cown.at[1])
+    d = exchange_columns(here, wdn, dns, half // CUBE, (0,), CUBE, csend.at[2], crecv.at[2], cown.at[2])
+    ga.forward(o[3])
+    other_core(0, qkvs)
+    get = pltpu.make_async_copy(qkvs, wq, late)
+    get.start()
+    get.wait()
+    copies = []
+    for k, j in enumerate(o):
+        ga.settle(j)
+        blocks = pl.ds(here.flip(4 * j) - here.lo % 4, 4)
+        x = n1g[blocks].reshape(4 * tokens, width)
+        raw[blocks] = dot(x, wq[...].reshape(width, wq.shape[-1])).astype(BF).reshape(4, tokens, wq.shape[-1])
+        c = pltpu.make_async_copy(n1g.at[blocks], n1g_out.at[blocks], group_out.at[k])
+        c.start()
+        copies.append(c)
+    bins = rope.shape[0]
+    for b in range(bins):
+        attend(raw, attended, tables, b)
+        if b < 3:
+            gc.spread(o[b + 1])
+            gc.forward(o[b])
+    swaps = []
+    at = pl.ds(pl.multiple_of(here.lo * HEAD_DIM, HEAD_DIM), HEAD_DIM)
+    for m in ALL:
+        c = rcopy(attended.at[here.flip(m)], attn.at[:, at], ssend.at[m], srecv.at[m], here.dev(m))
+        c.start()
+        swaps.append(c)
+    mine = pltpu.make_async_copy(attended.at[here.lo], attn.at[:, at], sown)
+    mine.start()
+    gb.begin(own.at[1])
+    gc.forward(o[3])
+    gb.spread(1)
+    gb.forward(0)
+    for j in o:
+        gc.settle(j)
+    out_pass = hand_over(3, outs)
+    gb.forward(1)
+    u[0]()
+    u_pass = hand_over(1, gus)
+    d[0]()
+    d_pass = hand_over(2, dns)
+    gb.settle(0)
+    gb.settle(1)
+    mine.wait()
+    for m in ALL:
+        ref = attn.at[:, pl.ds(pl.multiple_of(here.flip(m) * HEAD_DIM, HEAD_DIM), HEAD_DIM)]
+        rcopy(ref, ref, ssend.at[m], srecv.at[m], here.dev(m)).wait_recv()
+    for i, dst in ((1, gus), (2, dns), (3, outs)):
+        other_core(i, dst)
+    for c in (q_pass, u_pass, d_pass, out_pass, *swaps):
+        c.wait_send()
+    for c in copies:
+        c.wait()
+    for g in (ga, gb, gc):
         g.end()
     for _, end in (q, u, d):
         end()
 
 
-def front(n1, dy2, wqkv, wout, wgu, wdn, cid):
+def front(n1, tables, dy2, wqkv, wout, wgu, wdn, cid):
     hi, rows, _ = wqkv.shape
-    d = n1.shape[1]
     ff = wdn.shape[2]
+    tokens = n1.shape[0]
     shape = lambda *s: jax.ShapeDtypeStruct(s, BF)
     out_rows = wout.shape[0]
+    head = 3 * HEAD_DIM
     return pl.pallas_call(
         front_kernel,
         out_shape=(
+            shape(GROUP, tokens, head),
             shape(GROUP, *n1.shape),
-            shape(GROUP, *dy2.shape),
-            shape(2, hi, GROUP, rows, 3 * HEAD_DIM),
+            shape(CUBE, *dy2.shape),
+            shape(2, hi, GROUP, rows, head),
             shape(2, GROUP, out_rows, wout.shape[1]),
-            shape(2, hi, GROUP, rows, 2 * ff // GROUP),
-            shape(2, hi, GROUP, rows, ff // GROUP),
+            shape(2, hi, GROUP, rows, 2 * ff // CUBE),
+            shape(2, hi, GROUP, rows, ff // CUBE),
+            shape(tokens, GROUP * HEAD_DIM),
         ),
-        in_specs=any_spec(6),
-        out_specs=any_spec(6),
+        in_specs=[*vmem_spec(4), *any_spec(5)],
+        out_specs=(*vmem_spec(1), *any_spec(7)),
         scratch_shapes=[
+            pltpu.VMEM((GROUP, *n1.shape), BF),
+            pltpu.VMEM((2, hi, GROUP, rows, head), BF),
+            pltpu.VMEM((GROUP, tokens, HEAD_DIM), BF),
             pltpu.SemaphoreType.DMA((3,) + Gather.sems),
             pltpu.SemaphoreType.DMA((3,) + Gather.sems),
             pltpu.SemaphoreType.DMA((3,)),
@@ -356,52 +432,14 @@
             pltpu.SemaphoreType.DMA((3, 3)),
             pltpu.SemaphoreType.DMA((4,)),
             pltpu.SemaphoreType.DMA((4,)),
-        ],
-        compiler_params=params(cid, 16),
-    )(n1, dy2, wqkv, wout, wgu, wdn)
-
-
-def swap_kernel(x, out, send, recv, own):
-    here = Here()
-    barrier(here, ALL, False)
-
-    def block(ref, l):
-        if len(ref.shape) == 3:
-            return ref.at[l]
-        return ref.at[:, pl.ds(pl.multiple_of(l * HEAD_DIM, HEAD_DIM), HEAD_DIM)]
-
-    cps = []
-    for m in ALL:
-        c = rcopy(block(x, here.flip(m)), block(out, here.lo), send.at[m], recv.at[m], here.dev(m))
-        c.start()
-        cps.append(c)
-    c = pltpu.make_async_copy(block(x, here.lo), block(out, here.lo), own)
-    c.start()
-    c.wait()
-    for m in ALL:
-        ref = block(out, here.flip(m))
-        rcopy(ref, ref, send.at[m], recv.at[m], here.dev(m)).wait_recv()
-    for c in cps:
-        c.wait_send()
-
-
-def swap(x, cid):
-    if x.ndim == 3:
-        shape = (x.shape[1], GROUP * HEAD_DIM)
-    else:
-        shape = (GROUP, x.shape[0], HEAD_DIM)
-    return pl.pallas_call(
-        swap_kernel,
-        out_shape=jax.ShapeDtypeStruct(shape, x.dtype),
-        in_specs=any_spec(1),
-        out_specs=pl.BlockSpec(memory_space=pl.ANY),
-        scratch_shapes=[
+            pltpu.SemaphoreType.DMA,
+            pltpu.SemaphoreType.DMA((4,)),
             pltpu.SemaphoreType.DMA((GROUP,)),
             pltpu.SemaphoreType.DMA((GROUP,)),
             pltpu.SemaphoreType.DMA,
         ],
-        compiler_params=params(cid, 16),
-    )(x)
+        compiler_params=params(cid, 40),
+    )(n1, *tables, dy2, wqkv, wout, wgu, wdn)
 
 
 def pair_add(here, g, inbox, send, recv):
@@ -460,7 +498,7 @@
     gsend, grecv, own, load, y2sem, psend, precv, late, *scratch,
 ):
     here = Here()
-    barrier(here, TREE, True)
+    barrier(here, (1, 2, 4), True)
     g = Gather(here, n2, n2g, gsend, grecv)
     rs = Scatter(here, part, scratch)
     g.begin(own)
@@ -476,7 +514,7 @@
     y2copies = []
 
     def compute(j):
-        first = here.flip(4 * j) - here.lo % 4
+        first = here.flip(4 * j) - here.lo % 4 - g.off
         blocks = pl.ds(first, 4)
         if not y2copies:
             for c in loads:
@@ -521,40 +559,25 @@
     def weight_grads(which, k):
         cols = pl.ds(pl.multiple_of(which * half + k * step, step), step)
         rows = pl.ds(pl.multiple_of(k * step, step), step)
-        x = n2g[:, :, cols].reshape(GROUP * tokens, step)
-        grads[which, rows, : 2 * ff] = t_dot(x, dgu[...].reshape(GROUP * tokens, 2 * ff)).astype(BF)
-        x = dy2g[:, :, cols].reshape(GROUP * tokens, step)
-        grads[which, rows, 2 * ff :] = t_dot(x, hidden[...].reshape(GROUP * tokens, ff)).astype(BF)
+        x = n2g[:, :, cols].reshape(CUBE * tokens, step)
+        grads[which, rows, : 2 * ff] = t_dot(x, dgu[...].reshape(CUBE * tokens, 2 * ff)).astype(BF)
+        x = dy2g[:, :, cols].reshape(CUBE * tokens, step)
+        grads[which, rows, 2 * ff :] = t_dot(x, hidden[...].reshape(CUBE * tokens, ff)).astype(BF)
 
     def pass_chunk(k):
         rows = pl.ds(pl.multiple_of(k * step, step), step)
         return rcopy(grads.at[1 - here.rep, rows], inbox.at[rows], psend.at[k], precv.at[k], here.partner())
 
-    o = g.ORDER
-    g.spread(o[1])
-    g.forward(o[0])
-    g.settle(o[0])
-    compute(o[0])
-    rs.start(o[0])
-    g.spread(o[2])
-    g.forward(o[1])
-    g.settle(o[1])
-    compute(o[1])
-    rs.start(o[1])
-    g.spread(o[3])
-    g.forward(o[2])
-    rs.cross(o[0])
-    g.settle(o[2])
-    compute(o[2])
-    rs.start(o[2])
-    g.forward(o[3])
-    rs.cross(o[1])
-    g.settle(o[3])
-    rs.finish(o[1])
-    compute(o[3])
-    rs.start(o[3])
-    rs.cross(o[2])
-    rs.finish(o[2])
+    g.spread(1)
+    g.forward(0)
+    g.settle(0)
+    compute(0)
+    rs.start(0)
+    g.forward(1)
+    rs.cross(0)
+    g.settle(1)
+    compute(1)
+    rs.start(1)
 
     def other_half(k, carry):
         weight_grads(1 - here.rep, k)
@@ -562,8 +585,8 @@
         return carry
 
     lax.fori_loop(0, chunks, other_half, 0)
-    rs.cross(o[3])
-    rs.finish(o[3])
+    rs.cross(1)
+    rs.finish(1)
 
     def own_half(k, carry):
         weight_grads(here.rep, k)
@@ -573,7 +596,7 @@
     g.end()
     streams = hs.shape[0]
     loads = []
-    for i, (src, dst) in enumerate(((hs, n2g.at[:streams]), (gs, n2g.at[streams : 2 * streams]), (wout, dy2g))):
+    for i, (src, dst) in enumerate(((hs, n2g.at[:streams]), (gs, n2g.at[streams : 2 * streams]), (wout, wgu))):
         c = pltpu.make_async_copy(src, dst, late.at[i])
         c.start()
         loads.append(c)
@@ -594,7 +617,7 @@
     rs.finish(0, dn2)
     for c in loads:
         c.wait()
-    turn(read_mix(mixa), read_mix(mixm), n2g, y1, dn2, dy2g, dx2, dy1, d_out, sums)
+    turn(read_mix(mixa), read_mix(mixm), n2g, y1, dn2, wgu, dx2, dy1, d_out, sums)
     out.wait()
     y2copies[-1].wait()
     rs.end()
@@ -604,7 +627,7 @@
     tokens, width = n2.shape
     ff = wdn.shape[1]
     half = width // 2
-    blocks = (GROUP, tokens)
+    blocks = (CUBE, tokens)
     return pl.pallas_call(
         mlp_kernel,
         out_shape=(
@@ -637,47 +660,13 @@
             pltpu.SemaphoreType.DMA((half // 256,)),
             pltpu.SemaphoreType.DMA((half // 256,)),
             pltpu.SemaphoreType.DMA((4,)),
-            *Scatter.scratch(tokens, width),
+            *Scatter.scratch(tokens, width, CUBE),
         ],
         compiler_params=params(cid, 63),
         cost_estimate=pl.CostEstimate(
-            flops=2 * GROUP * tokens * width * ff * 9, bytes_accessed=60 * MIB, transcendentals=0
+            flops=2 * CUBE * tokens * width * ff * 9, bytes_accessed=60 * MIB, transcendentals=0
         ),
-    )(mixa, mixm, n2, dy2g, wgu, wdn, hs, gs, wout.reshape(GROUP, tokens, width), y1)
-
-
-def rope_parts(rope):
-    other = pltpu.roll(rope, HEAD_DIM // 2, 1)
-    first = lax.broadcasted_iota(jnp.int32, rope.shape, 1) < HEAD_DIM // 2
-    return jnp.where(first, rope, other), jnp.where(first, -other, rope)
-
-
-def turned(x, cosine, sine):
-    return x * cosine + pltpu.roll(x, HEAD_DIM // 2, 1) * sine
-
-
-CODE = 4096
-
-
-def head_of_bin(qkv, tables, b):
-    rope, code_row, code_col = tables
-    slots = qkv.shape[1] // rope.shape[0]
-    rows = pl.ds(b * slots, slots)
-    n = GROUP * slots
-
-    def piece(i):
-        return qkv[:, rows, i * HEAD_DIM : (i + 1) * HEAD_DIM].reshape(n, HEAD_DIM)
-
-    cos, sin = rope_parts(rope[b])
-    queries = turned(piece(0).astype(F32), cos, sin).astype(BF)
-    keys = turned(piece(1).astype(F32), cos, sin).astype(BF)
-    query_code, key_code = code_row[b], code_col[b]
-    segment_code = query_code - jnp.bitwise_and(query_code, CODE - 1)
-    seen = (key_code <= query_code) & (key_code >= segment_code)
-    scores = jnp.where(seen, dot_t(queries, keys) * (1.0 / math.sqrt(HEAD_DIM)), -1e30)
-    weights = jnp.exp(scores - jnp.max(scores, -1, keepdims=True))
-    probability = weights / jnp.sum(weights, -1, keepdims=True)
-    return queries, keys, piece(2), probability, rows, cos, sin
+    )(mixa, mixm, n2, dy2g, wgu, wdn, hs, gs, wout, y1)
 
 
 def attend_back(qkv, d_out, dqkv, tables, b):
@@ -722,10 +711,10 @@
     rs_y2 = Scatter(here, y2, scratch[k : 2 * k])
     rs_go = Scatter(here, gout.reshape(GROUP, gout.shape[0] // GROUP, width), scratch[2 * k : 3 * k])
     qhome, mhome = scratch[3 * k : 3 * k + 3], scratch[3 * k + 3 :]
-    order = rs_y2.ORDER
+    order = (2, 3, 1, 0)
     y2_load.wait()
-    for j in order:
-        rs_y2.start(j)
+    rs_y2.start(1)
+    rs_y2.start(0)
     end_mlp = send_home(here, gmlp, gmlp_out, *mhome)
     mine.wait()
     for m in ALL:
@@ -748,13 +737,11 @@
 
     for b in range(bins):
         attend_back(qkv, d_out, dqkv, tables, b)
-        if b == 0:
-            rs_y2.cross(order[0])
-        elif b < 3:
-            rs_y2.cross(order[b])
-            rs_y2.finish(order[b - 1])
-    rs_y2.cross(order[3])
-    rs_y2.finish(order[2])
+        if b == 1:
+            rs_y2.cross(1)
+        elif b == 2:
+            rs_y2.cross(0)
+            rs_y2.finish(1)
 
     narrow = tiles.shape[3]
 
@@ -836,7 +823,6 @@
     tokens, width = d_rows.shape
     half = width // 2
     w = qkv.shape[2]
-    blocks = (GROUP, tokens, width)
     return pl.pallas_call(
         back_kernel,
         out_shape=(
@@ -851,8 +837,8 @@
         scratch_shapes=[
             pltpu.VMEM((GROUP, tokens, HEAD_DIM), BF),
             pltpu.VMEM((GROUP, tokens, w), BF),
-            pltpu.VMEM(blocks, BF),
-            pltpu.VMEM(blocks, BF),
+            pltpu.VMEM((GROUP, tokens, width), BF),
+            pltpu.VMEM((CUBE, tokens, width), BF),
             pltpu.VMEM((half, width), BF),
             pltpu.VMEM((2, 256, width), BF),
             pltpu.VMEM((2, half, w), BF),
@@ -869,7 +855,7 @@
             pltpu.SemaphoreType.DMA,
             pltpu.SemaphoreType.DMA,
             *Scatter.scratch(tokens, width),
-            *Scatter.scratch(tokens, width),
+            *Scatter.scratch(tokens, width, CUBE),
             *Scatter.scratch(half // GROUP, width),
             *home_sems(hi),
             *home_sems(hi),
@@ -1037,12 +1023,9 @@
                     sums[j * 6 + 1 + i] += lane_sums(h1[j] * g[i])
 
     rowwise(tokens, 16, body)
-    blocks = TILE // wout.shape[1]
-
     def tile(i, carry):
         at = pl.ds(pl.multiple_of(i * TILE, TILE), TILE)
-        rows = wout[pl.ds(i * blocks, blocks)].reshape(TILE, width)
-        d_out[:, at] = dot_t(dy1[...], rows).astype(BF)
+        d_out[:, at] = dot_t(dy1[...], wout[at, :]).astype(BF)
         return carry
 
     lax.fori_loop(0, width // TILE, tile, 0)
@@ -1151,15 +1134,6 @@
     return (jnp.cos(angles), jnp.sin(angles))
 
 
-def rotate(inputs, cosine, sine_table):
-    half_width = inputs.shape[-1] // 2
-    first = inputs[..., :half_width]
-    second = inputs[..., half_width:]
-    return jnp.concatenate(
-        [first * cosine - second * sine_table, second * cosine + first * sine_table], axis=-1
-    )
-
-
 def dot(a, b):
     return jnp.dot(a, b, preferred_element_type=F32)
 
@@ -1211,47 +1185,28 @@
     hs, gs, n1, low_grad_mlp = open_streams(mix_attn, mix_mlp, sorter, streams, cotangent)
     low_attn = to_bins(n1)
 
-    n1g, dy2g, qkvs, outs, gus, dns = front(
-        low_attn, low_grad_mlp, gather_hi(w_qkv), gather_hi(w_out).reshape(-1, width), gather_hi(w_gu), gather_hi(w_down), 1
+    bins = lax.axis_index("rep") * bin_count + my_hi * my_bins
+    lengths_here = lax.dynamic_slice_in_dim(lengths, bins, my_bins, 0)
+    segment, position = slot_layout(lengths_here, capacity)
+
+    def local_order(x):
+        return x.reshape(my_bins, hi, GROUP, per_bin).swapaxes(1, 2).reshape(my_bins, capacity)
+
+    segment, position = local_order(segment), local_order(position)
+    cosine, sine = rope_tables(position, HEAD_DIM)
+    code = segment * CODE + position
+    tables = (jnp.concatenate([cosine, sine], -1), code[:, :, None], code[:, None, :])
+
+    raw_qkv, n1g, dy2g, qkvs, outs, gus, dns, attn_rows = front(
+        low_attn, tables, low_grad_mlp,
+        gather_hi(w_qkv), gather_hi(w_out).reshape(-1, width), gather_hi(w_gu), gather_hi(w_down), 1,
     )
     rows = w_qkv.shape[0]
     qkvs = qkvs.reshape(width, 3 * HEAD_DIM)
     outs = outs.reshape(2, GROUP, hi, rows, width).swapaxes(1, 2).reshape(width, width)
-    gus = gus.reshape(width, 2 * ff // GROUP)
-    dns = dns.reshape(width, ff // GROUP)
-
-    bins = lax.axis_index("rep") * bin_count + my_hi * my_bins
-    lengths_here = lax.dynamic_slice_in_dim(lengths, bins, my_bins, 0)
-    segment, position = slot_layout(lengths_here, capacity)
-
-    def local_order(x):
-        return x.reshape(my_bins, hi, GROUP, per_bin).swapaxes(1, 2).reshape(my_bins, capacity)
-
-    segment, position = local_order(segment), local_order(position)
-    cosine, sine = rope_tables(position, HEAD_DIM)
-    slots = GROUP * tokens // my_bins // GROUP
-
-    def by_bin(x):
-        return x.reshape(GROUP, my_bins, slots, -1).swapaxes(0, 1).reshape(my_bins, capacity, -1)
-
-    def by_token(x):
-        return x.reshape(my_bins, GROUP, slots, -1).swapaxes(0, 1).reshape(GROUP, tokens, -1)
-
-    scale = 1.0 / math.sqrt(HEAD_DIM)
-    raw_qkv = dot(n1g.reshape(GROUP * tokens, width), qkvs).astype(BF)
-    qkv = by_bin(raw_qkv)
-    queries = rotate(qkv[..., :HEAD_DIM].astype(F32), cosine, sine).astype(BF)
-    keys = rotate(qkv[..., HEAD_DIM : 2 * HEAD_DIM].astype(F32), cosine, sine).astype(BF)
-    values = qkv[..., 2 * HEAD_DIM :]
-    seen = (segment[:, :, None] == segment[:, None, :]) & (position[:, None, :] <= position[:, :, None])
-    scores = jnp.einsum("bqd,bkd->bqk", queries, keys, preferred_element_type=F32) * scale
-    scores = jnp.where(seen, scores, -1e30)
-    peak = jnp.max(scores, -1, keepdims=True)
-    weights = jnp.exp(scores - peak)
-    probability = weights / jnp.sum(weights, -1, keepdims=True)
-    low_probability = probability.astype(BF)
-    attended = jnp.einsum("bqk,bkd->bqd", low_probability, values, preferred_element_type=F32).astype(BF)
-    attn_rows = from_bins(swap(by_token(attended), 2))
+    gus = gus.reshape(width, 2 * ff // CUBE)
+    dns = dns.reshape(width, ff // CUBE)
+    attn_rows = from_bins(attn_rows)
     y1, n2 = middle(mix_attn, mix_mlp, hs, attn_rows, outs)
     y2_part, g_mlp, dx2, low_grad_attn, grad_attn, mlp_sums = mlp(
         mix_attn, mix_mlp, n2, dy2g, gus, dns, hs, gs, outs, y1, 4
@@ -1259,15 +1214,14 @@
 
     def own_rows(x):
         x = x.astype(F32).transpose(1, 2, 0, 3)
-        return sum_hi(x.reshape(hi, rows, -1)).reshape(rows, GROUP, -1)
-
-    code = segment * CODE + position
-    tables = (jnp.concatenate([cosine, sine], -1), code[:, :, None], code[:, None, :])
+        return sum_hi(x.reshape(hi, rows, -1)).reshape(rows, x.shape[2], -1)
+
     attn_cols = attn_rows.reshape(tokens, 2, hi, GROUP, rows).swapaxes(2, 3).reshape(tokens, width)
     dn1, y2, g_out, g_qkv, g_mlp = back(
-        to_bins(grad_attn), raw_qkv.reshape(GROUP, tokens, -1), qkvs, low_grad_attn, attn_cols, tables,
+        to_bins(grad_attn), raw_qkv, qkvs, low_grad_attn, attn_cols, tables,
         n1g, y2_part, g_mlp, hi, 7,
     )
+    g_mlp = g_mlp.astype(F32).reshape(2, CUBE, *g_mlp.shape[1:]).sum(0)
     g_mlp = own_rows(g_mlp)
     g_out = sum_hi(g_out.reshape(hi, rows, width))
     g_qkv = own_rows(g_qkv)
@@ -1278,7 +1232,7 @@
         sums = lax.psum(sums, "shard", axis_index_groups=hi_groups)
     sums = jnp.sum(sums, axis=-1).reshape(2, 4, 6)
     g_mix_attn, g_mix_mlp = sums[0], sums[1]
-    block = ff // GROUP
+    block = ff // CUBE
     return (
         new_streams,
         d_streams,

time: 858 us -> 742 us (0.86)
  Pallas kernels: 785 us -> 688 us
  matrix products: 13 us -> 0 us
    pallas_call x1, Pallas kernels: 201 us -> 130 us  [mlp(): pl.pallas_call(mlp_kernel, out_shape=(jax.ShapeDtypeStruct((*blocks, widt...]
    pallas_call x2 -> x1, Pallas kernels: 271 us -> 242 us  [front(): pl.pallas_call(front_kernel, out_shape=(shape(GROUP, tokens, head), shape...]
    dot_general x2 -> x0, matrix products: 9.32 us -> none  [the longest x1 4.8 us: shards(): jnp.einsum('bqk,bkd->bqd', low_probability, values, preferred_element_typ...]
    unnamed x41 -> x37, local copies, waits for them, and re-layouts: 21.2 us -> 17.7 us
where the time goes in v4:
time: 742 us; the launch traced here: 734 us
  Pallas kernels  688 us (93%)
  local copies, waits for them, and re-layouts  28.7 us (4%)
  other arithmetic  16.3 us (2%)
    pallas_call x1, Pallas kernels, back(): pl.pallas_call(back_kernel, out_shape=(jax.ShapeDtypeStruct((tokens, widt...  252 us
    pallas_call x1, Pallas kernels, front(): pl.pallas_call(front_kernel, out_shape=(shape(GROUP, tokens, head), shape...  242 us
    pallas_call x1, Pallas kernels, mlp(): pl.pallas_call(mlp_kernel, out_shape=(jax.ShapeDtypeStruct((*blocks, widt...  130 us
    pallas_call x1, Pallas kernels, close(): pl.pallas_call(close_kernel, out_shape=(jax.ShapeDtypeStruct((tokens, str...  35.5 us
    pallas_call x1, Pallas kernels, open_streams(): pl.pallas_call(open_kernel, out_shape=(jax.ShapeDtypeStruct((streams, tok...  18.9 us
    unnamed x37, local copies, waits for them, and re-layouts  17.7 us

profile of v4, /device:TPU:0, one launch (start us, length us, event | category | flops | bytes accessed | tf_op | source)
XLA Modules:
  0.0 734.2 jit_solution(6393304615078755961)
XLA Ops:
  0.7 0.8 constant_dynamic-slice_fusion
  1.5 0.8 fusion.6
  2.7 1.3 fusion.2.sorter
  4.3 1.4 copy.68
  5.7 1.5 fusion.1.code_row
  7.2 3.7 multiply_cosine_fusion
  11.2 18.9 %shard_map.161 = (bf16[4,128,2048]{2,1,0:T(8,128)(2,1)}, bf16[4,128,2048]{2,1,0:T(8,128)(2,1)}, bf16[128,2048]{1,0:T(8,128)(2,1)}, bf16[128,2048]{1,0:T(8,128)(2,1)}) custom-call(f32[4,6]{1,0:T(4,128)} %mixa.7, f32[4,6]{1,0:T(4,128)} %mixm.7, bf16[128,128]{1,0:T(8,128)(2,1)} %fusion.2.sorter, bf16[128,4,2048]{2,1,0:T(4,128)(2,1)} %x.1, bf16[128,4,2048]{2,1,0:T(4,128)(2,1)} %g.1), custom_call_target="tpu_custom_call" | custom-call | tf_op jit(solution)/shard_map/pallas_call | solution.py:941
  30.2 1.6 copy-done.3
  31.8 1.0 copy-done.8
  32.8 1.0 copy-done.9
  33.9 0.9 copy-done.10
  34.8 242.3 %shard_map.162 = (bf16[16,128,384]{2,1,0:T(8,128)(2,1)S(1)}, bf16[16,128,2048]{2,1,0:T(8,128)(2,1)}, bf16[8,128,2048]{2,1,0:T(8,128)(2,1)}, bf16[2,1,16,64,384]{...) custom-call(bf16[128,2048]{1,0:T(8,128)(2,1)S(1)} %copy-done.8, ...), custom_call_target="tpu_custom_call" | custom-call | tf_op jit(solution)/shard_map/pallas_call | solution.py:409
  277.1 0.8 copy-done.2
  277.9 1.1 copy-done.4
  279.0 1.1 copy-done.5
  280.2 9.1 %shard_map.163 = (f32[128,2048]{1,0:T(8,128)}, bf16[128,2048]{1,0:T(8,128)(2,1)}) custom-call(f32[4,6]{1,0:T(4,128)} %mixa.7, f32[4,6]{1,0:T(4,128)} %mixm.7, bf16[4,128,2048]{2,1,0:T(8,128)(2,1)} %get-tuple-element.36.hs, bf16[128,2048]{1,0:T(8,128)(2,1)} %copy-done.2, bf16[2048,2048]{1,0:T(8,128)(2,1)} %bitcast.43), custom_call_target="tpu_custom_call" | custom-call | tf_op jit(solution)/shard_map/pallas_call | solution.py:976
  289.3 130.3 %shard_map.164 = (bf16[8,128,2048]{2,1,0:T(8,128)(2,1)}, bf16[1024,3072]{1,0:T(8,128)(2,1)}, f32[128,2048]{1,0:T(8,128)}, bf16[128,2048]{1,0:T(8,128)(2,1)}, bf1...) custom-call(f32[4,6]{1,0:T(4,128)} %mixa.7, f32[4,6]{1,0:T(4,128)} %mixm.7, bf16[128,2048]{1,0:T(8,128)(2,1)} %get-tuple-element.42.n2, ...), custom_call_target="tpu_custom_call" | custom-call | flops 38654705664 | bytes 62914560 | tf_op jit(solution)/shard_map/pallas_call | solution.py:631
  419.6 251.7 %shard_map.165 = (f32[128,2048]{1,0:T(8,128)}, f32[128,2048]{1,0:T(8,128)}, f32[64,2048]{1,0:T(8,128)}, bf16[16,1,64,384]{3,2,1,0:T(8,128)(2,1)}, bf16[16,1,64,3072]{3,2,1,0:T(8,128)(2,1)}) custom-call(bf16[128,2048]{1,0:T(8,128)(2,1)} %get-tuple-element.48.d_rows, bf16[16,128,384]{2,1,0:T(8,128)(2,1)} %copy-done.4, bf16[2048,384]{1,0:T(8,128)(2,1)} %bitcast.38, ...), custom_call_target="tpu_custom_call" | custom-call | tf_op jit(solution)/shard_map/pallas_call | solution.py:826
  671.3 35.5 %shard_map.166 = (f32[128,4,2048]{2,1,0:T(4,128)}, f32[128,4,2048]{2,1,0:T(4,128)}, f32[48,128]{1,0:T(8,128)}) custom-call(f32[4,6]{1,0:T(4,128)} %mixa.7, f32[4,6]{1,0:T(4,128)} %mixm.7, bf16[128,128]{1,0:T(8,128)(2,1)} %fusion.2.sorter, bf16[4,128,2048]{2,1,0:T(8,128)(2,1)} %get-tuple-element.36.hs, bf16[4,128,2048]{2,1,0:T(8,128)(2,1)} %get-tuple-element.37.gs, ...), custom_call_target="tpu_custom_call" | custom-call | tf_op jit(solution)/shard_map/pallas_call | solution.py:1092
  706.9 0.8 reduce_sum.52
  707.8 0.7 squeeze.7
  709.3 2.1 copy.71
  711.3 2.8 reshape.198
  714.3 1.6 copy.81
  715.9 5.0 convert_reduce_fusion
  721.5 1.5 copy.78
  723.5 2.4 pad_maximum_fusion
  725.9 1.3 copy-done.13
  727.2 2.1 copy.85
  729.3 1.6 copy-done.12
  730.9 2.0 copy.86
  732.9 0.8 copy.87
  (41 shorter events, 3.3 us)
Async XLA Ops:
  2.6 27.5 %copy-start.11 = (s32[4,1,512]{2,1,0:T(1,128)}, s32[4,1,512]{2,1,0:T(1,128)S(1)}, u32[]{:S(2)}) copy-start(s32[4,1,512]{2,1,0:T(1,128)S(1)} %fusion.4.code_col) | copy-start | bytes 24580
  7.2 23.0 %copy-start.1 = (s32[4,512,1]{2,1,0:T(8,128)}, s32[4,512,1]{2,1,0:T(8,128)S(1)}, u32[]{:S(2)}) copy-start(s32[4,512,1]{2,1,0:T(8,128)S(1)} %fusion.1.code_row) | copy-start | bytes 24580
  11.2 18.9 %copy-start = (f32[4,512,128]{2,1,0:T(8,128)}, f32[4,512,128]{2,1,0:T(8,128)S(1)}, u32[]{:S(2)}) copy-start(f32[4,512,128]{2,1,0:T(8,128)S(1)} %pad_maximum_fusion.1.rope) | copy-start | bytes 3145732
  11.2 18.9 %copy-start.6 = (bf16[64,8192]{1,0:T(8,128)(2,1)S(1)}, bf16[64,8192]{1,0:T(8,128)(2,1)}, u32[]{:S(2)}) copy-start(bf16[64,8192]{1,0:T(8,128)(2,1)} %param.19) | copy-start | bytes 3145732
  11.2 18.9 %copy-start.7 = (bf16[64,6144]{1,0:T(8,128)(2,1)S(1)}, bf16[64,6144]{1,0:T(8,128)(2,1)}, u32[]{:S(2)}) copy-start(bf16[64,6144]{1,0:T(8,128)(2,1)} %param.16) | copy-start | bytes 2359300
  30.2 1.6 copy-start.3
  31.8 1.0 copy-start.8
  32.8 1.0 copy-start.9
  33.8 0.9 copy-start.10
  277.1 0.8 copy-start.2
  277.9 1.1 copy-start.4
  279.0 1.1 copy-start.5
  671.3 37.8 %copy-start.14 = (bf16[16,1,64,384]{3,2,1,0:T(8,128)(2,1)S(1)}, bf16[16,1,64,384]{3,2,1,0:T(8,128)(2,1)}, u32[]{:S(2)}) copy-start(bf16[16,1,64,384]{3,2,1,0:T(8,128)(2,1)} %get-tuple-element.61) | copy-start | bytes 2359300
  723.5 3.7 copy-start.13
  727.2 3.7 copy-start.12
  730.9 2.0 copy-start.15

commit v5 on v4

--- a/solution.py
+++ b/solution.py
@@ -28,6 +28,14 @@
         self.lo = shard % GROUP
         self.base = shard - self.lo
         self.bits = [(self.lo // (1 << i)) % 2 for i in range(4)]
+        one, two, three = (self.flip(m) - self.lo for m in (4, 8, 12))
+        self.inner = self.bits[2] + self.bits[3] - 2 * self.bits[2] * self.bits[3]
+        self.away = (
+            0,
+            one,
+            self.inner * three + (1 - self.inner) * two,
+            self.inner * two + (1 - self.inner) * three,
+        )
 
     def flip(self, mask):
         out = self.lo
@@ -134,7 +142,7 @@
 
 
 class Scatter:
-    sems = (4, 7)
+    sems = (5, 7)
 
     @staticmethod
     def scratch(rows, d, span=GROUP):
@@ -143,7 +151,7 @@
         return [
             pltpu.VMEM((zs, 4, h, d), BF),
             pltpu.VMEM((zs, 2, h, d), BF),
-            pltpu.VMEM((zs - 1, rows, d), BF),
+            pltpu.VMEM((5 if span == GROUP else 1, rows, d), BF),
             pltpu.SemaphoreType.DMA(Scatter.sems),
             pltpu.SemaphoreType.DMA(Scatter.sems),
         ]
@@ -152,67 +160,105 @@
         self.here, self.part = here, part
         self.first, self.second, self.zin, self.send, self.recv = scratch
         self.rows = part.shape[1]
+        self.half = self.rows // 2
         self.off = here.lo - here.lo % part.shape[0]
-        self.far = tuple(range(1, part.shape[0] // 4))
-        self.half = self.rows // 2
+        self.line = part.shape[0] == GROUP
         self.sent = []
 
-    def _copy(self, j, slot, src, dst, mask):
-        return rcopy(src, dst, self.send.at[j, slot], self.recv.at[j, slot], self.here.dev(mask))
+    def _copy(self, k, slot, src, dst, mask):
+        return rcopy(src, dst, self.send.at[k, slot], self.recv.at[k, slot], self.here.dev(mask))
 
     def _go(self, *a):
         c = self._copy(*a)
         c.start()
         self.sent.append(c)
 
-    def _piece(self, mask, part):
-        return self.part.at[self.here.flip(mask) - self.off, pl.ds(part * self.half, self.half)]
-
-    def start(self, j):
-        m = 4 * j
-        self._go(j, 1, self._piece(m ^ 3, 0), self.first.at[j, 1], 2)
-        self._go(j, 3, self._piece(m ^ 3, 1), self.first.at[j, 3], 1)
-        self._go(j, 0, self._piece(m ^ 2, 0), self.first.at[j, 0], 2)
-        self._go(j, 2, self._piece(m ^ 1, 1), self.first.at[j, 2], 1)
-
-    def cross(self, j):
-        m = 4 * j
+    def _block(self, k, q):
+        return self.here.flip(q) + self.here.away[k] - self.off
+
+    def _piece(self, k, q, part):
+        return self.part.at[self._block(k, q), pl.ds(part * self.half, self.half)]
+
+    def start(self, k):
+        self._go(k, 1, self._piece(k, 3, 0), self.first.at[k, 1], 2)
+        self._go(k, 3, self._piece(k, 3, 1), self.first.at[k, 3], 1)
+        self._go(k, 0, self._piece(k, 2, 0), self.first.at[k, 0], 2)
+        self._go(k, 2, self._piece(k, 1, 1), self.first.at[k, 2], 1)
+
+    def cross(self, k):
         h = self.half
-        for slot, mask, part, to in ((1, 1, 0, 1), (3, 2, 1, 2)):
-            self._copy(j, slot, self.first.at[j, slot], self.first.at[j, slot], 1).wait_recv()
-            own = self._piece(m ^ mask, part)
+        for slot, q, part, to in ((1, 1, 0, 1), (3, 2, 1, 2)):
+            self._copy(k, slot, self.first.at[k, slot], self.first.at[k, slot], 1).wait_recv()
+            own = self._piece(k, q, part)
 
             def body(r, own=own, slot=slot):
-                own[r] = (own[r].astype(F32) + self.first[j, slot, r].astype(F32)).astype(BF)
+                own[r] = (own[r].astype(F32) + self.first[k, slot, r].astype(F32)).astype(BF)
 
             rowwise(h, 16, body)
-            self._go(j, 4 + part, own, self.second.at[j, part], to)
-
-    def finish(self, j, out=None):
-        m = 4 * j
+            self._go(k, 4 + part, own, self.second.at[k, part], to)
+
+    def _reduce(self, k, boxes, out):
         h = self.half
         for part, slot in ((0, 0), (1, 2)):
-            self._copy(j, slot, self.first.at[j, slot], self.first.at[j, slot], 1).wait_recv()
-            self._copy(j, 4 + part, self.second.at[j, part], self.second.at[j, part], 1).wait_recv()
-        if out is not None:
-            for k in self.far:
-                self._copy(k, 6, self.zin.at[k - 1], self.zin.at[k - 1], 4).wait_recv()
-        for part, slot in ((0, 0), (1, 2)):
-            own = self._piece(m, part)
+            own = self._piece(k, 0, part)
 
             def body(r, own=own, part=part, slot=slot):
-                total = own[r].astype(F32) + self.first[j, slot, r].astype(F32) + self.second[j, part, r].astype(F32)
+                total = own[r].astype(F32) + self.first[k, slot, r].astype(F32) + self.second[k, part, r].astype(F32)
                 at = pl.ds(part * h + r.start, r.size)
+                for b in boxes:
+                    total = total + self.zin[b, at].astype(F32)
                 if out is None:
                     own[r] = total.astype(BF)
                 else:
-                    for k in self.far:
-                        total = total + self.zin[k - 1, at].astype(F32)
                     out[at] = total.astype(out.dtype)
 
             rowwise(h, 16, body)
-        if out is None:
-            self._go(j, 6, self.part.at[self.here.flip(m) - self.off], self.zin.at[j - 1], m)
+
+    def _box(self, b):
+        return self.zin.at[b], self.recv.at[(1, 2, 3, 0, 4)[b], 6]
+
+    def _pass(self, k, b, mask):
+        box, full = self._box(b)
+        return rcopy(self.part.at[self._block(k, 0)], box, self.send.at[k, 6], full, self.here.dev(mask))
+
+    def _full(self, b):
+        box, full = self._box(b)
+        rcopy(box, box, self.send.at[0, 6], full, self.here.dev(4)).wait_recv()
+
+    def finish(self, k, out=None):
+        for part, slot in ((0, 0), (1, 2)):
+            self._copy(k, slot, self.first.at[k, slot], self.first.at[k, slot], 1).wait_recv()
+            self._copy(k, 4 + part, self.second.at[k, part], self.second.at[k, part], 1).wait_recv()
+        if k == 0:
+            self._full(0)
+        if not self.line:
+            self._reduce(k, () if k else (0,), out)
+            if k:
+                self._pass(k, 0, 4).start()
+                self.sent.append(self._pass(k, 0, 4))
+            return
+        inner = self.here.inner
+
+        @pl.when(inner == 0)
+        def _():
+            self._reduce(k, () if k else (0,), out)
+            if k:
+                self._pass(k, k - 1, 4).start()
+
+        @pl.when(inner == 1)
+        def _():
+            boxes = ((0, 3), (4,), (1,), (2,))[k]
+            for b in boxes:
+                if b:
+                    self._full(b)
+            self._reduce(k, boxes, out)
+            if k == 1:
+                self._pass(k, 0, 4).start()
+            elif k:
+                self._pass(k, k + 1, 12).start()
+
+        if k:
+            self.sent.append(self._pass(k, 0, 4))
 
     def end(self):
         for c in self.sent:
@@ -304,9 +350,9 @@
 
 
 def front_kernel(
-    n1, rope, code_row, code_col, dy2, wqkv, wout, wgu, wdn,
-    raw, n1g_out, dy2g, qkvs, outs, gus, dns, attn,
-    n1g, wq, attended,
+    mixm, n1, rope, code_row, code_col, sorter, g, wqkv, wout, wgu, wdn,
+    raw, gs, n1g_out, dy2g, qkvs, outs, gus, dns, attn,
+    n1g, wq, attended, plane, dy2,
     gsend, grecv, own, csend, crecv, cown, psend, precv, late, group_out, ssend, srecv, sown,
 ):
     here = Here()
@@ -342,6 +388,13 @@
     u = exchange_columns(here, wgu, gus, half // CUBE, (0, half), CUBE, csend.at[1], crecv.at[1], cown.at[1])
     d = exchange_columns(here, wdn, dns, half // CUBE, (0,), CUBE, csend.at[2], crecv.at[2], cown.at[2])
     ga.forward(o[3])
+    sort_planes(sorter, g, gs, plane)
+    p = read_mix(mixm)
+
+    def to_branch(r):
+        dy2[r] = mixed([p[j][5] for j in range(4)], [gs[j, r].astype(F32) for j in range(4)]).astype(BF)
+
+    rowwise(tokens, 16, to_branch)
     other_core(0, qkvs)
     get = pltpu.make_async_copy(qkvs, wq, late)
     get.start()
@@ -399,7 +452,7 @@
         end()
 
 
-def front(n1, tables, dy2, wqkv, wout, wgu, wdn, cid):
+def front(mixm, n1, tables, sorter, g, wqkv, wout, wgu, wdn, cid):
     hi, rows, _ = wqkv.shape
     ff = wdn.shape[2]
     tokens = n1.shape[0]
@@ -410,20 +463,23 @@
         front_kernel,
         out_shape=(
             shape(GROUP, tokens, head),
+            shape(g.shape[1], tokens, g.shape[2]),
             shape(GROUP, *n1.shape),
-            shape(CUBE, *dy2.shape),
+            shape(CUBE, *n1.shape),
             shape(2, hi, GROUP, rows, head),
             shape(2, GROUP, out_rows, wout.shape[1]),
             shape(2, hi, GROUP, rows, 2 * ff // CUBE),
             shape(2, hi, GROUP, rows, ff // CUBE),
             shape(tokens, GROUP * HEAD_DIM),
         ),
-        in_specs=[*vmem_spec(4), *any_spec(5)],
-        out_specs=(*vmem_spec(1), *any_spec(7)),
+        in_specs=[*smem_spec(1), *vmem_spec(6), *any_spec(4)],
+        out_specs=(*vmem_spec(2), *any_spec(7)),
         scratch_shapes=[
             pltpu.VMEM((GROUP, *n1.shape), BF),
             pltpu.VMEM((2, hi, GROUP, rows, head), BF),
             pltpu.VMEM((GROUP, tokens, HEAD_DIM), BF),
+            pltpu.VMEM((g.shape[1], tokens, g.shape[2]), BF),
+            pltpu.VMEM(n1.shape, BF),
             pltpu.SemaphoreType.DMA((3,) + Gather.sems),
             pltpu.SemaphoreType.DMA((3,) + Gather.sems),
             pltpu.SemaphoreType.DMA((3,)),
@@ -438,8 +494,8 @@
             pltpu.SemaphoreType.DMA((GROUP,)),
             pltpu.SemaphoreType.DMA,
         ],
-        compiler_params=params(cid, 40),
-    )(n1, *tables, dy2, wqkv, wout, wgu, wdn)
+        compiler_params=params(cid, 62),
+    )(mixm, n1, *tables, sorter, g, wqkv, wout, wgu, wdn)
 
 
 def pair_add(here, g, inbox, send, recv):
@@ -684,6 +740,70 @@
         dqkv[:, rows, i * HEAD_DIM : (i + 1) * HEAD_DIM] = v.astype(BF).reshape(GROUP, slots, HEAD_DIM)
 
 
+class GradsHome:
+    @staticmethod
+    def scratch(hi, rows, w):
+        return [
+            pltpu.VMEM((hi, CUBE, rows, w), BF),
+            pltpu.VMEM((hi, CUBE, rows, w), BF),
+            *[pltpu.SemaphoreType.DMA((hi, CUBE))] * 6,
+        ]
+
+    def __init__(self, here, gmlp, out, scratch):
+        self.here, self.out = here, out
+        self.mine, self.box, self.zsend, self.zrecv, self.load, self.send, self.recv, self.own = scratch
+        self.hi, _, self.rows, _ = self.mine.shape
+        self.sent = []
+        self.loads = {}
+        self.gmlp = gmlp
+
+    def begin(self, wave):
+        here = self.here
+        for h in range(self.hi):
+            for m in wave:
+
+                def block(mask, h=h):
+                    at = (h * GROUP + here.flip(mask)) * self.rows
+                    return self.gmlp.at[pl.ds(pl.multiple_of(at, self.rows), self.rows)]
+
+                c = rcopy(block(m ^ 8), self.box.at[h, m], self.zsend.at[h, m], self.zrecv.at[h, m], here.dev(8))
+                c.start()
+                self.sent.append(c)
+                c = pltpu.make_async_copy(block(m), self.mine.at[h, m], self.load.at[h, m])
+                c.start()
+                self.loads[h, m] = c
+
+    def relay(self, m):
+        here = self.here
+        for h in range(self.hi):
+            box, mine = self.box.at[h, m], self.mine.at[h, m]
+            self.loads[h, m].wait()
+            rcopy(box, box, self.zsend.at[h, m], self.zrecv.at[h, m], here.dev(8)).wait_recv()
+
+            def body(r, box=box, mine=mine):
+                mine[r] = (mine[r].astype(F32) + box[r].astype(F32)).astype(BF)
+
+            rowwise(self.rows, 16, body)
+            to = self.out.at[here.lo % CUBE, h]
+            if m:
+                c = rcopy(mine, to, self.send.at[h, m], self.recv.at[h, m], here.dev(m))
+                self.sent.append(c)
+            else:
+                c = pltpu.make_async_copy(mine, to, self.own.at[h, 0])
+                self.loads[h, 0] = c
+            c.start()
+
+    def end(self):
+        here = self.here
+        for h in range(self.hi):
+            self.loads[h, 0].wait()
+            for m in range(1, CUBE):
+                ref = self.out.at[here.flip(m) % CUBE, h]
+                rcopy(ref, ref, self.send.at[h, m], self.recv.at[h, m], here.dev(m)).wait_recv()
+        for c in self.sent:
+            c.wait_send()
+
+
 def back_kernel(
     d_rows, qkv, qkvs, dy1, attn, rope, code_row, code_col, n1g, y2_in, gmlp,
     dn_out, y2_out, gout_out, gqkv_out, gmlp_out,
@@ -710,12 +830,14 @@
     rs_dn = Scatter(here, dn, scratch[:k])
     rs_y2 = Scatter(here, y2, scratch[k : 2 * k])
     rs_go = Scatter(here, gout.reshape(GROUP, gout.shape[0] // GROUP, width), scratch[2 * k : 3 * k])
-    qhome, mhome = scratch[3 * k : 3 * k + 3], scratch[3 * k + 3 :]
-    order = (2, 3, 1, 0)
+    qhome = scratch[3 * k : 3 * k + 3]
+    gm = GradsHome(here, gmlp, gmlp_out, scratch[3 * k + 3 :])
+    gm.begin((0, 1))
+    order = (3, 2, 1, 0)
     y2_load.wait()
     rs_y2.start(1)
     rs_y2.start(0)
-    end_mlp = send_home(here, gmlp, gmlp_out, *mhome)
+    gm.begin((2,))
     mine.wait()
     for m in ALL:
         ref = d_out.at[here.flip(m)]
@@ -750,8 +872,10 @@
         return pltpu.make_async_copy(n1g.at[:, :, cols], tiles.at[k % 2], tile_sem.at[k % 2])
 
     qkv_tile(0).start()
+    gm.relay(0)
+    gm.begin((3,))
     for j in order:
-        blocks = pl.ds(here.flip(4 * j) - here.lo % 4, 4)
+        blocks = pl.ds(here.lo + here.away[j] - here.lo % 4, 4)
 
         def part(k, carry, blocks=blocks):
             at = pl.ds(pl.multiple_of(k * TILE, TILE), TILE)
@@ -770,6 +894,8 @@
         rows = pl.ds((k % (count // 2)) * narrow, narrow)
         gqkv[k // (count // 2), rows, :] = t_dot(x, dqkv[...].reshape(GROUP * tokens, 3 * HEAD_DIM)).astype(BF)
     gqkv_pair.start()
+    gm.relay(1)
+    gm.begin((4,))
     rs_y2.finish(0, y2_out)
     rs_dn.cross(order[0])
     for k in range(chunks):
@@ -790,6 +916,8 @@
 
     gqkv_pair.wait()
     add(gqkv.at[here.rep], qbox)
+    gm.relay(2)
+    gm.begin((5,))
     end_qkv = send_home(here, gqkv.at[here.rep], gqkv_out, *qhome)
     rs_dn.cross(order[2])
     rs_dn.finish(order[1])
@@ -803,15 +931,22 @@
     rs_dn.cross(order[3])
     rs_dn.finish(order[2])
     rs_go.cross(order[0])
+    gm.relay(3)
+    gm.begin((6,))
     rs_go.cross(order[1])
     rs_go.finish(order[0])
+    gm.relay(4)
+    gm.begin((7,))
     rs_go.cross(order[2])
     rs_go.finish(order[1])
+    gm.relay(5)
     rs_go.cross(order[3])
     rs_go.finish(order[2])
     rs_dn.finish(0, dn_out)
+    gm.relay(6)
     rs_go.finish(0, gout_out)
-    end_mlp()
+    gm.relay(7)
+    gm.end()
     end_qkv()
     for c in swaps:
         c.wait_send()
@@ -830,7 +965,7 @@
             jax.ShapeDtypeStruct((tokens, width), F32),
             jax.ShapeDtypeStruct((half // GROUP, width), F32),
             jax.ShapeDtypeStruct((GROUP, hi, half // (hi * GROUP), w), BF),
-            jax.ShapeDtypeStruct((GROUP, hi, half // (hi * GROUP), gmlp.shape[1]), BF),
+            jax.ShapeDtypeStruct((CUBE, hi, half // (hi * GROUP), gmlp.shape[1]), BF),
         ),
         in_specs=[*vmem_spec(8), *any_spec(3)],
         out_specs=(*vmem_spec(3), *any_spec(2)),
@@ -858,7 +993,7 @@
             *Scatter.scratch(tokens, width, CUBE),
             *Scatter.scratch(half // GROUP, width),
             *home_sems(hi),
-            *home_sems(hi),
+            *GradsHome.scratch(hi, half // (hi * GROUP), gmlp.shape[1]),
         ],
         compiler_params=params(cid, 63),
     )(d_rows, qkv, qkvs, dy1, attn, *tables, n1g, y2, gmlp)
@@ -904,28 +1039,30 @@
 TILE = 512
 
 
-def open_kernel(mixa, mixm, sorter, x, g, hs, gs, n1, dy2, plane):
-    m, p = read_mix(mixa), read_mix(mixm)
+def sort_planes(sorter, x, planes, plane):
     tokens, streams, width = x.shape
-    for src, dst in ((x, hs), (g, gs)):
-
-        def split(r, src=src):
-            v = src[r].astype(F32)
-            for i in range(streams):
-                plane[i, r] = v[:, i, :].astype(BF)
-
-        rowwise(tokens, 16, split)
+
+    def split(r):
+        v = x[r].astype(F32)
         for i in range(streams):
-            for c in range(0, width, TILE):
-                at = slice(c, c + TILE)
-                dst[i, :, at] = dot(sorter[...], plane[i, :, at]).astype(BF)
+            plane[i, r] = v[:, i, :].astype(BF)
+
+    rowwise(tokens, 16, split)
+    for i in range(streams):
+        for c in range(0, width, TILE):
+            at = slice(c, c + TILE)
+            planes[i, :, at] = dot(sorter[...], plane[i, :, at]).astype(BF)
+
+
+def open_kernel(mixa, sorter, x, hs, n1, plane):
+    m = read_mix(mixa)
+    sort_planes(sorter, x, hs, plane)
 
     def norm(r):
         x1 = mixed([m[j][0] for j in range(4)], [hs[j, r].astype(F32) for j in range(4)])
         n1[r] = moments(x1)[0].astype(BF)
-        dy2[r] = mixed([p[j][5] for j in range(4)], [gs[j, r].astype(F32) for j in range(4)]).astype(BF)
-
-    rowwise(tokens, 16, norm)
+
+    rowwise(x.shape[0], 16, norm)
 
 
 def smem_spec(n):
@@ -936,21 +1073,19 @@
     return pltpu.CompilerParams(vmem_limit_bytes=mib * MIB)
 
 
-def open_streams(mixa, mixm, sorter, x, g):
+def open_streams(mixa, sorter, x):
     tokens, streams, width = x.shape
     return pl.pallas_call(
         open_kernel,
         out_shape=(
             jax.ShapeDtypeStruct((streams, tokens, width), BF),
-            jax.ShapeDtypeStruct((streams, tokens, width), BF),
-            jax.ShapeDtypeStruct((tokens, width), BF),
             jax.ShapeDtypeStruct((tokens, width), BF),
         ),
-        in_specs=[*smem_spec(2), *vmem_spec(3)],
-        out_specs=tuple(vmem_spec(4)),
+        in_specs=[*smem_spec(1), *vmem_spec(2)],
+        out_specs=tuple(vmem_spec(2)),
         scratch_shapes=[pltpu.VMEM((streams, tokens, width), BF)],
         compiler_params=local_params(),
-    )(mixa, mixm, sorter, x, g)
+    )(mixa, sorter, x)
 
 
 def middle_kernel(mixa, mixm, hs, attn, wout, y1, n2):
@@ -1032,7 +1167,7 @@
 
 
 def close_kernel(
-    mixa, mixm, sorter, hs, gs, dx2, y1, y2, dn1, other, new, d_streams, total,
+    mixa, mixm, sorter, hs, gs, dx2, y1, y2, dn1, other, new, d_streams, mix_a, mix_m,
     sums, planes, fresh, mine, inbox, send, recv,
 ):
     here = Here()
@@ -1084,7 +1219,16 @@
         c.wait()
     for k in ALL:
         everyone = everyone + inbox[k]
-    total[...] = everyone
+    everyone = jnp.sum(everyone, axis=1, keepdims=True)
+    for n, out in enumerate((mix_a, mix_m)):
+        row = lax.broadcasted_iota(jnp.int32, out.shape, 0)
+        col = lax.broadcasted_iota(jnp.int32, out.shape, 1)
+        value = jnp.zeros(out.shape, F32)
+        for j in range(4):
+            for c in range(6):
+                k = n * 24 + j * 6 + c
+                value = jnp.where((row == j) & (col == c), everyone[k : k + 1], value)
+        out[...] = value
 
 
 def close(mixa, mixm, sorter, hs, gs, dx2, y1, y2, dn1, other, cid):
@@ -1094,10 +1238,11 @@
         out_shape=(
             jax.ShapeDtypeStruct((tokens, streams, width), F32),
             jax.ShapeDtypeStruct((tokens, streams, width), F32),
-            jax.ShapeDtypeStruct((48, 128), F32),
+            jax.ShapeDtypeStruct(mixa.shape, F32),
+            jax.ShapeDtypeStruct(mixm.shape, F32),
         ),
         in_specs=[*smem_spec(2), *vmem_spec(8)],
-        out_specs=tuple(vmem_spec(3)),
+        out_specs=tuple(vmem_spec(4)),
         scratch_shapes=[
             pltpu.VMEM((48, 16, 128), F32),
             pltpu.VMEM((streams, tokens, width), F32),
@@ -1109,6 +1254,34 @@
         ],
         compiler_params=params(cid),
     )(mixa, mixm, sorter, hs, gs, dx2, y1, y2, dn1, other)
+
+
+def lay_out_kernel(qkv, out, mlp, gqkv, gout, ggu, gdown):
+    head = HEAD_DIM
+    for l in range(qkv.shape[0]):
+        for i in range(3):
+            at = i * GROUP * head + l * head
+            gqkv[:, :, at : at + head] = qkv[l, :, :, i * head : (i + 1) * head].astype(F32)
+    block = mlp.shape[3] // 3
+    for l in range(CUBE):
+        for i in range(2):
+            at = (i * CUBE + l) * block
+            ggu[:, :, at : at + block] = mlp[l, :, :, i * block : (i + 1) * block].astype(F32)
+        gdown[:, :, l * block : (l + 1) * block] = mlp[l, :, :, 2 * block :].astype(F32)
+    gout[...] = out[...]
+
+
+def lay_out(qkv, out, mlp):
+    _, hi, rows, w = mlp.shape
+    ff = w // 3 * CUBE
+    shapes = [(hi, rows, GROUP * qkv.shape[3]), out.shape, (hi, rows, 2 * ff), (hi, rows, ff)]
+    return pl.pallas_call(
+        lay_out_kernel,
+        out_shape=tuple(jax.ShapeDtypeStruct(s, F32) for s in shapes),
+        in_specs=vmem_spec(3),
+        out_specs=tuple(vmem_spec(4)),
+        compiler_params=local_params(),
+    )(qkv, out, mlp)
 
 
 def slot_layout(lengths_row, capacity):
@@ -1182,7 +1355,7 @@
 
     sorter = (jnp.arange(tokens, dtype=jnp.int32)[:, None] == deal[None, :]).astype(BF)
 
-    hs, gs, n1, low_grad_mlp = open_streams(mix_attn, mix_mlp, sorter, streams, cotangent)
+    hs, n1 = open_streams(mix_attn, sorter, streams)
     low_attn = to_bins(n1)
 
     bins = lax.axis_index("rep") * bin_count + my_hi * my_bins
@@ -1197,8 +1370,8 @@
     code = segment * CODE + position
     tables = (jnp.concatenate([cosine, sine], -1), code[:, :, None], code[:, None, :])
 
-    raw_qkv, n1g, dy2g, qkvs, outs, gus, dns, attn_rows = front(
-        low_attn, tables, low_grad_mlp,
+    raw_qkv, gs, n1g, dy2g, qkvs, outs, gus, dns, attn_rows = front(
+        mix_mlp, low_attn, tables, sorter, cotangent,
         gather_hi(w_qkv), gather_hi(w_out).reshape(-1, width), gather_hi(w_gu), gather_hi(w_down), 1,
     )
     rows = w_qkv.shape[0]
@@ -1212,37 +1385,18 @@
         mix_attn, mix_mlp, n2, dy2g, gus, dns, hs, gs, outs, y1, 4
     )
 
-    def own_rows(x):
-        x = x.astype(F32).transpose(1, 2, 0, 3)
-        return sum_hi(x.reshape(hi, rows, -1)).reshape(rows, x.shape[2], -1)
-
     attn_cols = attn_rows.reshape(tokens, 2, hi, GROUP, rows).swapaxes(2, 3).reshape(tokens, width)
     dn1, y2, g_out, g_qkv, g_mlp = back(
         to_bins(grad_attn), raw_qkv, qkvs, low_grad_attn, attn_cols, tables,
         n1g, y2_part, g_mlp, hi, 7,
     )
-    g_mlp = g_mlp.astype(F32).reshape(2, CUBE, *g_mlp.shape[1:]).sum(0)
-    g_mlp = own_rows(g_mlp)
-    g_out = sum_hi(g_out.reshape(hi, rows, width))
-    g_qkv = own_rows(g_qkv)
-    new_streams, d_streams, sums = close(
+    weight_grads = lay_out(g_qkv, g_out.reshape(hi, rows, width), g_mlp)
+    new_streams, d_streams, g_mix_attn, g_mix_mlp = close(
         mix_attn, mix_mlp, sorter, hs, gs, dx2, y1, y2, from_bins(dn1), mlp_sums, 8
     )
     if hi > 1:
-        sums = lax.psum(sums, "shard", axis_index_groups=hi_groups)
-    sums = jnp.sum(sums, axis=-1).reshape(2, 4, 6)
-    g_mix_attn, g_mix_mlp = sums[0], sums[1]
-    block = ff // CUBE
-    return (
-        new_streams,
-        d_streams,
-        g_mix_attn,
-        g_mix_mlp,
-        g_qkv.reshape(rows, GROUP, 3, HEAD_DIM).swapaxes(1, 2).reshape(rows, -1),
-        g_out,
-        jnp.concatenate([g_mlp[:, :, :block].reshape(rows, ff), g_mlp[:, :, block : 2 * block].reshape(rows, ff)], axis=1),
-        g_mlp[:, :, 2 * block :].reshape(rows, ff),
-    )
+        g_mix_attn, g_mix_mlp = lax.psum((g_mix_attn, g_mix_mlp), "shard", axis_index_groups=hi_groups)
+    return (new_streams, d_streams, g_mix_attn, g_mix_mlp, *(sum_hi(g) for g in weight_grads))
 
 
 def solution(mesh):

time: 742 us -> 700 us (0.943)
  local copies, waits for them, and re-layouts: 28.7 us -> 9.79 us
  Pallas kernels: 688 us -> 673 us
    pallas_call x1, Pallas kernels: 252 us -> 238 us  [back(): pl.pallas_call(back_kernel, out_shape=(jax.ShapeDtypeStruct((tokens, widt...]
    unnamed x37 -> x10, local copies, waits for them, and re-layouts: 17.7 us -> 8.12 us
    pallas_call x1, Pallas kernels: 18.9 us -> 10.9 us  [open_streams(): pl.pallas_call(open_kernel, out_shape=(jax.ShapeDtypeStruct((streams, tok...]
where the time goes in v5:
time: 700 us; the launch traced here: 693 us
  Pallas kernels  673 us (96%)
  local copies, waits for them, and re-layouts  9.79 us (1%)
  other arithmetic  9.15 us (1%)
    pallas_call x1, Pallas kernels, front(): pl.pallas_call(front_kernel, out_shape=(shape(GROUP, tokens, head), shape...  247 us
    pallas_call x1, Pallas kernels, back(): pl.pallas_call(back_kernel, out_shape=(jax.ShapeDtypeStruct((tokens, widt...  238 us
    pallas_call x1, Pallas kernels, mlp(): pl.pallas_call(mlp_kernel, out_shape=(jax.ShapeDtypeStruct((*blocks, widt...  131 us
    pallas_call x1, Pallas kernels, close(): pl.pallas_call(close_kernel, out_shape=(jax.ShapeDtypeStruct((tokens, str...  30.8 us

profile of v5, /device:TPU:0, one launch (start us, length us, event | category | flops | bytes accessed | tf_op | source)
XLA Modules:
  0.0 693.0 jit_solution(17917245352404220447)
XLA Ops:
  0.7 0.8 constant_dynamic-slice_fusion
  1.5 0.8 fusion.5
  2.2 0.1 copy.26
  2.3 0.1 copy.27
  2.4 0.1 convert_reduce_fusion
  2.5 0.1 select_reduce_fusion
  2.6 0.6 fusion.4.code_col
  3.2 1.3 fusion.2.sorter
  4.5 0.4 copy.30
  4.9 0.4 copy.28
  5.3 1.2 fusion.1.code_row
  6.5 3.7 multiply_cosine_fusion
  10.2 1.3 pad_maximum_fusion.rope
  11.5 10.9 %shard_map.161 = (bf16[4,128,2048]{2,1,0:T(8,128)(2,1)}, bf16[128,2048]{1,0:T(8,128)(2,1)}) custom-call(f32[4,6]{1,0:T(4,128)} %mixa.7, bf16[128,128]{1,0:T(8,128)(2,1)} %fusion.2.sorter, bf16[128,4,2048]{2,1,0:T(4,128)(2,1)} %x.1), custom_call_target="tpu_custom_call" | custom-call | tf_op jit(solution)/shard_map/pallas_call | solution.py:1078
  22.5 247.1 %shard_map.162 = (bf16[16,128,384]{2,1,0:T(8,128)(2,1)}, bf16[4,128,2048]{2,1,0:T(8,128)(2,1)}, bf16[16,128,2048]{2,1,0:T(8,128)(2,1)}, bf16[8,128,2048]{2,1,0:T...) custom-call(f32[4,6]{1,0:T(4,128)} %mixm.7, ...), custom_call_target="tpu_custom_call" | custom-call | tf_op jit(solution)/shard_map/pallas_call | solution.py:462
  269.5 9.1 %shard_map.163 = (f32[128,2048]{1,0:T(8,128)}, bf16[128,2048]{1,0:T(8,128)(2,1)}) custom-call(f32[4,6]{1,0:T(4,128)} %mixa.7, f32[4,6]{1,0:T(4,128)} %mixm.7, bf16[4,128,2048]{2,1,0:T(8,128)(2,1)} %get-tuple-element.40.hs, bf16[128,2048]{1,0:T(8,128)(2,1)} %get-tuple-element.43.attn, bf16[2048,2048]{1,0:T(8,128)(2,1)} %bitcast.14), custom_call_target="tpu_custom_call" | custom-call | tf_op jit(solution)/shard_map/pallas_call | solution.py:1111
  278.6 130.9 %shard_map.164 = (bf16[8,128,2048]{2,1,0:T(8,128)(2,1)}, bf16[1024,3072]{1,0:T(8,128)(2,1)}, f32[128,2048]{1,0:T(8,128)}, bf16[128,2048]{1,0:T(8,128)(2,1)}, bf1...) custom-call(f32[4,6]{1,0:T(4,128)} %mixa.7, f32[4,6]{1,0:T(4,128)} %mixm.7, bf16[128,2048]{1,0:T(8,128)(2,1)} %get-tuple-element.45.n2, ...), custom_call_target="tpu_custom_call" | custom-call | flops 38654705664 | bytes 62914560 | tf_op jit(solution)/shard_map/pallas_call | solution.py:687
  409.5 238.4 %shard_map.165 = (f32[128,2048]{1,0:T(8,128)}, f32[128,2048]{1,0:T(8,128)}, f32[64,2048]{1,0:T(8,128)}, bf16[16,1,64,384]{3,2,1,0:T(8,128)(2,1)}, bf16[8,1,64,3072]{3,2,1,0:T(8,128)(2,1)}) custom-call(bf16[128,2048]{1,0:T(8,128)(2,1)} %get-tuple-element.51.d_rows, bf16[16,128,384]{2,1,0:T(8,128)(2,1)} %get-tuple-element.52.qkv, bf16[2048,384]{1,0:T(8,128)(2,1)} %bitcast.17, ...), custom_call_target="tpu_custom_call" | custom-call | tf_op jit(solution)/shard_map/pallas_call | solution.py:961
  647.9 30.8 %shard_map.166 = (f32[128,4,2048]{2,1,0:T(4,128)}, f32[128,4,2048]{2,1,0:T(4,128)}, f32[4,6]{1,0:T(4,128)}, f32[4,6]{1,0:T(4,128)}) custom-call(f32[4,6]{1,0:T(4,128)} %mixa.7, f32[4,6]{1,0:T(4,128)} %mixm.7, bf16[128,128]{1,0:T(8,128)(2,1)} %fusion.2.sorter, bf16[4,128,2048]{2,1,0:T(8,128)(2,1)} %get-tuple-element.40.hs, ...), custom_call_target="tpu_custom_call" | custom-call | tf_op jit(solution)/shard_map/pallas_call | solution.py:1236
  678.7 5.7 shard_map.167
  684.5 0.0 copy-start
  684.5 4.9 copy.35
  689.4 0.0 copy-done
  689.4 0.0 copy-start.2
  689.4 0.0 copy-start.1
  689.4 2.0 copy.36
  691.4 0.0 copy-done.2
  691.4 0.6 copy.37
  692.0 0.0 copy-done.1
  692.0 0.6 copy.38
  (4 shorter events, 0.1 us)
Async XLA Ops:
  684.5 4.9 copy-start
  689.4 2.0 copy-start.2
  689.4 2.6 copy-start.1

commit v6 on v5

--- a/solution.py
+++ b/solution.py
@@ -837,7 +837,7 @@
     y2_load.wait()
     rs_y2.start(1)
     rs_y2.start(0)
-    gm.begin((2,))
+    gm.begin((2, 3))
     mine.wait()
     for m in ALL:
         ref = d_out.at[here.flip(m)]
@@ -872,8 +872,6 @@
         return pltpu.make_async_copy(n1g.at[:, :, cols], tiles.at[k % 2], tile_sem.at[k % 2])
 
     qkv_tile(0).start()
-    gm.relay(0)
-    gm.begin((3,))
     for j in order:
         blocks = pl.ds(here.lo + here.away[j] - here.lo % 4, 4)
 
@@ -894,8 +892,9 @@
         rows = pl.ds((k % (count // 2)) * narrow, narrow)
         gqkv[k // (count // 2), rows, :] = t_dot(x, dqkv[...].reshape(GROUP * tokens, 3 * HEAD_DIM)).astype(BF)
     gqkv_pair.start()
+    gm.relay(0)
     gm.relay(1)
-    gm.begin((4,))
+    gm.begin((4, 5))
     rs_y2.finish(0, y2_out)
     rs_dn.cross(order[0])
     for k in range(chunks):
@@ -917,10 +916,12 @@
     gqkv_pair.wait()
     add(gqkv.at[here.rep], qbox)
     gm.relay(2)
-    gm.begin((5,))
+    gm.begin((6,))
     end_qkv = send_home(here, gqkv.at[here.rep], gqkv_out, *qhome)
     rs_dn.cross(order[2])
     rs_dn.finish(order[1])
+    gm.relay(3)
+    gm.begin((7,))
     for k in range(chunks):
         gout_pass(k).wait_recv()
         if k >= chunks - 2:
@@ -931,19 +932,16 @@
     rs_dn.cross(order[3])
     rs_dn.finish(order[2])
     rs_go.cross(order[0])
-    gm.relay(3)
-    gm.begin((6,))
+    gm.relay(4)
     rs_go.cross(order[1])
     rs_go.finish(order[0])
-    gm.relay(4)
-    gm.begin((7,))
+    gm.relay(5)
     rs_go.cross(order[2])
     rs_go.finish(order[1])
-    gm.relay(5)
+    gm.relay(6)
     rs_go.cross(order[3])
     rs_go.finish(order[2])
     rs_dn.finish(0, dn_out)
-    gm.relay(6)
     rs_go.finish(0, gout_out)
     gm.relay(7)
     gm.end()

time: 700 us -> 685 us (0.979)
  Pallas kernels: 673 us -> 657 us
    pallas_call x1, Pallas kernels: 238 us -> 221 us  [back(): pl.pallas_call(back_kernel, out_shape=(jax.ShapeDtypeStruct((tokens, widt...]
where the time goes in v6:
time: 685 us; the launch traced here: 678 us
  Pallas kernels  657 us (96%)
  local copies, waits for them, and re-layouts  9.79 us (1%)
  other arithmetic  9.15 us (1%)
    pallas_call x1, Pallas kernels, front(): pl.pallas_call(front_kernel, out_shape=(shape(GROUP, tokens, head), shape...  247 us
    pallas_call x1, Pallas kernels, back(): pl.pallas_call(back_kernel, out_shape=(jax.ShapeDtypeStruct((tokens, widt...  221 us
    pallas_call x1, Pallas kernels, mlp(): pl.pallas_call(mlp_kernel, out_shape=(jax.ShapeDtypeStruct((*blocks, widt...  131 us
    pallas_call x1, Pallas kernels, close(): pl.pallas_call(close_kernel, out_shape=(jax.ShapeDtypeStruct((tokens, str...  32.9 us

profile of v6, /device:TPU:0, one launch (start us, length us, event | category | flops | bytes accessed | tf_op | source)
XLA Modules:
  0.0 677.5 jit_solution(12059057676104525444)
XLA Ops:
  0.7 0.8 constant_dynamic-slice_fusion
  1.5 0.8 fusion.5
  2.2 0.1 copy.26
  2.3 0.1 copy.27
  2.4 0.1 convert_reduce_fusion
  2.5 0.1 select_reduce_fusion
  2.6 0.6 fusion.4.code_col
  3.2 1.3 fusion.2.sorter
  4.5 0.4 copy.30
  4.9 0.4 copy.28
  5.3 1.2 fusion.1.code_row
  6.5 3.7 multiply_cosine_fusion
  10.2 1.3 pad_maximum_fusion.rope
  11.5 10.9 %shard_map.161 = (bf16[4,128,2048]{2,1,0:T(8,128)(2,1)}, bf16[128,2048]{1,0:T(8,128)(2,1)}) custom-call(f32[4,6]{1,0:T(4,128)} %mixa.7, bf16[128,128]{1,0:T(8,128)(2,1)} %fusion.2.sorter, bf16[128,4,2048]{2,1,0:T(4,128)(2,1)} %x.1), custom_call_target="tpu_custom_call" | custom-call | tf_op jit(solution)/shard_map/pallas_call | solution.py:1076
  22.5 247.1 %shard_map.162 = (bf16[16,128,384]{2,1,0:T(8,128)(2,1)}, bf16[4,128,2048]{2,1,0:T(8,128)(2,1)}, bf16[16,128,2048]{2,1,0:T(8,128)(2,1)}, bf16[8,128,2048]{2,1,0:T...) custom-call(f32[4,6]{1,0:T(4,128)} %mixm.7, ...), custom_call_target="tpu_custom_call" | custom-call | tf_op jit(solution)/shard_map/pallas_call | solution.py:462
  269.5 9.1 %shard_map.163 = (f32[128,2048]{1,0:T(8,128)}, bf16[128,2048]{1,0:T(8,128)(2,1)}) custom-call(f32[4,6]{1,0:T(4,128)} %mixa.7, f32[4,6]{1,0:T(4,128)} %mixm.7, bf16[4,128,2048]{2,1,0:T(8,128)(2,1)} %get-tuple-element.40.hs, bf16[128,2048]{1,0:T(8,128)(2,1)} %get-tuple-element.43.attn, bf16[2048,2048]{1,0:T(8,128)(2,1)} %bitcast.14), custom_call_target="tpu_custom_call" | custom-call | tf_op jit(solution)/shard_map/pallas_call | solution.py:1109
  278.6 130.9 %shard_map.164 = (bf16[8,128,2048]{2,1,0:T(8,128)(2,1)}, bf16[1024,3072]{1,0:T(8,128)(2,1)}, f32[128,2048]{1,0:T(8,128)}, bf16[128,2048]{1,0:T(8,128)(2,1)}, bf1...) custom-call(f32[4,6]{1,0:T(4,128)} %mixa.7, f32[4,6]{1,0:T(4,128)} %mixm.7, bf16[128,2048]{1,0:T(8,128)(2,1)} %get-tuple-element.45.n2, ...), custom_call_target="tpu_custom_call" | custom-call | flops 38654705664 | bytes 62914560 | tf_op jit(solution)/shard_map/pallas_call | solution.py:687
  409.5 220.8 %shard_map.165 = (f32[128,2048]{1,0:T(8,128)}, f32[128,2048]{1,0:T(8,128)}, f32[64,2048]{1,0:T(8,128)}, bf16[16,1,64,384]{3,2,1,0:T(8,128)(2,1)}, bf16[8,1,64,3072]{3,2,1,0:T(8,128)(2,1)}) custom-call(bf16[128,2048]{1,0:T(8,128)(2,1)} %get-tuple-element.51.d_rows, bf16[16,128,384]{2,1,0:T(8,128)(2,1)} %get-tuple-element.52.qkv, bf16[2048,384]{1,0:T(8,128)(2,1)} %bitcast.17, ...), custom_call_target="tpu_custom_call" | custom-call | tf_op jit(solution)/shard_map/pallas_call | solution.py:959
  630.3 32.9 %shard_map.166 = (f32[128,4,2048]{2,1,0:T(4,128)}, f32[128,4,2048]{2,1,0:T(4,128)}, f32[4,6]{1,0:T(4,128)}, f32[4,6]{1,0:T(4,128)}) custom-call(f32[4,6]{1,0:T(4,128)} %mixa.7, f32[4,6]{1,0:T(4,128)} %mixm.7, bf16[128,128]{1,0:T(8,128)(2,1)} %fusion.2.sorter, bf16[4,128,2048]{2,1,0:T(8,128)(2,1)} %get-tuple-element.40.hs, ...), custom_call_target="tpu_custom_call" | custom-call | tf_op jit(solution)/shard_map/pallas_call | solution.py:1234
  663.2 5.7 shard_map.167
  669.0 0.0 copy-start
  669.0 4.9 copy.35
  673.9 0.0 copy-done
  673.9 0.0 copy-start.2
  673.9 0.0 copy-start.1
  673.9 2.0 copy.36
  675.9 0.0 copy-done.2
  675.9 0.6 copy.37
  676.5 0.0 copy-done.1
  676.5 0.6 copy.38
  (4 shorter events, 0.1 us)
Async XLA Ops:
  669.0 4.9 copy-start
  673.9 2.0 copy-start.2
  673.9 2.6 copy-start.1

commit v7 on v6

--- a/solution.py
+++ b/solution.py
@@ -583,7 +583,8 @@
             up = dot(x, wgu[:, up_at])
             gate = dot(x, wgu[:, gate_at])
             dh = dot(dy2g[blocks].reshape(group_rows, width), wdn[:, up_at])
-            sigmoid = 1.0 / (1.0 + jnp.exp(-gate))
+            small = jnp.exp(-jnp.abs(gate))
+            sigmoid = jnp.where(gate >= 0.0, 1.0, small) / (1.0 + small)
             silu = gate * sigmoid
             hidden[blocks, :, up_at] = (silu * up).astype(BF).reshape(4, tokens, step)
             dgu[blocks, :, up_at] = (dh * silu).astype(BF).reshape(4, tokens, step)
@@ -936,14 +937,14 @@
     rs_go.cross(order[1])
     rs_go.finish(order[0])
     gm.relay(5)
+    gm.relay(6)
+    gm.relay(7)
     rs_go.cross(order[2])
     rs_go.finish(order[1])
-    gm.relay(6)
     rs_go.cross(order[3])
     rs_go.finish(order[2])
     rs_dn.finish(0, dn_out)
     rs_go.finish(0, gout_out)
-    gm.relay(7)
     gm.end()
     end_qkv()
     for c in swaps:

time: 685 us -> 684 us (level)
  no operation moved by 1% of the time
where the time goes in v7:
time: 684 us; the launch traced here: 677 us
  Pallas kernels  657 us (96%)
  local copies, waits for them, and re-layouts  9.79 us (1%)
  other arithmetic  9.15 us (1%)
    pallas_call x1, Pallas kernels, front(): pl.pallas_call(front_kernel, out_shape=(shape(GROUP, tokens, head), shape...  247 us
    pallas_call x1, Pallas kernels, back(): pl.pallas_call(back_kernel, out_shape=(jax.ShapeDtypeStruct((tokens, widt...  220 us
    pallas_call x1, Pallas kernels, mlp(): pl.pallas_call(mlp_kernel, out_shape=(jax.ShapeDtypeStruct((*blocks, widt...  131 us
    pallas_call x1, Pallas kernels, close(): pl.pallas_call(close_kernel, out_shape=(jax.ShapeDtypeStruct((tokens, str...  33 us

profile of v7, /device:TPU:0, one launch (start us, length us, event | category | flops | bytes accessed | tf_op | source)
XLA Modules:
  0.0 677.0 jit_solution(15823953660101467275)
XLA Ops:
  0.7 0.8 constant_dynamic-slice_fusion
  1.5 0.8 fusion.5
  2.2 0.1 copy.26
  2.3 0.1 copy.27
  2.4 0.1 convert_reduce_fusion
  2.5 0.1 select_reduce_fusion
  2.6 0.6 fusion.4.code_col
  3.2 1.3 fusion.2.sorter
  4.5 0.4 copy.30
  4.9 0.4 copy.28
  5.3 1.2 fusion.1.code_row
  6.5 3.7 multiply_cosine_fusion
  10.2 1.3 pad_maximum_fusion.rope
  11.5 10.9 %shard_map.161 = (bf16[4,128,2048]{2,1,0:T(8,128)(2,1)}, bf16[128,2048]{1,0:T(8,128)(2,1)}) custom-call(f32[4,6]{1,0:T(4,128)} %mixa.7, bf16[128,128]{1,0:T(8,128)(2,1)} %fusion.2.sorter, bf16[128,4,2048]{2,1,0:T(4,128)(2,1)} %x.1), custom_call_target="tpu_custom_call" | custom-call | tf_op jit(solution)/shard_map/pallas_call | solution.py:1077
  22.5 247.1 %shard_map.162 = (bf16[16,128,384]{2,1,0:T(8,128)(2,1)}, bf16[4,128,2048]{2,1,0:T(8,128)(2,1)}, bf16[16,128,2048]{2,1,0:T(8,128)(2,1)}, bf16[8,128,2048]{2,1,0:T...) custom-call(f32[4,6]{1,0:T(4,128)} %mixm.7, ...), custom_call_target="tpu_custom_call" | custom-call | tf_op jit(solution)/shard_map/pallas_call | solution.py:462
  269.5 9.1 %shard_map.163 = (f32[128,2048]{1,0:T(8,128)}, bf16[128,2048]{1,0:T(8,128)(2,1)}) custom-call(f32[4,6]{1,0:T(4,128)} %mixa.7, f32[4,6]{1,0:T(4,128)} %mixm.7, bf16[4,128,2048]{2,1,0:T(8,128)(2,1)} %get-tuple-element.40.hs, bf16[128,2048]{1,0:T(8,128)(2,1)} %get-tuple-element.43.attn, bf16[2048,2048]{1,0:T(8,128)(2,1)} %bitcast.14), custom_call_target="tpu_custom_call" | custom-call | tf_op jit(solution)/shard_map/pallas_call | solution.py:1110
  278.6 131.3 %shard_map.164 = (bf16[8,128,2048]{2,1,0:T(8,128)(2,1)}, bf16[1024,3072]{1,0:T(8,128)(2,1)}, f32[128,2048]{1,0:T(8,128)}, bf16[128,2048]{1,0:T(8,128)(2,1)}, bf1...) custom-call(f32[4,6]{1,0:T(4,128)} %mixa.7, f32[4,6]{1,0:T(4,128)} %mixm.7, bf16[128,2048]{1,0:T(8,128)(2,1)} %get-tuple-element.45.n2, ...), custom_call_target="tpu_custom_call" | custom-call | flops 38654705664 | bytes 62914560 | tf_op jit(solution)/shard_map/pallas_call | solution.py:688
  409.9 219.8 %shard_map.165 = (f32[128,2048]{1,0:T(8,128)}, f32[128,2048]{1,0:T(8,128)}, f32[64,2048]{1,0:T(8,128)}, bf16[16,1,64,384]{3,2,1,0:T(8,128)(2,1)}, bf16[8,1,64,3072]{3,2,1,0:T(8,128)(2,1)}) custom-call(bf16[128,2048]{1,0:T(8,128)(2,1)} %get-tuple-element.51.d_rows, bf16[16,128,384]{2,1,0:T(8,128)(2,1)} %get-tuple-element.52.qkv, bf16[2048,384]{1,0:T(8,128)(2,1)} %bitcast.17, ...), custom_call_target="tpu_custom_call" | custom-call | tf_op jit(solution)/shard_map/pallas_call | solution.py:960
  629.7 33.0 %shard_map.166 = (f32[128,4,2048]{2,1,0:T(4,128)}, f32[128,4,2048]{2,1,0:T(4,128)}, f32[4,6]{1,0:T(4,128)}, f32[4,6]{1,0:T(4,128)}) custom-call(f32[4,6]{1,0:T(4,128)} %mixa.7, f32[4,6]{1,0:T(4,128)} %mixm.7, bf16[128,128]{1,0:T(8,128)(2,1)} %fusion.2.sorter, bf16[4,128,2048]{2,1,0:T(8,128)(2,1)} %get-tuple-element.40.hs, ...), custom_call_target="tpu_custom_call" | custom-call | tf_op jit(solution)/shard_map/pallas_call | solution.py:1235
  662.7 5.7 shard_map.167
  668.5 0.0 copy-start
  668.5 4.9 copy.35
  673.4 0.0 copy-done
  673.4 0.0 copy-start.2
  673.4 0.0 copy-start.1
  673.4 2.0 copy.36
  675.4 0.0 copy-done.2
  675.4 0.6 copy.37
  676.0 0.0 copy-done.1
  676.0 0.6 copy.38
  (4 shorter events, 0.1 us)
Async XLA Ops:
  668.5 4.9 copy-start
  673.4 2.0 copy-start.2
  673.4 2.6 copy-start.1

commit v8 on v7

--- a/solution.py
+++ b/solution.py
@@ -567,6 +567,7 @@
     tokens = n2.shape[0]
     group_rows = 4 * tokens
     step = 256
+    wide = 512
     y2copies = []
 
     def compute(j):
@@ -598,14 +599,14 @@
             y2copies[-1].wait()
 
         def outputs(k, carry):
-            at = pl.ds(pl.multiple_of(k * step, step), step)
+            at = pl.ds(pl.multiple_of(k * wide, wide), wide)
             h = hidden[blocks].reshape(group_rows, ff)
-            y2s[:, :, at] = dot_t(h, wdn[at, :]).astype(BF).reshape(4, tokens, step)
+            y2s[:, :, at] = dot_t(h, wdn[at, :]).astype(BF).reshape(4, tokens, wide)
             d = dgu[blocks].reshape(group_rows, 2 * ff)
-            part[blocks, :, at] = dot_t(d, wgu[at, :]).astype(BF).reshape(4, tokens, step)
+            part[blocks, :, at] = dot_t(d, wgu[at, :]).astype(BF).reshape(4, tokens, wide)
             return carry
 
-        lax.fori_loop(0, width // step, outputs, 0)
+        lax.fori_loop(0, width // wide, outputs, 0)
         c = pltpu.make_async_copy(y2s, y2p.at[blocks], y2sem.at[len(y2copies)])
         c.start()
         y2copies.append(c)
@@ -1087,16 +1088,19 @@
     )(mixa, sorter, x)
 
 
-def middle_kernel(mixa, mixm, hs, attn, wout, y1, n2):
+def middle_kernel(mixa, mixm, hs, attn, wout_in, y1, n2, wout, load):
     m, p = read_mix(mixa), read_mix(mixm)
     tokens, width = attn.shape
 
-    def tile(i, carry):
-        at = pl.ds(pl.multiple_of(i * TILE, TILE), TILE)
-        y1[:, at] = dot(attn[...], wout[:, at])
-        return carry
-
-    lax.fori_loop(0, width // TILE, tile, 0)
+    copies = []
+    for i in range(width // TILE):
+        at = slice(i * TILE, (i + 1) * TILE)
+        c = pltpu.make_async_copy(wout_in.at[:, at], wout.at[i], load.at[i])
+        c.start()
+        copies.append(c)
+    for i, c in enumerate(copies):
+        c.wait()
+        y1[:, i * TILE : (i + 1) * TILE] = dot(attn[...], wout[i])
 
     def norm(r):
         x2 = read_x2(m, p, [hs[j, r].astype(F32) for j in range(4)], y1[r])
@@ -1113,8 +1117,12 @@
             jax.ShapeDtypeStruct((tokens, width), F32),
             jax.ShapeDtypeStruct((tokens, width), BF),
         ),
-        in_specs=[*smem_spec(2), *vmem_spec(3)],
+        in_specs=[*smem_spec(2), *vmem_spec(2), *any_spec(1)],
         out_specs=tuple(vmem_spec(2)),
+        scratch_shapes=[
+            pltpu.VMEM((width // TILE, width, TILE), BF),
+            pltpu.SemaphoreType.DMA((width // TILE,)),
+        ],
         compiler_params=local_params(),
     )(mixa, mixm, hs, attn, wout)
 

time: 684 us -> 683 us (level)
  no operation moved by 1% of the time
where the time goes in v8:
time: 683 us; the launch traced here: 676 us
  Pallas kernels  656 us (96%)
  local copies, waits for them, and re-layouts  9.79 us (1%)
  other arithmetic  9.15 us (1%)
    pallas_call x1, Pallas kernels, front(): pl.pallas_call(front_kernel, out_shape=(shape(GROUP, tokens, head), shape...  247 us
    pallas_call x1, Pallas kernels, back(): pl.pallas_call(back_kernel, out_shape=(jax.ShapeDtypeStruct((tokens, widt...  218 us
    pallas_call x1, Pallas kernels, mlp(): pl.pallas_call(mlp_kernel, out_shape=(jax.ShapeDtypeStruct((*blocks, widt...  130 us
    pallas_call x1, Pallas kernels, close(): pl.pallas_call(close_kernel, out_shape=(jax.ShapeDtypeStruct((tokens, str...  35.1 us

profile of v8, /device:TPU:0, one launch (start us, length us, event | category | flops | bytes accessed | tf_op | source)
XLA Modules:
  0.0 676.1 jit_solution(4199492971698564911)
XLA Ops:
  0.7 0.8 constant_dynamic-slice_fusion
  1.5 0.8 fusion.5
  2.2 0.1 copy.26
  2.3 0.1 copy.27
  2.4 0.1 convert_reduce_fusion
  2.5 0.1 select_reduce_fusion
  2.6 0.6 fusion.4.code_col
  3.2 1.3 fusion.2.sorter
  4.5 0.4 copy.30
  4.9 0.4 copy.28
  5.3 1.2 fusion.1.code_row
  6.5 3.7 multiply_cosine_fusion
  10.2 1.3 pad_maximum_fusion.rope
  11.5 10.9 %shard_map.161 = (bf16[4,128,2048]{2,1,0:T(8,128)(2,1)}, bf16[128,2048]{1,0:T(8,128)(2,1)}) custom-call(f32[4,6]{1,0:T(4,128)} %mixa.7, bf16[128,128]{1,0:T(8,128)(2,1)} %fusion.2.sorter, bf16[128,4,2048]{2,1,0:T(4,128)(2,1)} %x.1), custom_call_target="tpu_custom_call" | custom-call | tf_op jit(solution)/shard_map/pallas_call | solution.py:1078
  22.5 247.1 %shard_map.162 = (bf16[16,128,384]{2,1,0:T(8,128)(2,1)}, bf16[4,128,2048]{2,1,0:T(8,128)(2,1)}, bf16[16,128,2048]{2,1,0:T(8,128)(2,1)}, bf16[8,128,2048]{2,1,0:T...) custom-call(f32[4,6]{1,0:T(4,128)} %mixm.7, ...), custom_call_target="tpu_custom_call" | custom-call | tf_op jit(solution)/shard_map/pallas_call | solution.py:462
  269.6 8.7 %shard_map.163 = (f32[128,2048]{1,0:T(8,128)}, bf16[128,2048]{1,0:T(8,128)(2,1)}) custom-call(f32[4,6]{1,0:T(4,128)} %mixa.7, f32[4,6]{1,0:T(4,128)} %mixm.7, bf16[4,128,2048]{2,1,0:T(8,128)(2,1)} %get-tuple-element.40.hs, bf16[128,2048]{1,0:T(8,128)(2,1)} %get-tuple-element.43.attn, bf16[2048,2048]{1,0:T(8,128)(2,1)} %bitcast.14), custom_call_target="tpu_custom_call" | custom-call | tf_op jit(solution)/shard_map/pallas_call | solution.py:1114
  278.3 130.0 %shard_map.164 = (bf16[8,128,2048]{2,1,0:T(8,128)(2,1)}, bf16[1024,3072]{1,0:T(8,128)(2,1)}, f32[128,2048]{1,0:T(8,128)}, bf16[128,2048]{1,0:T(8,128)(2,1)}, bf1...) custom-call(f32[4,6]{1,0:T(4,128)} %mixa.7, f32[4,6]{1,0:T(4,128)} %mixm.7, bf16[128,2048]{1,0:T(8,128)(2,1)} %get-tuple-element.45.n2, ...), custom_call_target="tpu_custom_call" | custom-call | flops 38654705664 | bytes 62914560 | tf_op jit(solution)/shard_map/pallas_call | solution.py:689
  408.4 218.3 %shard_map.165 = (f32[128,2048]{1,0:T(8,128)}, f32[128,2048]{1,0:T(8,128)}, f32[64,2048]{1,0:T(8,128)}, bf16[16,1,64,384]{3,2,1,0:T(8,128)(2,1)}, bf16[8,1,64,3072]{3,2,1,0:T(8,128)(2,1)}) custom-call(bf16[128,2048]{1,0:T(8,128)(2,1)} %get-tuple-element.51.d_rows, bf16[16,128,384]{2,1,0:T(8,128)(2,1)} %get-tuple-element.52.qkv, bf16[2048,384]{1,0:T(8,128)(2,1)} %bitcast.17, ...), custom_call_target="tpu_custom_call" | custom-call | tf_op jit(solution)/shard_map/pallas_call | solution.py:961
  626.6 35.1 %shard_map.166 = (f32[128,4,2048]{2,1,0:T(4,128)}, f32[128,4,2048]{2,1,0:T(4,128)}, f32[4,6]{1,0:T(4,128)}, f32[4,6]{1,0:T(4,128)}) custom-call(f32[4,6]{1,0:T(4,128)} %mixa.7, f32[4,6]{1,0:T(4,128)} %mixm.7, bf16[128,128]{1,0:T(8,128)(2,1)} %fusion.2.sorter, bf16[4,128,2048]{2,1,0:T(8,128)(2,1)} %get-tuple-element.40.hs, ...), custom_call_target="tpu_custom_call" | custom-call | tf_op jit(solution)/shard_map/pallas_call | solution.py:1243
  661.7 5.7 shard_map.167
  667.5 0.0 copy-start
  667.5 4.9 copy.35
  672.4 0.0 copy-done
  672.4 0.0 copy-start.2
  672.4 0.0 copy-start.1
  672.4 2.0 copy.36
  674.4 0.0 copy-done.2
  674.4 0.6 copy.37
  675.0 0.0 copy-done.1
  675.0 0.6 copy.38
  (4 shorter events, 0.1 us)
Async XLA Ops:
  667.5 4.9 copy-start
  672.4 2.0 copy-start.2
  672.4 2.6 copy-start.1
